TPU v7x, 32 devices: a whole 2x2x4 slice. The times are simulated.
32 devices in a mesh: pair: 2 (over core), seq: 4 (over z), asset: 4 (over y, x).
Axes of the slice: x: 2, y: 2, z: 4, core: 2. Of those that a mesh axis runs over, the one named last changes fastest.
Arguments:
- latents: float32 [4, 8, 512], P('asset', None, 'seq'), may hold values from -6 to 6
- voxel_coords: int32 [4, 3, 512], P('asset', None, 'seq'), may hold values from 0 to 63
- owner_map: int32 [4, 512, 1], P('asset', 'seq'), may hold values from 0 to 3; in each aligned block of 128 rows (0 to 127, 128 to 255, ..., all dimensions but the last counted through in order) at most 64 rows name the same one
- step_time: float32 [4], P('asset'), may hold values from 0.2 to 0.5
- modulation: float32 [4, 2, 5, 1024], P('asset', 'pair'), may hold values from -3 to 3
- in_proj: float32 [8, 1024], replicated, may hold values from -2 to 2
- qkv_proj: bfloat16 [1024, 1536], replicated, may hold values from -0.1875 to 0.1875
- norm_gain: float32 [2, 512], replicated, may hold values from 1.5 to 3
- out_proj: bfloat16 [512, 1024], replicated, may hold values from -0.25 to 0.25
- head_proj: float32 [1024, 8], replicated, may hold values from -0.1875 to 0.1875
- decoder_projection: float32 [8, 768], replicated, may hold values from -2 to 2
- border_blocks: int32 [4, 4, 2, 8], P('asset', 'seq'), may hold values from 0 to 15
- kernel_map: int32 [4, 4, 27, 1024], P('asset', 'seq'), may hold values from 0 to 512
- conv_weight: bfloat16 [27, 768, 192], P(None, None, 'pair'), may hold values from -0.0390625 to 0.0390625
Outputs:
- owned_latents: float32 [4, 4, 8, 256], P('asset', 'seq')
- decoded: bfloat16 [4, 4, 1024, 192], P('asset', 'seq', None, 'pair')
Inputs may be any that keep to these rules, and one draw needn't show every extreme that they name: `owner_map`: in each aligned block of 128 tokens (the tokens of one device) no owner is named by more than 64 tokens. `kernel_map`: rows below 256 are the owner's slots, the next 128 come from the owner below, the next 128 from the owner above, and 512 is the zero row.
All inputs are finite; a program needn't handle non-finite values.
Results may differ from a plain program's by a relative error of at most 0.0075.
Values may be sent and summed in bfloat16 or wider, within the bound.
No kernel may reach another device: no remote copies, remote signals or barrier semaphores. Data moves between devices by JAX's collectives and lax.ppermute only.
A program may use at most 128 MiB of HBM per device.

v0:
```python
import math

import jax
import jax.numpy as jnp
from jax import lax
from jax.sharding import PartitionSpec as P

HEADS = 8
HEAD = 64
LAT = 8
BLK = 16


EPSILON = 1e-06
GUIDANCE = 3.0
TOP_PRECISION = lax.Precision.HIGHEST


def from_partner(shard, axis, apart):
    return lax.ppermute(shard, axis, [(i, i ^ 1 << apart) for i in range(lax.axis_size(axis))])


def extended(cells, sides, width):
    for axis, dim in sides:
        count = lax.axis_size(axis)
        ends = count - 1
        head = lax.slice_in_dim(cells, 0, width, axis=dim)
        tail = lax.slice_in_dim(cells, cells.shape[dim] - width, cells.shape[dim], axis=dim)
        cells = jnp.concatenate(
            [
                lax.ppermute(tail, axis, [(i, (i + 1) % count) for i in range(ends)]),
                cells,
                lax.ppermute(head, axis, [((i + 1) % count, i) for i in range(ends)]),
            ],
            axis=dim,
        )
    return cells


def layer_norm(values):
    center = values - jnp.mean(values, axis=-1, keepdims=True)
    variance = jnp.mean(center * center, axis=-1, keepdims=True)
    return center / jnp.sqrt(variance + EPSILON)


def position_table(coord_rows, model_width):
    freqs = model_width // 6
    steps = jnp.arange(freqs, dtype=jnp.float32) / freqs
    omegas = jnp.exp(-math.log(10000.0) * steps)
    angles = coord_rows.astype(jnp.float32)[:, :, None] * omegas[None, None, :]
    halves = jnp.concatenate([jnp.sin(angles), jnp.cos(angles)], axis=2)
    rows_out = jnp.transpose(halves, (1, 0, 2)).reshape(coord_rows.shape[1], 6 * freqs)
    return jnp.pad(rows_out, ((0, 0), (0, model_width - 6 * freqs)))


def head_norm(values, gains):
    row_count = values.shape[0]
    per_head = values.reshape(row_count, HEADS, HEAD)
    mean_square = jnp.mean(per_head * per_head, axis=2, keepdims=True)
    return (per_head / jnp.sqrt(mean_square + EPSILON)).reshape(row_count, HEADS * HEAD) * gains


def pack_slots(columns, owner_rows, seq_count, capacity):
    owner_ids = jnp.arange(seq_count, dtype=jnp.int32)
    onehot = (owner_rows[:, None] == owner_ids[None, :]).astype(jnp.int32)
    ranks = jnp.sum(onehot * (jnp.cumsum(onehot, axis=0) - 1), axis=1)
    slot_ids = owner_rows * capacity + ranks
    targets = jnp.arange(seq_count * capacity, dtype=jnp.int32)
    dispatch = (slot_ids[:, None] == targets[None, :]).astype(jnp.float32)
    packed = jnp.dot(columns, dispatch, precision=TOP_PRECISION)
    return packed.reshape(columns.shape[0], seq_count, capacity)


def per_device(
    latents,
    voxel_coords,
    owner_map,
    step_time,
    modulation,
    in_proj,
    qkv_proj,
    norm_gain,
    out_proj,
    head_proj,
    decoder_projection,
    border_blocks,
    kernel_map,
    conv_weight,
):
    latent_block = latents[0]
    token_count = latent_block.shape[1]
    model_width = in_proj.shape[1]
    inner_width = out_proj.shape[0]
    factor = HEAD ** (-0.5)
    mod_rows = modulation[0, 0]
    hidden = jnp.dot(latent_block.T, in_proj, precision=TOP_PRECISION) + position_table(
        voxel_coords[0], model_width
    )
    normed = (layer_norm(hidden) * (1.0 + mod_rows[1]) + mod_rows[0]).astype(jnp.bfloat16)
    projected = jnp.dot(normed, qkv_proj, preferred_element_type=jnp.float32)
    queries = head_norm(projected[:, :inner_width], norm_gain[0]).astype(jnp.bfloat16)
    keys_in = head_norm(projected[:, inner_width : 2 * inner_width], norm_gain[1]).astype(
        jnp.bfloat16
    )
    values_in = projected[:, 2 * inner_width :].astype(jnp.bfloat16)
    query_heads = queries.reshape(token_count, HEADS, HEAD)
    start_pair = (
        jnp.zeros((token_count, HEADS, HEAD), jnp.float32),
        jnp.zeros((token_count, HEADS), jnp.float32),
    )
    key_row_list = lax.all_gather(keys_in, "seq", axis=0, tiled=True)
    value_rows = lax.all_gather(values_in, "seq", axis=0, tiled=True)
    row_count = key_row_list.shape[0]
    block_rows = math.gcd(row_count, 512)
    key_blocks = key_row_list.reshape(row_count // block_rows, block_rows, HEADS, HEAD)
    value_blocks = value_rows.reshape(row_count // block_rows, block_rows, HEADS, HEAD)

    def one_block(running, block_pair):
        numer_run, denom_run = running
        key_block, value_block = block_pair
        scores = (
            jnp.einsum("qhd,khd->hqk", query_heads, key_block, preferred_element_type=jnp.float32)
            * factor
        )
        exp_scores = jnp.exp(scores)
        numer_run = numer_run + jnp.einsum(
            "hqk,khd->qhd",
            exp_scores.astype(jnp.bfloat16),
            value_block,
            preferred_element_type=jnp.float32,
        )
        denom_run = denom_run + jnp.sum(exp_scores, axis=2).T
        return ((numer_run, denom_run), None)

    result_pair, unused = lax.scan(one_block, start_pair, (key_blocks, value_blocks))
    numerator, denominator = result_pair
    attended = (
        (numerator / denominator[:, :, None]).reshape(token_count, inner_width).astype(jnp.bfloat16)
    )
    hidden = hidden + mod_rows[2] * jnp.dot(attended, out_proj, preferred_element_type=jnp.float32)
    final = layer_norm(hidden) * (1.0 + mod_rows[4]) + mod_rows[3]
    velocity = jnp.dot(final, head_proj, precision=TOP_PRECISION).T
    seq_count = lax.axis_size("seq")
    slot_count = kernel_map.shape[3] // 4
    capacity = slot_count // seq_count
    owner_rows = owner_map[0, :, 0]
    when_step = step_time[0]
    is_cond = lax.axis_index("pair") == 0
    partner = from_partner(velocity, "pair", 0)
    cond_velocity = jnp.where(is_cond, velocity, partner)
    uncond_velocity = jnp.where(is_cond, partner, velocity)
    clean = latent_block - when_step * (
        uncond_velocity + GUIDANCE * (cond_velocity - uncond_velocity)
    )
    packed = pack_slots(clean, owner_rows, seq_count, capacity)
    received = lax.all_to_all(packed, "seq", split_axis=1, concat_axis=1, tiled=True)
    owned_rows = received.reshape(LAT, slot_count)
    voxel_features = jax.nn.silu(
        jnp.dot(owned_rows.T, decoder_projection, precision=TOP_PRECISION)
    ).astype(jnp.bfloat16)
    block_count = slot_count // BLK
    chosen = border_blocks[0, 0].reshape(-1)
    halo_rows = border_blocks.shape[3] * BLK
    dec_width = decoder_projection.shape[1]
    tiles = voxel_features.reshape(block_count, BLK, dec_width)
    outgoing = jnp.take(tiles, chosen, axis=0).reshape(2 * halo_rows, dec_width)
    padded = extended(outgoing, (("seq", 0),), halo_rows)
    rim_features = jnp.concatenate([padded[:halo_rows], padded[-halo_rows:]], axis=0)
    zero_row = jnp.zeros((1, dec_width), jnp.bfloat16)
    rows_table = jnp.concatenate([voxel_features, rim_features, zero_row], axis=0)
    table_rows = rows_table.shape[0]
    products = jnp.einsum(
        "rc,kco->kro", rows_table, conv_weight, preferred_element_type=jnp.float32
    )
    row_ids = jnp.arange(table_rows, dtype=jnp.int32)
    index_maps = kernel_map[0, 0]
    fine_rows = index_maps.shape[1]

    def add_offset(total, offset_pair):
        product_rows, index_rows = offset_pair
        selector = (index_rows[:, None] == row_ids[None, :]).astype(jnp.float32)
        return (total + jnp.dot(selector, product_rows, precision=TOP_PRECISION), None)

    start_total = jnp.zeros((fine_rows, products.shape[2]), jnp.float32)
    summed, unused_rows = lax.scan(add_offset, start_total, (products, index_maps))
    decoded = summed.astype(jnp.bfloat16)
    return (owned_rows[None, None], decoded[None, None])


def solution(mesh):
    placed = (
        P("asset", None, "seq"),
        P("asset", None, "seq"),
        P("asset", "seq", None),
        P("asset"),
        P("asset", "pair", None, None),
        P(),
        P(),
        P(),
        P(),
        P(),
        P(),
        P("asset", "seq", None, None),
        P("asset", "seq", None, None),
        P(None, None, "pair"),
    )
    return jax.shard_map(
        per_device,
        mesh=mesh,
        in_specs=placed,
        out_specs=(P("asset", "seq", None, None), P("asset", "seq", None, "pair")),
        check_vma=False,
    )
```

profile of v0, /device:TPU:0, one launch (start us, length us, event | category | flops | bytes accessed | tf_op | source)
XLA Modules:
  0.0 194.6 jit_solution(157521716403114253)
XLA Ops:
  3.4 1.9 reshape.158
  5.3 2.0 %copy.40 = f32[128,1020]{1,0:T(8,128)} copy(f32[128,1020]{0,1:T(8,128)} %reshape.158) | data formatting | bytes 1044480 | tf_op jit(solution)/shard_map/reshape | solution.py:52
  7.3 1.7 fusion.55
  14.0 1.8 copy.45
  17.5 1.8 copy.46
  20.1 1.9 multiply_convert_fusion.1
  21.9 18.0 %all_gather.7 = bf16[512,512]{1,0:T(8,128)(2,1)} all-gather(bf16[128,512]{1,0:T(8,128)(2,1)S(1)} %get-tuple-element.89), channel_id=1, replica_groups=mesh['pair'=2,'seq'=4,'asset'=4] {'seq'}, dimensions={0}, use_global_device_ids=true | all-gather | bytes 655360 | tf_op jit(solution)/shard_map/all_gather | solution.py:111
  39.9 2.0 %copy.47 = bf16[512,512]{0,1:T(8,128)(2,1)} copy(bf16[512,512]{1,0:T(8,128)(2,1)} %all_gather.7) | data formatting | bytes 1048576 | tf_op jit(solution)/shard_map/all_gather | solution.py:111
  43.0 17.0 %all_gather.6 = bf16[512,512]{1,0:T(8,128)(2,1)} all-gather(bf16[128,512]{1,0:T(8,128)(2,1)S(1)} %slice.76), channel_id=1, replica_groups=mesh['pair'=2,'seq'=4,'asset'=4] {'seq'}, dimensions={0}, use_global_device_ids=true | all-gather | bytes 655360 | tf_op jit(solution)/shard_map/all_gather | solution.py:112
  60.0 2.1 %copy.41 = bf16[512,512]{0,1:T(8,128)(2,1)} copy(bf16[512,512]{1,0:T(8,128)(2,1)} %all_gather.6) | data formatting | bytes 1048576 | tf_op jit(solution)/shard_map/all_gather | solution.py:112
  62.1 1.8 fusion.8
  68.6 4.1 %all-to-all-start = ((f32[4,1,512]{2,1,0:T(1,128)}), f32[4,1,512]{2,1,0:T(1,128)S(1)}, u32[]{:S(2)}, u32[]{:S(2)}) async-start(f32[4,1,512]{2,1,0:T(1,128)} %reshape.174), calls=%async_computation | async-start | bytes 16384 | tf_op jit(solution)/shard_map/all_to_all | solution.py:156
  73.4 5.0 %all-to-all-done = f32[4,1,512]{2,1,0:T(1,128)S(1)} async-done(((f32[4,1,512]{2,1,0:T(1,128)}), f32[4,1,512]{2,1,0:T(1,128)S(1)}, u32[]{:S(2)}, u32[]{:S(2)}) %all-to-all-start) | async-done | bytes 8224 | tf_op jit(solution)/shard_map/all_to_all | solution.py:156
  79.7 1.7 multiply_convert_fusion
  81.4 1.7 gather_fusion
  84.6 3.2 %collective-permute-start.1 = (bf16[128,768]{1,0:T(8,128)(2,1)}, bf16[128,768]{1,0:T(8,128)(2,1)}, u32[]{:S(2)}, u32[]{:S(2)}) collective-permute-start(bf16[128,768]{1,0:T(8,128)(2,1)} %bitcast.24), channel_id=1, source_target_pairs={{0,4},{4,8},{8,12},{1,5},{5,9},{9,13},{2,6},{6,10},{10,14},{3,7},{... | collective-permute-start | bytes 589832 | tf_op jit(solution)/shard_map/ppermute | solution.py:31
  87.8 1.3 collective-permute-start.2
  89.1 1.6 copy.58
  92.0 3.7 %collective-permute-done.2 = bf16[128,768]{1,0:T(8,128)(2,1)} collective-permute-done((bf16[128,768]{1,0:T(8,128)(2,1)}, bf16[128,768]{1,0:T(8,128)(2,1)}, u32[]{:S(2)}, u32[]{:S(2)}) %collective-permute-start.2) | collective-permute-done | bytes 196640 | tf_op jit(solution)/shard_map/ppermute | solution.py:33
  95.7 8.6 %fusion.15 = f32[513,2592]{0,1} fusion(bf16[768,2592]{0,1:T(8,128)(2,1)} %bitcast.107, bf16[128,768]{1,0:T(8,128)(2,1)} %collective-permute-done.2, bf16[128,768]{1,0:T(8,128)(2,1)} %collective-permute-done.1, bf16[256,768]{1,0:T(8,128)(2,1)} %multiply_convert_fusion, bf16[513]{0:T(1024)(128)(2,1)} %pad.8.clone), kind=kOutput, calls=%fused_computation.21 | convolution fusion | flops 2045564928 | bytes 10087554
  104.3 89.6 %while.3 = (s32[]{:T(128)}, f32[1024,96]{0,1:T(8,128)S(1)}, s32[27,1024]{1,0:T(8,128)}, f32[27,513,96]{1,2,0:T(8,128)}, s32[]{:T(128)}, /*index=5*/s32[]{:T(128)}) while((s32[]{:T(128)}, f32[1024,96]{0,1:T(8,128)S(1)}, s32[27,1024]{1,0:T(8,128)}, f32[27,513,96]{1,2,0:T(8,128)}, s32[]{:T(128)}, /*index=5*/s32[]{:T(128)}) %tuple.48), condition=%wide.region_10.11_spmd.clone, body=%wide.region_9.10_spmd.clone.sunk | while | flops 605881344 | bytes 1045075 | solution.py:185
  105.1 2.5 %fusion.71 = f32[1024,96]{0,1:T(8,128)S(1)} fusion(s32[1024]{0:T(1024)S(1)} %bitcast.93, f32[1024,96]{0,1:T(8,128)S(1)} %get-tuple-element.142, f32[27,513,96]{1,2,0:T(8,128)} %get-tuple-element.150, s32[]{:T(128)} %get-tuple-element.141, pred[]{:T(512)S(6)} %compare.4), kind=kOutput, calls=%fused_computation.5.clone.1 | convolution fusion | flops 605881344 | bytes 1036801 | tf_op jit(solution)/shard_map/while/body/eval_jaxpr/dot_general | solution.py:182
  108.4 2.5 %fusion.71 = f32[1024,96]{0,1:T(8,128)S(1)} fusion(s32[1024]{0:T(1024)S(1)} %bitcast.93, f32[1024,96]{0,1:T(8,128)S(1)} %get-tuple-element.142, f32[27,513,96]{1,2,0:T(8,128)} %get-tuple-element.150, s32[]{:T(128)} %get-tuple-element.141, pred[]{:T(512)S(6)} %compare.4), kind=kOutput, calls=%fused_computation.5.clone.1 | convolution fusion | flops 605881344 | bytes 1036801 | tf_op jit(solution)/shard_map/while/body/eval_jaxpr/dot_general | solution.py:182
  111.7 2.5 %fusion.71 = f32[1024,96]{0,1:T(8,128)S(1)} fusion(s32[1024]{0:T(1024)S(1)} %bitcast.93, f32[1024,96]{0,1:T(8,128)S(1)} %get-tuple-element.142, f32[27,513,96]{1,2,0:T(8,128)} %get-tuple-element.150, s32[]{:T(128)} %get-tuple-element.141, pred[]{:T(512)S(6)} %compare.4), kind=kOutput, calls=%fused_computation.5.clone.1 | convolution fusion | flops 605881344 | bytes 1036801 | tf_op jit(solution)/shard_map/while/body/eval_jaxpr/dot_general | solution.py:182
  115.0 2.5 %fusion.71 = f32[1024,96]{0,1:T(8,128)S(1)} fusion(s32[1024]{0:T(1024)S(1)} %bitcast.93, f32[1024,96]{0,1:T(8,128)S(1)} %get-tuple-element.142, f32[27,513,96]{1,2,0:T(8,128)} %get-tuple-element.150, s32[]{:T(128)} %get-tuple-element.141, pred[]{:T(512)S(6)} %compare.4), kind=kOutput, calls=%fused_computation.5.clone.1 | convolution fusion | flops 605881344 | bytes 1036801 | tf_op jit(solution)/shard_map/while/body/eval_jaxpr/dot_general | solution.py:182
  118.4 2.5 %fusion.71 = f32[1024,96]{0,1:T(8,128)S(1)} fusion(s32[1024]{0:T(1024)S(1)} %bitcast.93, f32[1024,96]{0,1:T(8,128)S(1)} %get-tuple-element.142, f32[27,513,96]{1,2,0:T(8,128)} %get-tuple-element.150, s32[]{:T(128)} %get-tuple-element.141, pred[]{:T(512)S(6)} %compare.4), kind=kOutput, calls=%fused_computation.5.clone.1 | convolution fusion | flops 605881344 | bytes 1036801 | tf_op jit(solution)/shard_map/while/body/eval_jaxpr/dot_general | solution.py:182
  121.7 2.5 %fusion.71 = f32[1024,96]{0,1:T(8,128)S(1)} fusion(s32[1024]{0:T(1024)S(1)} %bitcast.93, f32[1024,96]{0,1:T(8,128)S(1)} %get-tuple-element.142, f32[27,513,96]{1,2,0:T(8,128)} %get-tuple-element.150, s32[]{:T(128)} %get-tuple-element.141, pred[]{:T(512)S(6)} %compare.4), kind=kOutput, calls=%fused_computation.5.clone.1 | convolution fusion | flops 605881344 | bytes 1036801 | tf_op jit(solution)/shard_map/while/body/eval_jaxpr/dot_general | solution.py:182
  125.0 2.5 %fusion.71 = f32[1024,96]{0,1:T(8,128)S(1)} fusion(s32[1024]{0:T(1024)S(1)} %bitcast.93, f32[1024,96]{0,1:T(8,128)S(1)} %get-tuple-element.142, f32[27,513,96]{1,2,0:T(8,128)} %get-tuple-element.150, s32[]{:T(128)} %get-tuple-element.141, pred[]{:T(512)S(6)} %compare.4), kind=kOutput, calls=%fused_computation.5.clone.1 | convolution fusion | flops 605881344 | bytes 1036801 | tf_op jit(solution)/shard_map/while/body/eval_jaxpr/dot_general | solution.py:182
  128.3 2.5 %fusion.71 = f32[1024,96]{0,1:T(8,128)S(1)} fusion(s32[1024]{0:T(1024)S(1)} %bitcast.93, f32[1024,96]{0,1:T(8,128)S(1)} %get-tuple-element.142, f32[27,513,96]{1,2,0:T(8,128)} %get-tuple-element.150, s32[]{:T(128)} %get-tuple-element.141, pred[]{:T(512)S(6)} %compare.4), kind=kOutput, calls=%fused_computation.5.clone.1 | convolution fusion | flops 605881344 | bytes 1036801 | tf_op jit(solution)/shard_map/while/body/eval_jaxpr/dot_general | solution.py:182
  131.6 2.5 %fusion.71 = f32[1024,96]{0,1:T(8,128)S(1)} fusion(s32[1024]{0:T(1024)S(1)} %bitcast.93, f32[1024,96]{0,1:T(8,128)S(1)} %get-tuple-element.142, f32[27,513,96]{1,2,0:T(8,128)} %get-tuple-element.150, s32[]{:T(128)} %get-tuple-element.141, pred[]{:T(512)S(6)} %compare.4), kind=kOutput, calls=%fused_computation.5.clone.1 | convolution fusion | flops 605881344 | bytes 1036801 | tf_op jit(solution)/shard_map/while/body/eval_jaxpr/dot_general | solution.py:182
  135.0 2.5 %fusion.71 = f32[1024,96]{0,1:T(8,128)S(1)} fusion(s32[1024]{0:T(1024)S(1)} %bitcast.93, f32[1024,96]{0,1:T(8,128)S(1)} %get-tuple-element.142, f32[27,513,96]{1,2,0:T(8,128)} %get-tuple-element.150, s32[]{:T(128)} %get-tuple-element.141, pred[]{:T(512)S(6)} %compare.4), kind=kOutput, calls=%fused_computation.5.clone.1 | convolution fusion | flops 605881344 | bytes 1036801 | tf_op jit(solution)/shard_map/while/body/eval_jaxpr/dot_general | solution.py:182
  138.3 2.5 %fusion.71 = f32[1024,96]{0,1:T(8,128)S(1)} fusion(s32[1024]{0:T(1024)S(1)} %bitcast.93, f32[1024,96]{0,1:T(8,128)S(1)} %get-tuple-element.142, f32[27,513,96]{1,2,0:T(8,128)} %get-tuple-element.150, s32[]{:T(128)} %get-tuple-element.141, pred[]{:T(512)S(6)} %compare.4), kind=kOutput, calls=%fused_computation.5.clone.1 | convolution fusion | flops 605881344 | bytes 1036801 | tf_op jit(solution)/shard_map/while/body/eval_jaxpr/dot_general | solution.py:182
  141.6 2.5 %fusion.71 = f32[1024,96]{0,1:T(8,128)S(1)} fusion(s32[1024]{0:T(1024)S(1)} %bitcast.93, f32[1024,96]{0,1:T(8,128)S(1)} %get-tuple-element.142, f32[27,513,96]{1,2,0:T(8,128)} %get-tuple-element.150, s32[]{:T(128)} %get-tuple-element.141, pred[]{:T(512)S(6)} %compare.4), kind=kOutput, calls=%fused_computation.5.clone.1 | convolution fusion | flops 605881344 | bytes 1036801 | tf_op jit(solution)/shard_map/while/body/eval_jaxpr/dot_general | solution.py:182
  144.9 2.5 %fusion.71 = f32[1024,96]{0,1:T(8,128)S(1)} fusion(s32[1024]{0:T(1024)S(1)} %bitcast.93, f32[1024,96]{0,1:T(8,128)S(1)} %get-tuple-element.142, f32[27,513,96]{1,2,0:T(8,128)} %get-tuple-element.150, s32[]{:T(128)} %get-tuple-element.141, pred[]{:T(512)S(6)} %compare.4), kind=kOutput, calls=%fused_computation.5.clone.1 | convolution fusion | flops 605881344 | bytes 1036801 | tf_op jit(solution)/shard_map/while/body/eval_jaxpr/dot_general | solution.py:182
  148.2 2.5 %fusion.71 = f32[1024,96]{0,1:T(8,128)S(1)} fusion(s32[1024]{0:T(1024)S(1)} %bitcast.93, f32[1024,96]{0,1:T(8,128)S(1)} %get-tuple-element.142, f32[27,513,96]{1,2,0:T(8,128)} %get-tuple-element.150, s32[]{:T(128)} %get-tuple-element.141, pred[]{:T(512)S(6)} %compare.4), kind=kOutput, calls=%fused_computation.5.clone.1 | convolution fusion | flops 605881344 | bytes 1036801 | tf_op jit(solution)/shard_map/while/body/eval_jaxpr/dot_general | solution.py:182
  151.5 2.5 %fusion.71 = f32[1024,96]{0,1:T(8,128)S(1)} fusion(s32[1024]{0:T(1024)S(1)} %bitcast.93, f32[1024,96]{0,1:T(8,128)S(1)} %get-tuple-element.142, f32[27,513,96]{1,2,0:T(8,128)} %get-tuple-element.150, s32[]{:T(128)} %get-tuple-element.141, pred[]{:T(512)S(6)} %compare.4), kind=kOutput, calls=%fused_computation.5.clone.1 | convolution fusion | flops 605881344 | bytes 1036801 | tf_op jit(solution)/shard_map/while/body/eval_jaxpr/dot_general | solution.py:182
  154.9 2.5 %fusion.71 = f32[1024,96]{0,1:T(8,128)S(1)} fusion(s32[1024]{0:T(1024)S(1)} %bitcast.93, f32[1024,96]{0,1:T(8,128)S(1)} %get-tuple-element.142, f32[27,513,96]{1,2,0:T(8,128)} %get-tuple-element.150, s32[]{:T(128)} %get-tuple-element.141, pred[]{:T(512)S(6)} %compare.4), kind=kOutput, calls=%fused_computation.5.clone.1 | convolution fusion | flops 605881344 | bytes 1036801 | tf_op jit(solution)/shard_map/while/body/eval_jaxpr/dot_general | solution.py:182
  158.2 2.5 %fusion.71 = f32[1024,96]{0,1:T(8,128)S(1)} fusion(s32[1024]{0:T(1024)S(1)} %bitcast.93, f32[1024,96]{0,1:T(8,128)S(1)} %get-tuple-element.142, f32[27,513,96]{1,2,0:T(8,128)} %get-tuple-element.150, s32[]{:T(128)} %get-tuple-element.141, pred[]{:T(512)S(6)} %compare.4), kind=kOutput, calls=%fused_computation.5.clone.1 | convolution fusion | flops 605881344 | bytes 1036801 | tf_op jit(solution)/shard_map/while/body/eval_jaxpr/dot_general | solution.py:182
  161.5 2.5 %fusion.71 = f32[1024,96]{0,1:T(8,128)S(1)} fusion(s32[1024]{0:T(1024)S(1)} %bitcast.93, f32[1024,96]{0,1:T(8,128)S(1)} %get-tuple-element.142, f32[27,513,96]{1,2,0:T(8,128)} %get-tuple-element.150, s32[]{:T(128)} %get-tuple-element.141, pred[]{:T(512)S(6)} %compare.4), kind=kOutput, calls=%fused_computation.5.clone.1 | convolution fusion | flops 605881344 | bytes 1036801 | tf_op jit(solution)/shard_map/while/body/eval_jaxpr/dot_general | solution.py:182
  164.8 2.5 %fusion.71 = f32[1024,96]{0,1:T(8,128)S(1)} fusion(s32[1024]{0:T(1024)S(1)} %bitcast.93, f32[1024,96]{0,1:T(8,128)S(1)} %get-tuple-element.142, f32[27,513,96]{1,2,0:T(8,128)} %get-tuple-element.150, s32[]{:T(128)} %get-tuple-element.141, pred[]{:T(512)S(6)} %compare.4), kind=kOutput, calls=%fused_computation.5.clone.1 | convolution fusion | flops 605881344 | bytes 1036801 | tf_op jit(solution)/shard_map/while/body/eval_jaxpr/dot_general | solution.py:182
  168.1 2.5 %fusion.71 = f32[1024,96]{0,1:T(8,128)S(1)} fusion(s32[1024]{0:T(1024)S(1)} %bitcast.93, f32[1024,96]{0,1:T(8,128)S(1)} %get-tuple-element.142, f32[27,513,96]{1,2,0:T(8,128)} %get-tuple-element.150, s32[]{:T(128)} %get-tuple-element.141, pred[]{:T(512)S(6)} %compare.4), kind=kOutput, calls=%fused_computation.5.clone.1 | convolution fusion | flops 605881344 | bytes 1036801 | tf_op jit(solution)/shard_map/while/body/eval_jaxpr/dot_general | solution.py:182
  171.4 2.5 %fusion.71 = f32[1024,96]{0,1:T(8,128)S(1)} fusion(s32[1024]{0:T(1024)S(1)} %bitcast.93, f32[1024,96]{0,1:T(8,128)S(1)} %get-tuple-element.142, f32[27,513,96]{1,2,0:T(8,128)} %get-tuple-element.150, s32[]{:T(128)} %get-tuple-element.141, pred[]{:T(512)S(6)} %compare.4), kind=kOutput, calls=%fused_computation.5.clone.1 | convolution fusion | flops 605881344 | bytes 1036801 | tf_op jit(solution)/shard_map/while/body/eval_jaxpr/dot_general | solution.py:182
  174.8 2.5 %fusion.71 = f32[1024,96]{0,1:T(8,128)S(1)} fusion(s32[1024]{0:T(1024)S(1)} %bitcast.93, f32[1024,96]{0,1:T(8,128)S(1)} %get-tuple-element.142, f32[27,513,96]{1,2,0:T(8,128)} %get-tuple-element.150, s32[]{:T(128)} %get-tuple-element.141, pred[]{:T(512)S(6)} %compare.4), kind=kOutput, calls=%fused_computation.5.clone.1 | convolution fusion | flops 605881344 | bytes 1036801 | tf_op jit(solution)/shard_map/while/body/eval_jaxpr/dot_general | solution.py:182
  178.1 2.5 %fusion.71 = f32[1024,96]{0,1:T(8,128)S(1)} fusion(s32[1024]{0:T(1024)S(1)} %bitcast.93, f32[1024,96]{0,1:T(8,128)S(1)} %get-tuple-element.142, f32[27,513,96]{1,2,0:T(8,128)} %get-tuple-element.150, s32[]{:T(128)} %get-tuple-element.141, pred[]{:T(512)S(6)} %compare.4), kind=kOutput, calls=%fused_computation.5.clone.1 | convolution fusion | flops 605881344 | bytes 1036801 | tf_op jit(solution)/shard_map/while/body/eval_jaxpr/dot_general | solution.py:182
  181.4 2.5 %fusion.71 = f32[1024,96]{0,1:T(8,128)S(1)} fusion(s32[1024]{0:T(1024)S(1)} %bitcast.93, f32[1024,96]{0,1:T(8,128)S(1)} %get-tuple-element.142, f32[27,513,96]{1,2,0:T(8,128)} %get-tuple-element.150, s32[]{:T(128)} %get-tuple-element.141, pred[]{:T(512)S(6)} %compare.4), kind=kOutput, calls=%fused_computation.5.clone.1 | convolution fusion | flops 605881344 | bytes 1036801 | tf_op jit(solution)/shard_map/while/body/eval_jaxpr/dot_general | solution.py:182
  184.7 2.5 %fusion.71 = f32[1024,96]{0,1:T(8,128)S(1)} fusion(s32[1024]{0:T(1024)S(1)} %bitcast.93, f32[1024,96]{0,1:T(8,128)S(1)} %get-tuple-element.142, f32[27,513,96]{1,2,0:T(8,128)} %get-tuple-element.150, s32[]{:T(128)} %get-tuple-element.141, pred[]{:T(512)S(6)} %compare.4), kind=kOutput, calls=%fused_computation.5.clone.1 | convolution fusion | flops 605881344 | bytes 1036801 | tf_op jit(solution)/shard_map/while/body/eval_jaxpr/dot_general | solution.py:182
  188.0 2.5 %fusion.71 = f32[1024,96]{0,1:T(8,128)S(1)} fusion(s32[1024]{0:T(1024)S(1)} %bitcast.93, f32[1024,96]{0,1:T(8,128)S(1)} %get-tuple-element.142, f32[27,513,96]{1,2,0:T(8,128)} %get-tuple-element.150, s32[]{:T(128)} %get-tuple-element.141, pred[]{:T(512)S(6)} %compare.4), kind=kOutput, calls=%fused_computation.5.clone.1 | convolution fusion | flops 605881344 | bytes 1036801 | tf_op jit(solution)/shard_map/while/body/eval_jaxpr/dot_general | solution.py:182
  191.4 2.5 %fusion.71 = f32[1024,96]{0,1:T(8,128)S(1)} fusion(s32[1024]{0:T(1024)S(1)} %bitcast.93, f32[1024,96]{0,1:T(8,128)S(1)} %get-tuple-element.142, f32[27,513,96]{1,2,0:T(8,128)} %get-tuple-element.150, s32[]{:T(128)} %get-tuple-element.141, pred[]{:T(512)S(6)} %compare.4), kind=kOutput, calls=%fused_computation.5.clone.1 | convolution fusion | flops 605881344 | bytes 1036801 | tf_op jit(solution)/shard_map/while/body/eval_jaxpr/dot_general | solution.py:182
  (108 shorter events, 41.2 us)
Async XLA Ops:
  0.6 8.7 %copy-start = (bf16[1024,1536]{1,0:T(8,128)(2,1)S(1)}, bf16[1024,1536]{1,0:T(8,128)(2,1)}, u32[]{:S(2)}) copy-start(bf16[1024,1536]{1,0:T(8,128)(2,1)} %param.22) | copy-start | bytes 9437188
  0.6 6.7 %copy-start.8 = (f32[1,8,128]{2,1,0:T(8,128)S(1)}, f32[1,8,128]{2,1,0:T(8,128)}, u32[]{:S(2)}) copy-start(f32[1,8,128]{2,1,0:T(8,128)} %param.16) | copy-start | bytes 12292
  0.7 6.7 %copy-start.6 = (f32[8,1024]{1,0:T(8,128)S(1)}, f32[8,1024]{1,0:T(8,128)}, u32[]{:S(2)}) copy-start(f32[8,1024]{1,0:T(8,128)} %param.21) | copy-start | bytes 98308
  3.4 5.9 %copy-start.7 = (f32[1,1,5,1024]{3,1,2,0:T(1,128)S(1)}, f32[1,1,5,1024]{3,1,2,0:T(1,128)}, u32[]{:S(2)}) copy-start(f32[1,1,5,1024]{3,1,2,0:T(1,128)} %param.20) | copy-start | bytes 61444
  9.1 0.9 copy-start.1
  10.0 1.1 copy-start.4
  62.1 1.8 copy-start.3
  62.1 2.3 %copy-start.2 = (f32[128,1024]{1,0:T(8,128)S(1)}, f32[128,1024]{1,0:T(8,128)}, u32[]{:S(2)}) copy-start(f32[128,1024]{1,0:T(8,128)} %copy-done.1) | copy-start | bytes 1572868
  62.1 2.3 %copy-start.5 = (bf16[512,1024]{1,0:T(8,128)(2,1)S(1)}, bf16[512,1024]{1,0:T(8,128)(2,1)}, u32[]{:S(2)}) copy-start(bf16[512,1024]{1,0:T(8,128)(2,1)} %param.24) | copy-start | bytes 3145732
  63.9 1.2 copy-start.10
  64.4 1.3 copy-start.12
  64.4 1.5 copy-start.9
  64.9 14.9 %copy-start.11 = (f32[8,768]{1,0:T(8,128)S(1)}, f32[8,768]{1,0:T(8,128)}, u32[]{:S(2)}) copy-start(f32[8,768]{1,0:T(8,128)} %param.26) | copy-start | bytes 73732
  65.7 1.9 collective-permute-start
  68.6 9.7 %all-to-all-start = ((f32[4,1,512]{2,1,0:T(1,128)}), f32[4,1,512]{2,1,0:T(1,128)S(1)}, u32[]{:S(2)}, u32[]{:S(2)}) async-start(f32[4,1,512]{2,1,0:T(1,128)} %reshape.174), calls=%async_computation | async-start | bytes 16384 | tf_op jit(solution)/shard_map/all_to_all | solution.py:156
  84.6 7.3 %collective-permute-start.1 = (bf16[128,768]{1,0:T(8,128)(2,1)}, bf16[128,768]{1,0:T(8,128)(2,1)}, u32[]{:S(2)}, u32[]{:S(2)}) collective-permute-start(bf16[128,768]{1,0:T(8,128)(2,1)} %bitcast.24), channel_id=1, source_target_pairs={{0,4},{4,8},{8,12},{1,5},{5,9},{9,13},{2,6},{6,10},{10,14},{3,7},{... | collective-permute-start | bytes 589832 | tf_op jit(solution)/shard_map/ppermute | solution.py:31
  87.8 7.9 %collective-permute-start.2 = (bf16[128,768]{1,0:T(8,128)(2,1)}, bf16[128,768]{1,0:T(8,128)(2,1)}, u32[]{:S(2)}, u32[]{:S(2)}) collective-permute-start(bf16[128,768]{1,0:T(8,128)(2,1)} %bitcast.25), channel_id=1, source_target_pairs={{4,0},{8,4},{12,8},{5,1},{9,5},{13,9},{6,2},{10,6},{14,10},{7,3},{... | collective-permute-start | bytes 589832 | tf_op jit(solution)/shard_map/ppermute | solution.py:33
where the time goes:
time: 198 us; the launch traced here: 195 us
  matrix products  84.4 us (43%)
  local copies, waits for them, and re-layouts  44.9 us (23%)
  blocking collectives  35 us (18%)
  other arithmetic  10.7 us (5%)
  waiting for transfers between devices  8.72 us (4%)
  starting transfers between devices  8.59 us (4%)
    dot_general x27, matrix products, add_offset(): jnp.dot(selector, product_rows, precision=TOP_PRECISION)  68.2 us
    dynamic_slice x27, local copies, waits for them, and re-layouts, per_device(): lax.scan(add_offset, start_total, (products, index_maps))  20.7 us
    all_gather x1, blocking collectives, per_device(): key_row_list = lax.all_gather(keys_in, 'seq', axis=0, tiled=True)  18 us
    all_gather x1, blocking collectives, per_device(): value_rows = lax.all_gather(values_in, 'seq', axis=0, tiled=True)  17 us
    unnamed x1, matrix products  8.62 us
    all_to_all x1, waiting for transfers between devices, per_device(): lax.all_to_all(packed, 'seq', split_axis=1, concat_axis=1, tiled=True)  4.99 us
    div x4, local copies, waits for them, and re-layouts, head_norm(): per_head / jnp.sqrt(mean_square + EPSILON)  4.32 us
    all_to_all x1, starting transfers between devices, per_device(): lax.all_to_all(packed, 'seq', split_axis=1, concat_axis=1, tiled=True)  4.11 us
  transfers between devices with their start and end apart: 4, of which 2 were waited for; matrix products, arithmetic and copies ran while one was open for 2% of the time, Pallas kernels for 0%

commit v1 on v0

v1 whole, which is shorter than its diff:
```python
import functools
import math

import jax
import jax.numpy as jnp
import numpy as np
from jax import lax
from jax.experimental import pallas as pl
from jax.experimental.pallas import tpu as pltpu
from jax.sharding import PartitionSpec as P

HEADS = 8
HEAD = 64
LAT = 8
BLK = 16
RES = 64

EPSILON = 1e-06
GUIDANCE = 3.0
TOP_PRECISION = lax.Precision.HIGHEST
F32 = jnp.float32
BF16 = jnp.bfloat16
I32 = jnp.int32

ROW_COORD = 8
ROW_OWNER = 11
ROW_BORDER = 12
PACK_ROWS = 16
WHOLE_ASSET = 512

VMEM = pl.BlockSpec(memory_space=pltpu.VMEM)
SMEM = pl.BlockSpec(memory_space=pltpu.SMEM)


def dot_ab(a, b):
    return jnp.dot(a, b, preferred_element_type=F32)


def dot_abt(a, b):
    return lax.dot_general(a, b, (((1,), (1,)), ((), ())), preferred_element_type=F32)


def dot_atb(a, b):
    return lax.dot_general(a, b, (((0,), (0,)), ((), ())), preferred_element_type=F32)


def split_two(x):
    high = x.astype(BF16).astype(F32)
    return high, x - high


def split_three(x):
    high, rest = split_two(x)
    mid, low = split_two(rest)
    return high, mid, low


@functools.lru_cache(None)
def position_parts(model_width):
    freqs = model_width // 6
    steps = np.arange(freqs, dtype=np.float32) / np.float32(freqs)
    omegas = np.exp(np.float32(-math.log(10000.0)) * steps).astype(np.float32)
    angles = (np.arange(RES, dtype=np.float32)[:, None] * omegas[None, :]).astype(np.float64)
    halves = np.concatenate([np.sin(angles), np.cos(angles)], axis=1).astype(np.float32)
    table = np.zeros((3 * RES, model_width), np.float32)
    for c in range(3):
        table[c * RES : (c + 1) * RES, c * 2 * freqs : (c + 1) * 2 * freqs] = halves
    high = table.astype(jnp.bfloat16)
    low = (table - high.astype(np.float32)).astype(jnp.bfloat16)
    return np.concatenate([high, low], axis=0)


def velocity_kernel(
    own_ref,
    mixed_ref,
    swapped_ref,
    far_ref,
    mod_ref,
    in_ref,
    qkv_ref,
    gain_ref,
    out_ref,
    head_ref,
    pos_ref,
    vel_ref,
    blocks_ref,
    table_ref,
    hidden_ref,
    normed_ref,
    query_ref,
    key_ref,
    value_ref,
    att_ref,
):
    me = lax.axis_index("seq")
    side = lax.axis_index("pair")
    width = in_ref.shape[1]
    tokens = hidden_ref.shape[0]
    inner = out_ref.shape[0]
    block = own_ref.shape[1]

    blocks_ref[me] = own_ref[...]
    blocks_ref[me ^ 3] = far_ref[...]
    blocks_ref[me ^ (1 + side)] = mixed_ref[...]
    blocks_ref[me ^ (2 - side)] = swapped_ref[...]

    pos_rows = pos_ref.shape[0]
    table_ref[0:pos_rows, :] = pos_ref[...]
    in_high, in_low = split_two(in_ref[...])
    table_ref[pos_rows : pos_rows + 32, :] = jnp.concatenate(
        [in_high, in_high, in_low, jnp.zeros_like(in_low)], axis=0
    ).astype(BF16)

    shift = mod_ref[0]
    scale = 1.0 + mod_ref[1]
    for s in range(tokens // block):
        rows = blocks_ref[s]
        values = lax.broadcasted_iota(I32, (RES, block), 0).astype(F32)
        hots = [
            (values == rows[ROW_COORD + c : ROW_COORD + c + 1]).astype(F32).astype(BF16)
            for c in range(3)
        ]
        high, low = split_two(rows[0:LAT])
        tail = jnp.concatenate([high, low, high, jnp.zeros_like(low)], axis=0).astype(BF16)
        picks = jnp.concatenate(hots + hots + [tail], axis=0)
        hidden = dot_atb(picks, table_ref[...])
        hidden_ref[s * block : (s + 1) * block, :] = hidden
        center = hidden - jnp.mean(hidden, axis=1, keepdims=True)
        inverse = lax.rsqrt(jnp.mean(center * center, axis=1, keepdims=True) + EPSILON)
        normed_ref[s * block : (s + 1) * block, :] = (center * inverse * scale + shift).astype(BF16)

    group = 256
    same_head = (
        lax.broadcasted_iota(I32, (group, group), 0) // HEAD
        == lax.broadcasted_iota(I32, (group, group), 1) // HEAD
    )
    averager = jnp.where(same_head, 1.0 / HEAD, 0.0).astype(BF16)
    for j in range(3 * inner // group):
        projected = dot_ab(normed_ref[...], qkv_ref[:, j * group : (j + 1) * group])
        which, col = divmod(j * group, inner)
        if which == 2:
            for half in range(group // 128):
                pair = (col + half * 128) // 128
                value_ref[pair, :, 0:128] = projected[:, half * 128 : (half + 1) * 128].astype(BF16)
                value_ref[pair, :, 128:256] = jnp.ones((tokens, 128), BF16)
        else:
            square = dot_ab((projected * projected).astype(BF16), averager)
            gains = gain_ref[which : which + 1, col : col + group]
            if which == 0:
                gains = gains * (HEAD**-0.5)
            result = (projected * lax.rsqrt(square + EPSILON) * gains).astype(BF16)
            (query_ref, key_ref)[which][:, col : col + group] = result

    chunk = 256
    first = lax.broadcasted_iota(I32, (chunk, 128), 1) < HEAD
    for pair in range(inner // 128):
        lanes = slice(pair * 128, (pair + 1) * 128)
        for q in range(tokens // chunk):
            here = slice(q * chunk, (q + 1) * chunk)
            query = query_ref[here, lanes]
            parts = []
            for half in range(2):
                kept = jnp.where(first == (half == 0), query, jnp.zeros_like(query))
                scores = dot_abt(kept, key_ref[:, lanes])
                weights = jnp.exp(scores).astype(BF16)
                sums = dot_ab(weights, value_ref[pair])
                parts.append(sums[:, 0:128] / sums[:, 128:256])
            att_ref[here, lanes] = jnp.where(first, parts[0], parts[1]).astype(BF16)

    gate = mod_ref[2]
    head = head_ref[...]
    offset = jnp.sum(head * mod_ref[3], axis=1, keepdims=True)
    head_high, head_low = split_two(head * (1.0 + mod_ref[4]))
    heads = jnp.concatenate([head_high, head_low], axis=0).astype(BF16)
    for s in range(tokens // block):
        here = slice(s * block, (s + 1) * block)
        hidden = hidden_ref[here, :] + gate * dot_ab(att_ref[here, :], out_ref[...])
        center = hidden - jnp.mean(hidden, axis=1, keepdims=True)
        inverse = lax.rsqrt(jnp.mean(center * center, axis=1, keepdims=True) + EPSILON)
        final = center * inverse
        final_high, final_low = split_two(final)
        both = dot_abt(heads, final_high.astype(BF16))
        rest = dot_abt(heads, final_low.astype(BF16))
        vel_ref[:, here] = both[0:LAT] + both[LAT:] + rest[0:LAT] + offset


def decode_kernel(
    blocks_ref,
    mine_ref,
    other_ref,
    time_ref,
    proj_ref,
    map_ref,
    weight_ref,
    owned_ref,
    fine_ref,
    product_ref,
):
    me = lax.axis_index("seq")
    is_cond = lax.axis_index("pair") == 0
    count, _, block = blocks_ref.shape
    slots = owned_ref.shape[1]
    capacity = slots // count
    offsets, out_channels, dec_width = weight_ref.shape
    halo = 128
    table_rows = slots + 2 * halo

    mine, other = mine_ref[...], other_ref[...]
    cond = jnp.where(is_cond, mine, other)
    uncond = jnp.where(is_cond, other, mine)
    latents = jnp.concatenate([blocks_ref[s, 0:LAT, :] for s in range(count)], axis=1)
    clean = latents - time_ref[0] * (uncond + GUIDANCE * (cond - uncond))

    owners = jnp.concatenate(
        [blocks_ref[s, ROW_OWNER : ROW_OWNER + 1, :] for s in range(count)], axis=0
    ).astype(I32)
    earlier = (
        lax.broadcasted_iota(I32, (block, block), 0) < lax.broadcasted_iota(I32, (block, block), 1)
    ).astype(F32).astype(BF16)
    starts = lax.broadcasted_iota(I32, (count, block), 0) * capacity
    targets = []
    for step in (0, -1, 1):
        named = owners == me + step
        ranks = dot_ab(named.astype(F32).astype(BF16), earlier).astype(I32)
        slot_of = jnp.where(named, ranks + starts, -1)
        targets.append(jnp.concatenate([slot_of[s : s + 1] for s in range(count)], axis=1))
    tokens = count * block
    rows = lax.broadcasted_iota(I32, (slots, tokens), 0)
    picks = [(rows == targets[0]).astype(F32).astype(BF16)]
    small = lax.broadcasted_iota(I32, (BLK, tokens), 0)
    for step, direction in ((-1, 1), (1, 0)):
        source = jnp.clip(me + step, 0, count - 1)
        border = blocks_ref[source, ROW_BORDER : ROW_BORDER + 1, :].astype(I32)
        target = targets[1 if step < 0 else 2]
        for i in range(halo // BLK):
            at = direction * (halo // BLK) + i
            wanted = border[:, at : at + 1] * BLK
            picks.append((small + wanted == target).astype(F32).astype(BF16))
    picks = jnp.concatenate(picks, axis=0)
    parts = jnp.concatenate(split_three(clean), axis=0).astype(BF16)
    spread = dot_abt(parts, picks)
    table = spread[0:LAT] + spread[LAT : 2 * LAT] + spread[2 * LAT :]
    owned_ref[...] = table[:, 0:slots]

    proj_high, proj_low = split_two(proj_ref[...])
    table_high, table_low = split_two(table)
    left = jnp.concatenate([proj_high, proj_high, proj_low, jnp.zeros_like(proj_low)], axis=0)
    right = jnp.concatenate([table_high, table_low, table_high, jnp.zeros_like(table_low)], axis=0)
    before = dot_atb(left.astype(BF16), right.astype(BF16))
    features = (0.5 * before * (1.0 + jnp.tanh(0.5 * before))).astype(BF16)

    for k in range(offsets):
        product_ref[k] = dot_ab(weight_ref[k], features).astype(BF16)

    fine = map_ref.shape[2]
    width = 256
    table_ids = lax.broadcasted_iota(I32, (table_rows, width), 0)
    for f in range(fine // width):
        here = slice(f * width, (f + 1) * width)
        total = jnp.zeros((out_channels, width), F32)
        for k in range(offsets):
            chosen = (table_ids == map_ref[k, :, here]).astype(F32).astype(BF16)
            total = total + dot_ab(product_ref[k], chosen)
        fine_ref[:, here] = total.astype(BF16)


def swap_pair(x):
    return lax.ppermute(x, "pair", [(0, 1), (1, 0)])


def seq_swap(x, distance_of):
    count = lax.axis_size("seq")
    routes = [
        (p * count + (z ^ distance_of[p]), p * count + z) for p in range(2) for z in range(count)
    ]
    return lax.ppermute(x, ("pair", "seq"), routes)


def whole_asset_velocity(packed, modulation, in_proj, qkv_proj, norm_gain, out_proj, head_proj):
    count = lax.axis_size("seq")
    block = packed.shape[1]
    tokens = count * block
    width = in_proj.shape[1]
    inner = out_proj.shape[0]
    mixed = seq_swap(packed, (1, 2))
    far = seq_swap(packed, (3, 3))
    swapped = swap_pair(mixed)
    pos = jnp.asarray(position_parts(width))
    return pl.pallas_call(
        velocity_kernel,
        out_shape=(
            jax.ShapeDtypeStruct((LAT, tokens), F32),
            jax.ShapeDtypeStruct((count, PACK_ROWS, block), F32),
        ),
        in_specs=[VMEM] * 11,
        out_specs=(VMEM, VMEM),
        scratch_shapes=[
            pltpu.VMEM((pos.shape[0] + 32, width), BF16),
            pltpu.VMEM((tokens, width), F32),
            pltpu.VMEM((tokens, width), BF16),
            pltpu.VMEM((tokens, inner), BF16),
            pltpu.VMEM((tokens, inner), BF16),
            pltpu.VMEM((inner // 128, tokens, 256), BF16),
            pltpu.VMEM((tokens, inner), BF16),
        ],
        compiler_params=pltpu.CompilerParams(vmem_limit_bytes=40 << 20),
        name="velocity",
    )(
        packed,
        mixed,
        swapped,
        far,
        modulation[0, 0][:, None, :],
        in_proj,
        qkv_proj,
        norm_gain,
        out_proj,
        head_proj.T,
        pos,
    )


def layer_norm(values):
    center = values - jnp.mean(values, axis=-1, keepdims=True)
    variance = jnp.mean(center * center, axis=-1, keepdims=True)
    return center / jnp.sqrt(variance + EPSILON)


def position_table(coord_rows, model_width):
    freqs = model_width // 6
    steps = jnp.arange(freqs, dtype=F32) / freqs
    omegas = jnp.exp(-math.log(10000.0) * steps)
    angles = coord_rows.astype(F32)[:, :, None] * omegas[None, None, :]
    halves = jnp.concatenate([jnp.sin(angles), jnp.cos(angles)], axis=2)
    rows_out = jnp.transpose(halves, (1, 0, 2)).reshape(coord_rows.shape[1], 6 * freqs)
    return jnp.pad(rows_out, ((0, 0), (0, model_width - 6 * freqs)))


def head_norm(values, gains):
    row_count = values.shape[0]
    per_head = values.reshape(row_count, HEADS, HEAD)
    mean_square = jnp.mean(per_head * per_head, axis=2, keepdims=True)
    return (per_head / jnp.sqrt(mean_square + EPSILON)).reshape(row_count, HEADS * HEAD) * gains


def gathered_velocity(
    latent_block, coords, modulation, in_proj, qkv_proj, norm_gain, out_proj, head_proj
):
    token_count = latent_block.shape[1]
    model_width = in_proj.shape[1]
    inner_width = out_proj.shape[0]
    factor = HEAD ** (-0.5)
    mod_rows = modulation[0, 0]
    hidden = jnp.dot(latent_block.T, in_proj, precision=TOP_PRECISION) + position_table(
        coords, model_width
    )
    normed = (layer_norm(hidden) * (1.0 + mod_rows[1]) + mod_rows[0]).astype(BF16)
    projected = jnp.dot(normed, qkv_proj, preferred_element_type=F32)
    queries = head_norm(projected[:, :inner_width], norm_gain[0]).astype(BF16)
    keys_in = head_norm(projected[:, inner_width : 2 * inner_width], norm_gain[1]).astype(BF16)
    values_in = projected[:, 2 * inner_width :].astype(BF16)
    query_heads = queries.reshape(token_count, HEADS, HEAD)
    start_pair = (
        jnp.zeros((token_count, HEADS, HEAD), F32),
        jnp.zeros((token_count, HEADS), F32),
    )
    key_rows = lax.all_gather(keys_in, "seq", axis=0, tiled=True)
    value_rows = lax.all_gather(values_in, "seq", axis=0, tiled=True)
    row_count = key_rows.shape[0]
    block_rows = math.gcd(row_count, 512)
    key_blocks = key_rows.reshape(row_count // block_rows, block_rows, HEADS, HEAD)
    value_blocks = value_rows.reshape(row_count // block_rows, block_rows, HEADS, HEAD)

    def one_block(running, block_pair):
        numer_run, denom_run = running
        key_block, value_block = block_pair
        scores = (
            jnp.einsum("qhd,khd->hqk", query_heads, key_block, preferred_element_type=F32) * factor
        )
        exp_scores = jnp.exp(scores)
        numer_run = numer_run + jnp.einsum(
            "hqk,khd->qhd", exp_scores.astype(BF16), value_block, preferred_element_type=F32
        )
        denom_run = denom_run + jnp.sum(exp_scores, axis=2).T
        return ((numer_run, denom_run), None)

    (numerator, denominator), _ = lax.scan(one_block, start_pair, (key_blocks, value_blocks))
    attended = (
        (numerator / denominator[:, :, None]).reshape(token_count, inner_width).astype(BF16)
    )
    hidden = hidden + mod_rows[2] * jnp.dot(attended, out_proj, preferred_element_type=F32)
    final = layer_norm(hidden) * (1.0 + mod_rows[4]) + mod_rows[3]
    velocity = jnp.dot(final, head_proj, precision=TOP_PRECISION).T
    return lax.all_gather(velocity, "seq", axis=1, tiled=True)


def per_device(
    latents,
    voxel_coords,
    owner_map,
    step_time,
    modulation,
    in_proj,
    qkv_proj,
    norm_gain,
    out_proj,
    head_proj,
    decoder_projection,
    border_blocks,
    kernel_map,
    conv_weight,
):
    count = lax.axis_size("seq")
    block = latents.shape[2]
    chosen = border_blocks.reshape(1, -1)
    packed = jnp.concatenate(
        [
            latents[0],
            voxel_coords[0].astype(F32),
            owner_map[0].reshape(1, block).astype(F32),
            jnp.pad(chosen, ((0, 0), (0, block - chosen.shape[1]))).astype(F32),
            jnp.zeros((PACK_ROWS - ROW_BORDER - 1, block), F32),
        ],
        axis=0,
    )
    if count == 4 and count * block <= WHOLE_ASSET:
        velocity, blocks = whole_asset_velocity(
            packed, modulation, in_proj, qkv_proj, norm_gain, out_proj, head_proj
        )
    else:
        blocks = lax.all_gather(packed, "seq", axis=0)
        velocity = gathered_velocity(
            latents[0],
            voxel_coords[0],
            modulation,
            in_proj,
            qkv_proj,
            norm_gain,
            out_proj,
            head_proj,
        )
    partner = swap_pair(velocity)
    offsets, _, out_channels = conv_weight.shape
    fine = kernel_map.shape[3]
    slots = fine // 4
    table_rows = slots + 2 * border_blocks.shape[3] * BLK
    owned, decoded = pl.pallas_call(
        decode_kernel,
        out_shape=(
            jax.ShapeDtypeStruct((LAT, slots), F32),
            jax.ShapeDtypeStruct((out_channels, fine), BF16),
        ),
        in_specs=[VMEM, VMEM, VMEM, SMEM, VMEM, VMEM, VMEM],
        out_specs=(VMEM, VMEM),
        scratch_shapes=[pltpu.VMEM((offsets, out_channels, table_rows), BF16)],
        compiler_params=pltpu.CompilerParams(vmem_limit_bytes=40 << 20),
        name="decode",
    )(
        blocks,
        velocity,
        partner,
        step_time,
        decoder_projection,
        kernel_map.reshape(offsets, 1, fine),
        jnp.swapaxes(conv_weight, 1, 2),
    )
    return (owned[None, None], decoded.T[None, None])


def solution(mesh):
    placed = (
        P("asset", None, "seq"),
        P("asset", None, "seq"),
        P("asset", "seq", None),
        P("asset"),
        P("asset", "pair", None, None),
        P(),
        P(),
        P(),
        P(),
        P(),
        P(),
        P("asset", "seq", None, None),
        P("asset", "seq", None, None),
        P(None, None, "pair"),
    )
    return jax.shard_map(
        per_device,
        mesh=mesh,
        in_specs=placed,
        out_specs=(P("asset", "seq", None, None), P("asset", "seq", None, "pair")),
        check_vma=False,
    )
```

time: 198 us -> 39.7 us (0.20); the launches traced: 195 us -> 39.2 us
  matrix products: 84.4 us -> 0 us
  local copies, waits for them, and re-layouts: 44.9 us -> 8.66 us
  blocking collectives: 35 us -> 0 us
  Pallas kernels: 0 us -> 18.7 us
  other arithmetic: 10.7 us -> 1.35 us
  waiting for transfers between devices: 8.72 us -> 3.5 us
  starting transfers between devices: 8.59 us -> 5.6 us
    dot_general x35 -> x0, matrix products: 75.8 us -> none  [the longest x27 68.2 us: add_offset(): jnp.dot(selector, product_rows, precision=TOP_PRECISION)]
    all_gather x2 -> x0, blocking collectives: 35 us -> none  [the longest x1 18 us: per_device(): key_row_list = lax.all_gather(keys_in, 'seq', axis=0, tiled=True)]
    dynamic_slice x27 -> x0, local copies, waits for them, and re-layouts: 20.7 us -> none  [per_device(): lax.scan(add_offset, start_total, (products, index_maps))]
    pallas_call x0 -> x2, Pallas kernels: none -> 18.7 us  [the longest x1 9.74 us: per_device(): pl.pallas_call(decode_kernel, out_shape=(jax.ShapeDtypeStruct((LAT, slots...]
    unnamed x1 -> x0, matrix products: 8.62 us -> none
    all_to_all x1 -> x0, waiting for transfers between devices: 4.99 us -> none  [per_device(): lax.all_to_all(packed, 'seq', split_axis=1, concat_axis=1, tiled=True)]
    unnamed x30 -> x20, local copies, waits for them, and re-layouts: 2.53 us -> 7.19 us
    div x4 -> x0, local copies, waits for them, and re-layouts: 4.32 us -> none  [head_norm(): per_head / jnp.sqrt(mean_square + EPSILON)]
  transfers between devices with their start and end apart: 4 -> 4, of which waited for: 2 -> 2; matrix products, arithmetic and copies ran while one was open for 2% -> 0% of each run, Pallas kernels for 0% -> 0%
where the time goes in v1:
time: 39.7 us; the launch traced here: 39.2 us
  Pallas kernels  18.7 us (47%)
  local copies, waits for them, and re-layouts  8.66 us (22%)
  starting transfers between devices  5.6 us (14%)
  waiting for transfers between devices  3.5 us (9%)
  other arithmetic  1.35 us (3%)
  between operations  1.31 us (3%)
    pallas_call x1, Pallas kernels, per_device(): pl.pallas_call(decode_kernel, out_shape=(jax.ShapeDtypeStruct((LAT, slots...  9.74 us
    pallas_call x1, Pallas kernels, whole_asset_velocity(): pl.pallas_call(velocity_kernel, out_shape=(jax.ShapeDtypeStruct((LAT, tok...  8.99 us
    unnamed x20, local copies, waits for them, and re-layouts  7.19 us
    ppermute x2, starting transfers between devices, seq_swap(): return lax.ppermute(x, ('pair', 'seq'), routes)  5.56 us
    ppermute x2, waiting for transfers between devices, seq_swap(): return lax.ppermute(x, ('pair', 'seq'), routes)  2.97 us
  transfers between devices with their start and end apart: 4, of which 2 were waited for; matrix products, arithmetic and copies ran while one was open for 0% of the time, Pallas kernels for 0%

profile of v1, /device:TPU:0, one launch (start us, length us, event | category | flops | bytes accessed | tf_op | source)
XLA Modules:
  0.0 39.2 jit_solution(8305255334621496187)
XLA Ops:
  0.6 0.0 copy-start.7
  0.6 0.7 %convert_bitcast_fusion = f32[1,128]{1,0:T(1,128)S(1)} fusion(s32[1,128,1]{1,2,0:T(1,128)} %param.17), kind=kLoop, calls=%fused_computation.3 | loop fusion | flops 128 | bytes 1024 | tf_op jit(solution)/shard_map/convert_element_type | solution.py:420
  1.3 0.8 %reshape.24 = s32[1,16]{1,0:T(1,128)S(1)} reshape(s32[1,1,2,8]{3,2,1,0:T(2,128)} %param.26) | data formatting | bytes 128 | tf_op jit(solution)/shard_map/reshape | solution.py:415
  2.1 0.7 %fusion = f32[3,128]{1,0:T(4,128)S(1)} fusion(s32[1,3,128]{2,0,1:T(1,128)} %param.16), kind=kLoop, calls=%fused_computation.1 | loop fusion | flops 384 | bytes 3072 | tf_op jit(solution)/shard_map/convert_element_type | solution.py:419
  2.8 0.7 %concatenate.3.own_ref = f32[16,128]{1,0:T(8,128)S(1)} concatenate(f32[8,128]{1,0:T(8,128)} %bitcast.17, f32[3,128]{1,0:T(4,128)S(1)} %fusion, f32[1,128]{1,0:T(1,128)S(1)} %convert_bitcast_fusion, f32[1,128]{1,0:T(1,128)S(1)} %pad_convert_fusion, f32[3,128]{1,0:T(4,128)S(1)} %broadcast_in_dim.9), dimensions={0} | concatenate | bytes 16384 | tf_op jit(solution)/shard_map/concatenate | solution.py:416
  3.5 0.0 copy-start
  3.5 3.1 %collective-permute-start = (f32[16,128]{1,0:T(8,128)S(1)}, f32[16,128]{1,0:T(8,128)S(1)}, u32[]{:S(2)}, u32[]{:S(2)}) collective-permute-start(f32[16,128]{1,0:T(8,128)S(1)} %concatenate.3.own_ref), channel_id=1, source_target_pairs={{4,0},{0,4},{12,8},{8,12},{24,16},{28,20},{16,24},{20,28},{5,1},{1... | collective-permute-start | bytes 24584 | tf_op jit(solution)/shard_map/ppermute | solution.py:276
  6.6 2.5 %collective-permute-start.2 = (f32[16,128]{1,0:T(8,128)S(1)}, f32[16,128]{1,0:T(8,128)S(1)}, u32[]{:S(2)}, u32[]{:S(2)}) collective-permute-start(f32[16,128]{1,0:T(8,128)S(1)} %concatenate.3.own_ref), channel_id=1, source_target_pairs={{12,0},{8,4},{4,8},{0,12},{28,16},{24,20},{20,24},{16,28},{13,1},{... | collective-permute-start | bytes 24584 | tf_op jit(solution)/shard_map/ppermute | solution.py:276
  9.0 0.0 collective-permute-done.mixed_ref
  9.0 0.0 collective-permute-start.1
  9.0 3.0 %collective-permute-done.2.far_ref = f32[16,128]{1,0:T(8,128)S(1)} collective-permute-done((f32[16,128]{1,0:T(8,128)S(1)}, f32[16,128]{1,0:T(8,128)S(1)}, u32[]{:S(2)}, u32[]{:S(2)}) %collective-permute-start.2) | collective-permute-done | bytes 8224 | tf_op jit(solution)/shard_map/ppermute | solution.py:276
  12.0 0.0 collective-permute-done.1.swapped_ref
  12.0 0.0 copy-start.1
  12.0 1.9 %copy-done.1 = bf16[1024,1536]{1,0:T(8,128)(2,1)S(1)} copy-done((bf16[1024,1536]{1,0:T(8,128)(2,1)S(1)}, bf16[1024,1536]{1,0:T(8,128)(2,1)}, u32[]{:S(2)}) %copy-start.1) | copy-done | bytes 3145752
  13.9 0.0 copy-start.2
  13.9 1.2 %copy-done.2 = bf16[512,1024]{1,0:T(8,128)(2,1)S(1)} copy-done((bf16[512,1024]{1,0:T(8,128)(2,1)S(1)}, bf16[512,1024]{1,0:T(8,128)(2,1)}, u32[]{:S(2)}) %copy-start.2) | copy-done | bytes 1048600
  15.1 0.0 copy-start.3
  15.1 1.1 %copy-done.3 = bf16[384,1024]{1,0:T(8,128)(2,1)S(1)} copy-done((bf16[384,1024]{1,0:T(8,128)(2,1)S(1)}, bf16[384,1024]{1,0:T(8,128)(2,1)}, u32[]{:S(2)}) %copy-start.3) | copy-done | bytes 786456
  16.3 0.0 copy-start.5
  16.3 0.8 %copy-done.5 = f32[8,1024]{1,0:T(8,128)S(1)} copy-done((f32[8,1024]{1,0:T(8,128)S(1)}, f32[8,1024]{1,0:T(8,128)}, u32[]{:S(2)}) %copy-start.5) | copy-done | bytes 32792
  17.0 0.0 copy-start.6
  17.0 0.8 %copy-done.6 = f32[1024,8]{0,1:T(8,128)S(1)} copy-done((f32[1024,8]{0,1:T(8,128)S(1)}, f32[1024,8]{0,1:T(8,128)}, u32[]{:S(2)}) %copy-start.6) | copy-done | bytes 32792
  17.8 0.0 copy-start.8
  17.8 0.7 %copy-done.8 = f32[1,1,5,1024]{3,1,2,0:T(1,128)S(1)} copy-done((f32[1,1,5,1024]{3,1,2,0:T(1,128)S(1)}, f32[1,1,5,1024]{3,1,2,0:T(1,128)}, u32[]{:S(2)}) %copy-start.8) | copy-done | bytes 20504
  18.5 0.0 copy-start.9
  18.5 0.7 %copy-done.9 = f32[2,512]{1,0:T(2,128)S(1)} copy-done((f32[2,512]{1,0:T(2,128)S(1)}, f32[2,512]{1,0:T(2,128)}, u32[]{:S(2)}) %copy-start.9) | copy-done | bytes 4120
  19.2 0.0 copy-start.4
  19.2 9.0 %velocity.1 = (f32[8,512]{1,0:T(8,128)S(1)}, f32[4,16,128]{2,1,0:T(8,128)S(1)}) custom-call(f32[16,128]{1,0:T(8,128)S(1)} %concatenate.3.own_ref, f32[16,128]{1,0:T(8,128)S(1)} %collective-permute-done.mixed_ref, f32[16,128]{1,0:T(8,128)S(1)} %collective-permute-done.1.swapped_ref, f32[16,128]{1,0:T(8,128)S(1)} %collective-permute-done.2.far_ref, ...), custom_call_target="tpu_custom_call" | custom-call | tf_op jit(solution)/shard_map/velocity/pallas_call | solution.py:289
  28.2 0.0 collective-permute-start.3
  28.9 0.5 %collective-permute-done.3.other_ref = f32[8,512]{1,0:T(8,128)S(1)} collective-permute-done((f32[8,512]{1,0:T(8,128)S(1)}, f32[8,512]{1,0:T(8,128)S(1)}, u32[]{:S(2)}, u32[]{:S(2)}) %collective-permute-start.3) | collective-permute-done | bytes 16416 | tf_op jit(solution)/shard_map/ppermute | solution.py:268
  29.4 0.0 copy-done.7
  29.4 0.0 copy-done
  29.4 0.0 copy-done.4
  29.4 9.7 %decode.1 = (f32[8,256]{1,0:T(8,128)}, bf16[96,1024]{1,0:T(8,128)(2,1)}) custom-call(f32[4,16,128]{2,1,0:T(8,128)S(1)} %get-tuple-element.6.blocks_ref, f32[8,512]{1,0:T(8,128)S(1)} %get-tuple-element.7.mine_ref, f32[8,512]{1,0:T(8,128)S(1)} %collective-permute-done.3.other_ref, f32[1]{0:T(128)S(6)} %copy.21.time_ref, f32[8,768]{1,0:T(8,128)S(1)} %copy-done.7, ...), custom_call_target="tpu_custom_call" | custom-call | tf_op jit(solution)/shard_map/decode/pallas_call | solution.py:447
  (2 shorter events, 0.0 us)
Async XLA Ops:
  0.6 28.8 %copy-start.7 = (f32[8,768]{1,0:T(8,128)S(1)}, f32[8,768]{1,0:T(8,128)}, u32[]{:S(2)}) copy-start(f32[8,768]{1,0:T(8,128)} %proj_ref.1) | copy-start | bytes 73732
  3.5 25.9 %copy-start = (bf16[27,768,96]{1,2,0:T(8,128)(2,1)S(1)}, bf16[27,768,96]{1,2,0:T(8,128)(2,1)}, u32[]{:S(2)}) copy-start(bf16[27,768,96]{1,2,0:T(8,128)(2,1)} %param.28) | copy-start | bytes 11943940
  3.5 5.6 %collective-permute-start = (f32[16,128]{1,0:T(8,128)S(1)}, f32[16,128]{1,0:T(8,128)S(1)}, u32[]{:S(2)}, u32[]{:S(2)}) collective-permute-start(f32[16,128]{1,0:T(8,128)S(1)} %concatenate.3.own_ref), channel_id=1, source_target_pairs={{4,0},{0,4},{12,8},{8,12},{24,16},{28,20},{16,24},{20,28},{5,1},{1... | collective-permute-start | bytes 24584 | tf_op jit(solution)/shard_map/ppermute | solution.py:276
  6.6 5.4 %collective-permute-start.2 = (f32[16,128]{1,0:T(8,128)S(1)}, f32[16,128]{1,0:T(8,128)S(1)}, u32[]{:S(2)}, u32[]{:S(2)}) collective-permute-start(f32[16,128]{1,0:T(8,128)S(1)} %concatenate.3.own_ref), channel_id=1, source_target_pairs={{12,0},{8,4},{4,8},{0,12},{28,16},{24,20},{20,24},{16,28},{13,1},{... | collective-permute-start | bytes 24584 | tf_op jit(solution)/shard_map/ppermute | solution.py:276
  9.0 3.0 %collective-permute-start.1 = (f32[16,128]{1,0:T(8,128)S(1)}, f32[16,128]{1,0:T(8,128)S(1)}, u32[]{:S(2)}, u32[]{:S(2)}) collective-permute-start(f32[16,128]{1,0:T(8,128)S(1)} %collective-permute-done.mixed_ref), channel_id=1, source_target_pairs={{0,16},{16,0},{1,17},{17,1},{2,18},{18,2},{3,19},{19,3},{4,20},{20... | collective-permute-start | bytes 24584 | tf_op jit(solution)/shard_map/ppermute | solution.py:268
  12.0 1.9 %copy-start.1 = (bf16[1024,1536]{1,0:T(8,128)(2,1)S(1)}, bf16[1024,1536]{1,0:T(8,128)(2,1)}, u32[]{:S(2)}) copy-start(bf16[1024,1536]{1,0:T(8,128)(2,1)} %qkv_ref.1) | copy-start | bytes 9437188
  13.9 1.2 %copy-start.2 = (bf16[512,1024]{1,0:T(8,128)(2,1)S(1)}, bf16[512,1024]{1,0:T(8,128)(2,1)}, u32[]{:S(2)}) copy-start(bf16[512,1024]{1,0:T(8,128)(2,1)} %out_ref.1) | copy-start | bytes 3145732
  15.1 1.1 %copy-start.3 = (bf16[384,1024]{1,0:T(8,128)(2,1)S(1)}, bf16[384,1024]{1,0:T(8,128)(2,1)}, u32[]{:S(2)}) copy-start(bf16[384,1024]{1,0:T(8,128)(2,1)} %constant.6.clone.pos_ref) | copy-start | bytes 2359300
  16.3 0.8 %copy-start.5 = (f32[8,1024]{1,0:T(8,128)S(1)}, f32[8,1024]{1,0:T(8,128)}, u32[]{:S(2)}) copy-start(f32[8,1024]{1,0:T(8,128)} %in_ref.1) | copy-start | bytes 98308
  17.0 0.8 %copy-start.6 = (f32[1024,8]{0,1:T(8,128)S(1)}, f32[1024,8]{0,1:T(8,128)}, u32[]{:S(2)}) copy-start(f32[1024,8]{0,1:T(8,128)} %param.24) | copy-start | bytes 98308
  17.8 0.7 %copy-start.8 = (f32[1,1,5,1024]{3,1,2,0:T(1,128)S(1)}, f32[1,1,5,1024]{3,1,2,0:T(1,128)}, u32[]{:S(2)}) copy-start(f32[1,1,5,1024]{3,1,2,0:T(1,128)} %param.19) | copy-start | bytes 61444
  18.5 0.7 %copy-start.9 = (f32[2,512]{1,0:T(2,128)S(1)}, f32[2,512]{1,0:T(2,128)}, u32[]{:S(2)}) copy-start(f32[2,512]{1,0:T(2,128)} %gain_ref.1) | copy-start | bytes 12292
  19.2 10.2 %copy-start.4 = (s32[1,1,27,1024]{3,1,2,0:T(1,128)S(1)}, s32[1,1,27,1024]{3,1,2,0:T(1,128)}, u32[]{:S(2)}) copy-start(s32[1,1,27,1024]{3,1,2,0:T(1,128)} %param.27) | copy-start | bytes 331780
  28.2 1.2 %collective-permute-start.3 = (f32[8,512]{1,0:T(8,128)S(1)}, f32[8,512]{1,0:T(8,128)S(1)}, u32[]{:S(2)}, u32[]{:S(2)}) collective-permute-start(f32[8,512]{1,0:T(8,128)S(1)} %get-tuple-element.7.mine_ref), channel_id=1, source_target_pairs={{0,16},{16,0},{1,17},{17,1},{2,18},{18,2},{3,19},{19,3},{4,20},{20... | collective-permute-start | bytes 49160 | tf_op jit(solution)/shard_map/ppermute | solution.py:268

commit v2 on v1

--- a/solution.py
+++ b/solution.py
@@ -28,7 +28,10 @@
 PACK_ROWS = 16
 WHOLE_ASSET = 512
 
+VMEM_GRANT = 40 << 20
+
 VMEM = pl.BlockSpec(memory_space=pltpu.VMEM)
+HBM = pl.BlockSpec(memory_space=pltpu.HBM)
 SMEM = pl.BlockSpec(memory_space=pltpu.SMEM)
 
 
@@ -42,6 +45,10 @@
 
 def dot_atb(a, b):
     return lax.dot_general(a, b, (((0,), (0,)), ((), ())), preferred_element_type=F32)
+
+
+def in_hbm(*arrays):
+    return [pltpu.with_memory_space_constraint(x, pltpu.HBM) for x in arrays]
 
 
 def split_two(x):
@@ -70,20 +77,51 @@
     return np.concatenate([high, low], axis=0)
 
 
+def pack_kernel(
+    lat_hbm, coord_hbm, owner_hbm, border_hbm, pack_ref, coord_ref, owner_ref, border_ref, sems
+):
+    pack_ref[...] = jnp.zeros_like(pack_ref)
+    copies = [
+        pltpu.make_async_copy(source, target, sems.at[i])
+        for i, (source, target) in enumerate(
+            (
+                (lat_hbm, pack_ref.at[0:LAT]),
+                (coord_hbm, coord_ref),
+                (owner_hbm, owner_ref),
+                (border_hbm, border_ref),
+            )
+        )
+    ]
+    for copy in copies:
+        copy.start()
+    for copy in copies:
+        copy.wait()
+    for c in range(3):
+        pack_ref[ROW_COORD + c : ROW_COORD + c + 1] = coord_ref[c].astype(F32)
+    pack_ref[ROW_OWNER : ROW_OWNER + 1] = owner_ref[...].astype(F32)
+    pack_ref[ROW_BORDER : ROW_BORDER + 2, 0 : border_ref.shape[1]] = border_ref[...].astype(F32)
+
+
 def velocity_kernel(
     own_ref,
     mixed_ref,
     swapped_ref,
     far_ref,
+    mod_hbm,
+    in_hbm,
+    qkv_hbm,
+    gain_hbm,
+    out_hbm,
+    head_hbm,
+    pos_hbm,
+    vel_ref,
+    blocks_ref,
     mod_ref,
     in_ref,
     qkv_ref,
     gain_ref,
     out_ref,
     head_ref,
-    pos_ref,
-    vel_ref,
-    blocks_ref,
     table_ref,
     hidden_ref,
     normed_ref,
@@ -91,7 +129,25 @@
     key_ref,
     value_ref,
     att_ref,
+    sems,
 ):
+    pos_rows = pos_hbm.shape[0]
+    copies = [
+        pltpu.make_async_copy(source, target, sems.at[i])
+        for i, (source, target) in enumerate(
+            (
+                (pos_hbm, table_ref.at[0:pos_rows]),
+                (in_hbm, in_ref),
+                (mod_hbm, mod_ref),
+                (gain_hbm, gain_ref),
+                (head_hbm, head_ref),
+                (qkv_hbm, qkv_ref),
+                (out_hbm, out_ref),
+            )
+        )
+    ]
+    for copy in copies:
+        copy.start()
     me = lax.axis_index("seq")
     side = lax.axis_index("pair")
     width = in_ref.shape[1]
@@ -104,8 +160,8 @@
     blocks_ref[me ^ (1 + side)] = mixed_ref[...]
     blocks_ref[me ^ (2 - side)] = swapped_ref[...]
 
-    pos_rows = pos_ref.shape[0]
-    table_ref[0:pos_rows, :] = pos_ref[...]
+    for copy in copies[:5]:
+        copy.wait()
     in_high, in_low = split_two(in_ref[...])
     table_ref[pos_rows : pos_rows + 32, :] = jnp.concatenate(
         [in_high, in_high, in_low, jnp.zeros_like(in_low)], axis=0
@@ -129,6 +185,8 @@
         inverse = lax.rsqrt(jnp.mean(center * center, axis=1, keepdims=True) + EPSILON)
         normed_ref[s * block : (s + 1) * block, :] = (center * inverse * scale + shift).astype(BF16)
 
+    copies[5].wait()
+    copies[6].wait()
     group = 256
     same_head = (
         lax.broadcasted_iota(I32, (group, group), 0) // HEAD
@@ -189,21 +247,34 @@
     mine_ref,
     other_ref,
     time_ref,
+    proj_hbm,
+    map_hbm,
+    weight_hbm,
+    owned_ref,
+    fine_ref,
     proj_ref,
     map_ref,
     weight_ref,
-    owned_ref,
-    fine_ref,
     product_ref,
+    sems,
 ):
+    copies = [
+        pltpu.make_async_copy(source, target, sems.at[i])
+        for i, (source, target) in enumerate(
+            ((proj_hbm, proj_ref), (weight_hbm, weight_ref), (map_hbm, map_ref))
+        )
+    ]
+    for copy in copies:
+        copy.start()
     me = lax.axis_index("seq")
     is_cond = lax.axis_index("pair") == 0
     count, _, block = blocks_ref.shape
     slots = owned_ref.shape[1]
     capacity = slots // count
-    offsets, out_channels, dec_width = weight_ref.shape
-    halo = 128
-    table_rows = slots + 2 * halo
+    offsets = map_ref.shape[0]
+    out_channels = fine_ref.shape[0]
+    table_rows = product_ref.shape[1]
+    halo = (table_rows - slots) // 2
 
     mine, other = mine_ref[...], other_ref[...]
     cond = jnp.where(is_cond, mine, other)
@@ -230,11 +301,10 @@
     small = lax.broadcasted_iota(I32, (BLK, tokens), 0)
     for step, direction in ((-1, 1), (1, 0)):
         source = jnp.clip(me + step, 0, count - 1)
-        border = blocks_ref[source, ROW_BORDER : ROW_BORDER + 1, :].astype(I32)
+        border = blocks_ref[source, ROW_BORDER : ROW_BORDER + 2, :].astype(I32)
         target = targets[1 if step < 0 else 2]
         for i in range(halo // BLK):
-            at = direction * (halo // BLK) + i
-            wanted = border[:, at : at + 1] * BLK
+            wanted = border[direction : direction + 1, i : i + 1] * BLK
             picks.append((small + wanted == target).astype(F32).astype(BF16))
     picks = jnp.concatenate(picks, axis=0)
     parts = jnp.concatenate(split_three(clean), axis=0).astype(BF16)
@@ -242,6 +312,7 @@
     table = spread[0:LAT] + spread[LAT : 2 * LAT] + spread[2 * LAT :]
     owned_ref[...] = table[:, 0:slots]
 
+    copies[0].wait()
     proj_high, proj_low = split_two(proj_ref[...])
     table_high, table_low = split_two(table)
     left = jnp.concatenate([proj_high, proj_high, proj_low, jnp.zeros_like(proj_low)], axis=0)
@@ -249,9 +320,12 @@
     before = dot_atb(left.astype(BF16), right.astype(BF16))
     features = (0.5 * before * (1.0 + jnp.tanh(0.5 * before))).astype(BF16)
 
-    for k in range(offsets):
-        product_ref[k] = dot_ab(weight_ref[k], features).astype(BF16)
-
+    copies[1].wait()
+    step = 9 * out_channels
+    for k in range(0, offsets * out_channels, step):
+        product_ref[k : k + step] = dot_ab(weight_ref[k : k + step], features).astype(BF16)
+
+    copies[2].wait()
     fine = map_ref.shape[2]
     width = 256
     table_ids = lax.broadcasted_iota(I32, (table_rows, width), 0)
@@ -260,7 +334,8 @@
         total = jnp.zeros((out_channels, width), F32)
         for k in range(offsets):
             chosen = (table_ids == map_ref[k, :, here]).astype(F32).astype(BF16)
-            total = total + dot_ab(product_ref[k], chosen)
+            products = product_ref[k * out_channels : (k + 1) * out_channels]
+            total = total + dot_ab(products, chosen)
         fine_ref[:, here] = total.astype(BF16)
 
 
@@ -289,12 +364,18 @@
     return pl.pallas_call(
         velocity_kernel,
         out_shape=(
-            jax.ShapeDtypeStruct((LAT, tokens), F32),
-            jax.ShapeDtypeStruct((count, PACK_ROWS, block), F32),
+            pltpu.VMEM((LAT, tokens), F32),
+            pltpu.VMEM((count, PACK_ROWS, block), F32),
         ),
-        in_specs=[VMEM] * 11,
+        in_specs=[VMEM] * 4 + [HBM] * 7,
         out_specs=(VMEM, VMEM),
         scratch_shapes=[
+            pltpu.VMEM((5, 1, width), F32),
+            pltpu.VMEM(in_proj.shape, F32),
+            pltpu.VMEM(qkv_proj.shape, BF16),
+            pltpu.VMEM(norm_gain.shape, F32),
+            pltpu.VMEM(out_proj.shape, BF16),
+            pltpu.VMEM((LAT, width), F32),
             pltpu.VMEM((pos.shape[0] + 32, width), BF16),
             pltpu.VMEM((tokens, width), F32),
             pltpu.VMEM((tokens, width), BF16),
@@ -302,21 +383,24 @@
             pltpu.VMEM((tokens, inner), BF16),
             pltpu.VMEM((inner // 128, tokens, 256), BF16),
             pltpu.VMEM((tokens, inner), BF16),
+            pltpu.SemaphoreType.DMA((7,)),
         ],
-        compiler_params=pltpu.CompilerParams(vmem_limit_bytes=40 << 20),
+        compiler_params=pltpu.CompilerParams(vmem_limit_bytes=VMEM_GRANT),
         name="velocity",
     )(
         packed,
         mixed,
         swapped,
         far,
-        modulation[0, 0][:, None, :],
-        in_proj,
-        qkv_proj,
-        norm_gain,
-        out_proj,
-        head_proj.T,
-        pos,
+        *in_hbm(
+            modulation[0, 0][:, None, :],
+            in_proj,
+            qkv_proj,
+            norm_gain,
+            out_proj,
+            head_proj.T,
+            pos,
+        ),
     )
 
 
@@ -412,16 +496,26 @@
 ):
     count = lax.axis_size("seq")
     block = latents.shape[2]
-    chosen = border_blocks.reshape(1, -1)
-    packed = jnp.concatenate(
-        [
+    packed = pl.pallas_call(
+        pack_kernel,
+        out_shape=pltpu.VMEM((PACK_ROWS, block), F32),
+        in_specs=[HBM] * 4,
+        out_specs=VMEM,
+        scratch_shapes=[
+            pltpu.VMEM((3, 1, block), I32),
+            pltpu.VMEM((1, block), I32),
+            pltpu.VMEM(border_blocks.shape[2:], I32),
+            pltpu.SemaphoreType.DMA((4,)),
+        ],
+        compiler_params=pltpu.CompilerParams(vmem_limit_bytes=VMEM_GRANT),
+        name="pack",
+    )(
+        *in_hbm(
             latents[0],
-            voxel_coords[0].astype(F32),
-            owner_map[0].reshape(1, block).astype(F32),
-            jnp.pad(chosen, ((0, 0), (0, block - chosen.shape[1]))).astype(F32),
-            jnp.zeros((PACK_ROWS - ROW_BORDER - 1, block), F32),
-        ],
-        axis=0,
+            jnp.swapaxes(voxel_coords, 0, 1),
+            owner_map.reshape(1, block),
+            border_blocks[0, 0],
+        )
     )
     if count == 4 and count * block <= WHOLE_ASSET:
         velocity, blocks = whole_asset_velocity(
@@ -450,19 +544,27 @@
             jax.ShapeDtypeStruct((LAT, slots), F32),
             jax.ShapeDtypeStruct((out_channels, fine), BF16),
         ),
-        in_specs=[VMEM, VMEM, VMEM, SMEM, VMEM, VMEM, VMEM],
+        in_specs=[VMEM, VMEM, VMEM, SMEM, HBM, HBM, HBM],
         out_specs=(VMEM, VMEM),
-        scratch_shapes=[pltpu.VMEM((offsets, out_channels, table_rows), BF16)],
-        compiler_params=pltpu.CompilerParams(vmem_limit_bytes=40 << 20),
+        scratch_shapes=[
+            pltpu.VMEM(decoder_projection.shape, F32),
+            pltpu.VMEM((offsets, 1, fine), I32),
+            pltpu.VMEM((offsets * out_channels, decoder_projection.shape[1]), BF16),
+            pltpu.VMEM((offsets * out_channels, table_rows), BF16),
+            pltpu.SemaphoreType.DMA((3,)),
+        ],
+        compiler_params=pltpu.CompilerParams(vmem_limit_bytes=VMEM_GRANT),
         name="decode",
     )(
         blocks,
         velocity,
         partner,
         step_time,
-        decoder_projection,
-        kernel_map.reshape(offsets, 1, fine),
-        jnp.swapaxes(conv_weight, 1, 2),
+        *in_hbm(
+            decoder_projection,
+            kernel_map.reshape(offsets, 1, fine),
+            jnp.swapaxes(conv_weight, 1, 2).reshape(offsets * out_channels, -1),
+        ),
     )
     return (owned[None, None], decoded.T[None, None])
 

time: 39.7 us -> 32.6 us (0.82)
  local copies, waits for them, and re-layouts: 8.66 us -> 0 us
  Pallas kernels: 18.7 us -> 22 us
  other arithmetic: 1.35 us -> 0 us
    unnamed x20 -> x0, local copies, waits for them, and re-layouts: 7.19 us -> none
    pallas_call x1 -> x2, Pallas kernels: 8.99 us -> 11.4 us  [the longest x1 10.7 us: whole_asset_velocity(): pl.pallas_call(velocity_kernel, out_shape=(pltpu.VMEM((LAT, tokens), F32)...]
    convert_element_type x3 -> x0, other arithmetic: 1.35 us -> none  [the longest x1 0.68 us: per_device(): voxel_coords[0].astype(F32)]
    pallas_call x1, Pallas kernels: 9.74 us -> 10.5 us  [per_device(): pl.pallas_call(decode_kernel, out_shape=(jax.ShapeDtypeStruct((LAT, slots...]
    reshape x1 -> x0, local copies, waits for them, and re-layouts: 0.76 us -> none  [per_device(): chosen = border_blocks.reshape(1, -1)]
    concatenate x1 -> x0, local copies, waits for them, and re-layouts: 0.71 us -> none  [per_device(): jnp.concatenate([latents[0], voxel_coords[0].astype(F32), owner_map[0].re...]
where the time goes in v2:
time: 32.6 us; the launch traced here: 32.4 us
  Pallas kernels  22 us (67%)
  starting transfers between devices  5.64 us (17%)
  waiting for transfers between devices  3.5 us (11%)
  between operations  1.3 us (4%)
    pallas_call x1, Pallas kernels, whole_asset_velocity(): pl.pallas_call(velocity_kernel, out_shape=(pltpu.VMEM((LAT, tokens), F32)...  10.7 us
    pallas_call x1, Pallas kernels, per_device(): pl.pallas_call(decode_kernel, out_shape=(jax.ShapeDtypeStruct((LAT, slots...  10.5 us
    ppermute x2, starting transfers between devices, seq_swap(): return lax.ppermute(x, ('pair', 'seq'), routes)  5.56 us
    ppermute x2, waiting for transfers between devices, seq_swap(): return lax.ppermute(x, ('pair', 'seq'), routes)  2.97 us
    pallas_call x1, Pallas kernels, per_device(): pl.pallas_call(pack_kernel, out_shape=pltpu.VMEM((PACK_ROWS, block), F32)...  0.77 us
  transfers between devices with their start and end apart: 4, of which 2 were waited for; matrix products, arithmetic and copies ran while one was open for 0% of the time, Pallas kernels for 0%

profile of v2, /device:TPU:0, one launch (start us, length us, event | category | flops | bytes accessed | tf_op | source)
XLA Modules:
  0.0 32.4 jit_solution(2982909374641920457)
XLA Ops:
  0.6 0.8 %pack.1.own_ref = f32[16,128]{1,0:T(8,128)S(1)} custom-call(f32[8,128]{1,0:T(8,128)} %bitcast.18, s32[3,1,128]{2,1,0:T(1,128)} %bitcast.19, s32[1,128]{1,0:T(1,128)} %bitcast.21, s32[2,8]{1,0:T(2,128)} %bitcast.20), custom_call_target="tpu_custom_call" | custom-call | tf_op jit(solution)/shard_map/pack/pallas_call | solution.py:499
  1.4 3.1 %collective-permute-start = (f32[16,128]{1,0:T(8,128)S(1)}, f32[16,128]{1,0:T(8,128)S(1)}, u32[]{:S(2)}, u32[]{:S(2)}) collective-permute-start(f32[16,128]{1,0:T(8,128)S(1)} %pack.1.own_ref), channel_id=1, source_target_pairs={{4,0},{0,4},{12,8},{8,12},{24,16},{28,20},{16,24},{20,28},{5,1},{1... | collective-permute-start | bytes 24584 | tf_op jit(solution)/shard_map/ppermute | solution.py:351
  4.5 2.5 %collective-permute-start.2 = (f32[16,128]{1,0:T(8,128)S(1)}, f32[16,128]{1,0:T(8,128)S(1)}, u32[]{:S(2)}, u32[]{:S(2)}) collective-permute-start(f32[16,128]{1,0:T(8,128)S(1)} %pack.1.own_ref), channel_id=1, source_target_pairs={{12,0},{8,4},{4,8},{0,12},{28,16},{24,20},{20,24},{16,28},{13,1},{... | collective-permute-start | bytes 24584 | tf_op jit(solution)/shard_map/ppermute | solution.py:351
  7.0 0.0 collective-permute-done.mixed_ref
  7.0 0.0 collective-permute-start.1
  7.0 3.0 %collective-permute-done.2.far_ref = f32[16,128]{1,0:T(8,128)S(1)} collective-permute-done((f32[16,128]{1,0:T(8,128)S(1)}, f32[16,128]{1,0:T(8,128)S(1)}, u32[]{:S(2)}, u32[]{:S(2)}) %collective-permute-start.2) | collective-permute-done | bytes 8224 | tf_op jit(solution)/shard_map/ppermute | solution.py:351
  9.9 0.0 collective-permute-done.1.swapped_ref
  9.9 10.7 %velocity.1 = (f32[8,512]{1,0:T(8,128)S(1)}, f32[4,16,128]{2,1,0:T(8,128)S(1)}) custom-call(f32[16,128]{1,0:T(8,128)S(1)} %pack.1.own_ref, f32[16,128]{1,0:T(8,128)S(1)} %collective-permute-done.mixed_ref, f32[16,128]{1,0:T(8,128)S(1)} %collective-permute-done.1.swapped_ref, f32[16,128]{1,0:T(8,128)S(1)} %collective-permute-done.2.far_ref, ...), custom_call_target="tpu_custom_call" | custom-call | tf_op jit(solution)/shard_map/velocity/pallas_call | solution.py:364
  20.6 0.1 collective-permute-start.3
  21.3 0.5 %collective-permute-done.3.other_ref = f32[8,512]{1,0:T(8,128)S(1)} collective-permute-done((f32[8,512]{1,0:T(8,128)S(1)}, f32[8,512]{1,0:T(8,128)S(1)}, u32[]{:S(2)}, u32[]{:S(2)}) %collective-permute-start.3) | collective-permute-done | bytes 16416 | tf_op jit(solution)/shard_map/ppermute | solution.py:343
  21.9 10.5 %decode.1 = (f32[8,256]{1,0:T(8,128)}, bf16[96,1024]{1,0:T(8,128)(2,1)}) custom-call(f32[4,16,128]{2,1,0:T(8,128)S(1)} %get-tuple-element.6.blocks_ref, f32[8,512]{1,0:T(8,128)S(1)} %get-tuple-element.7.mine_ref, f32[8,512]{1,0:T(8,128)S(1)} %collective-permute-done.3.other_ref, f32[1]{0:T(128)S(6)} %copy.17.time_ref, f32[8,768]{1,0:T(8,128)} %proj_hbm.1, ...), custom_call_target="tpu_custom_call" | custom-call | tf_op jit(solution)/shard_map/decode/pallas_call | solution.py:541
Async XLA Ops:
  1.4 5.6 %collective-permute-start = (f32[16,128]{1,0:T(8,128)S(1)}, f32[16,128]{1,0:T(8,128)S(1)}, u32[]{:S(2)}, u32[]{:S(2)}) collective-permute-start(f32[16,128]{1,0:T(8,128)S(1)} %pack.1.own_ref), channel_id=1, source_target_pairs={{4,0},{0,4},{12,8},{8,12},{24,16},{28,20},{16,24},{20,28},{5,1},{1... | collective-permute-start | bytes 24584 | tf_op jit(solution)/shard_map/ppermute | solution.py:351
  4.5 5.4 %collective-permute-start.2 = (f32[16,128]{1,0:T(8,128)S(1)}, f32[16,128]{1,0:T(8,128)S(1)}, u32[]{:S(2)}, u32[]{:S(2)}) collective-permute-start(f32[16,128]{1,0:T(8,128)S(1)} %pack.1.own_ref), channel_id=1, source_target_pairs={{12,0},{8,4},{4,8},{0,12},{28,16},{24,20},{20,24},{16,28},{13,1},{... | collective-permute-start | bytes 24584 | tf_op jit(solution)/shard_map/ppermute | solution.py:351
  7.0 3.0 %collective-permute-start.1 = (f32[16,128]{1,0:T(8,128)S(1)}, f32[16,128]{1,0:T(8,128)S(1)}, u32[]{:S(2)}, u32[]{:S(2)}) collective-permute-start(f32[16,128]{1,0:T(8,128)S(1)} %collective-permute-done.mixed_ref), channel_id=1, source_target_pairs={{0,16},{16,0},{1,17},{17,1},{2,18},{18,2},{3,19},{19,3},{4,20},{20... | collective-permute-start | bytes 24584 | tf_op jit(solution)/shard_map/ppermute | solution.py:343
  20.6 1.2 %collective-permute-start.3 = (f32[8,512]{1,0:T(8,128)S(1)}, f32[8,512]{1,0:T(8,128)S(1)}, u32[]{:S(2)}, u32[]{:S(2)}) collective-permute-start(f32[8,512]{1,0:T(8,128)S(1)} %get-tuple-element.7.mine_ref), channel_id=1, source_target_pairs={{0,16},{16,0},{1,17},{17,1},{2,18},{18,2},{3,19},{19,3},{4,20},{20... | collective-permute-start | bytes 49160 | tf_op jit(solution)/shard_map/ppermute | solution.py:343

commit v3 on v2

--- a/solution.py
+++ b/solution.py
@@ -102,11 +102,49 @@
     pack_ref[ROW_BORDER : ROW_BORDER + 2, 0 : border_ref.shape[1]] = border_ref[...].astype(F32)
 
 
-def velocity_kernel(
+def hidden_rows(rows, table_ref):
+    block = rows.shape[1]
+    values = lax.broadcasted_iota(I32, (RES, block), 0).astype(F32)
+    hots = [
+        (values == rows[ROW_COORD + c : ROW_COORD + c + 1]).astype(F32).astype(BF16)
+        for c in range(3)
+    ]
+    high, low = split_two(rows[0:LAT])
+    tail = jnp.concatenate([high, low, high, jnp.zeros_like(low)], axis=0).astype(BF16)
+    return dot_atb(jnp.concatenate(hots + hots + [tail], axis=0), table_ref[...])
+
+
+def modulated(hidden, mod_ref):
+    center = hidden - jnp.mean(hidden, axis=1, keepdims=True)
+    inverse = lax.rsqrt(jnp.mean(center * center, axis=1, keepdims=True) + EPSILON)
+    return (center * inverse * (1.0 + mod_ref[1]) + mod_ref[0]).astype(BF16)
+
+
+def project(normed, qkv_ref, gain_ref, query_ref, key_ref, value_ref, rows):
+    inner = gain_ref.shape[1]
+    group = 256
+    same_head = (
+        lax.broadcasted_iota(I32, (group, group), 0) // HEAD
+        == lax.broadcasted_iota(I32, (group, group), 1) // HEAD
+    )
+    averager = jnp.where(same_head, 1.0 / HEAD, 0.0).astype(BF16)
+    for j in range(3 * inner // group):
+        projected = dot_ab(normed, qkv_ref[:, j * group : (j + 1) * group])
+        which, col = divmod(j * group, inner)
+        if which == 2:
+            value_ref[col : col + group, rows] = projected.astype(BF16).T
+        else:
+            square = dot_ab((projected * projected).astype(BF16), averager)
+            gains = gain_ref[which : which + 1, col : col + group]
+            if which == 0:
+                gains = gains * (HEAD**-0.5)
+            result = (projected * lax.rsqrt(square + EPSILON) * gains).astype(BF16)
+            (query_ref, key_ref)[which][rows, col : col + group] = result
+
+
+def own_kernel(
     own_ref,
-    mixed_ref,
-    swapped_ref,
-    far_ref,
+    later_ref,
     mod_hbm,
     in_hbm,
     qkv_hbm,
@@ -114,21 +152,17 @@
     out_hbm,
     head_hbm,
     pos_hbm,
-    vel_ref,
-    blocks_ref,
     mod_ref,
-    in_ref,
     qkv_ref,
     gain_ref,
     out_ref,
     head_ref,
     table_ref,
     hidden_ref,
-    normed_ref,
     query_ref,
     key_ref,
     value_ref,
-    att_ref,
+    in_ref,
     sems,
 ):
     pos_rows = pos_hbm.shape[0]
@@ -140,106 +174,110 @@
                 (in_hbm, in_ref),
                 (mod_hbm, mod_ref),
                 (gain_hbm, gain_ref),
+                (qkv_hbm, qkv_ref),
                 (head_hbm, head_ref),
-                (qkv_hbm, qkv_ref),
                 (out_hbm, out_ref),
             )
         )
     ]
     for copy in copies:
         copy.start()
-    me = lax.axis_index("seq")
-    side = lax.axis_index("pair")
-    width = in_ref.shape[1]
-    tokens = hidden_ref.shape[0]
-    inner = out_ref.shape[0]
-    block = own_ref.shape[1]
-
-    blocks_ref[me] = own_ref[...]
-    blocks_ref[me ^ 3] = far_ref[...]
-    blocks_ref[me ^ (1 + side)] = mixed_ref[...]
-    blocks_ref[me ^ (2 - side)] = swapped_ref[...]
-
-    for copy in copies[:5]:
+    for copy in copies[:4]:
         copy.wait()
     in_high, in_low = split_two(in_ref[...])
     table_ref[pos_rows : pos_rows + 32, :] = jnp.concatenate(
         [in_high, in_high, in_low, jnp.zeros_like(in_low)], axis=0
     ).astype(BF16)
-
-    shift = mod_ref[0]
-    scale = 1.0 + mod_ref[1]
-    for s in range(tokens // block):
-        rows = blocks_ref[s]
-        values = lax.broadcasted_iota(I32, (RES, block), 0).astype(F32)
-        hots = [
-            (values == rows[ROW_COORD + c : ROW_COORD + c + 1]).astype(F32).astype(BF16)
-            for c in range(3)
-        ]
-        high, low = split_two(rows[0:LAT])
-        tail = jnp.concatenate([high, low, high, jnp.zeros_like(low)], axis=0).astype(BF16)
-        picks = jnp.concatenate(hots + hots + [tail], axis=0)
-        hidden = dot_atb(picks, table_ref[...])
-        hidden_ref[s * block : (s + 1) * block, :] = hidden
-        center = hidden - jnp.mean(hidden, axis=1, keepdims=True)
-        inverse = lax.rsqrt(jnp.mean(center * center, axis=1, keepdims=True) + EPSILON)
-        normed_ref[s * block : (s + 1) * block, :] = (center * inverse * scale + shift).astype(BF16)
-
+    hidden = hidden_rows(own_ref[...], table_ref)
+    hidden_ref[...] = hidden
+    normed = modulated(hidden, mod_ref)
+    copies[4].wait()
+    block = own_ref.shape[1]
+    project(normed, qkv_ref, gain_ref, query_ref, key_ref, value_ref, slice(0, block))
     copies[5].wait()
     copies[6].wait()
-    group = 256
-    same_head = (
-        lax.broadcasted_iota(I32, (group, group), 0) // HEAD
-        == lax.broadcasted_iota(I32, (group, group), 1) // HEAD
-    )
-    averager = jnp.where(same_head, 1.0 / HEAD, 0.0).astype(BF16)
-    for j in range(3 * inner // group):
-        projected = dot_ab(normed_ref[...], qkv_ref[:, j * group : (j + 1) * group])
-        which, col = divmod(j * group, inner)
-        if which == 2:
-            for half in range(group // 128):
-                pair = (col + half * 128) // 128
-                value_ref[pair, :, 0:128] = projected[:, half * 128 : (half + 1) * 128].astype(BF16)
-                value_ref[pair, :, 128:256] = jnp.ones((tokens, 128), BF16)
-        else:
-            square = dot_ab((projected * projected).astype(BF16), averager)
-            gains = gain_ref[which : which + 1, col : col + group]
-            if which == 0:
-                gains = gains * (HEAD**-0.5)
-            result = (projected * lax.rsqrt(square + EPSILON) * gains).astype(BF16)
-            (query_ref, key_ref)[which][:, col : col + group] = result
+
+
+def velocity_kernel(
+    own_ref,
+    mixed_ref,
+    swapped_ref,
+    far_ref,
+    mod_ref,
+    qkv_ref,
+    gain_ref,
+    out_ref,
+    head_ref,
+    table_ref,
+    own_hidden_ref,
+    own_query_ref,
+    own_key_ref,
+    own_value_ref,
+    vel_ref,
+    blocks_ref,
+    hidden_ref,
+    normed_ref,
+    query_ref,
+    key_ref,
+    value_ref,
+    att_ref,
+):
+    me = lax.axis_index("seq")
+    side = lax.axis_index("pair")
+    width = qkv_ref.shape[0]
+    tokens = hidden_ref.shape[0]
+    inner = out_ref.shape[0]
+    block = own_ref.shape[1]
+    places = (me, me ^ (1 + side), me ^ (2 - side), me ^ 3)
+    sources = (own_ref, mixed_ref, swapped_ref, far_ref)
+    for place, source in zip(places, sources):
+        blocks_ref[place] = source[...]
+
+    hidden_ref[0:block, :] = own_hidden_ref[...]
+    query_ref[0:block, :] = own_query_ref[...]
+    key_ref[0:block, :] = own_key_ref[...]
+    value_ref[:, 0:block] = own_value_ref[...]
+    for s in range(1, len(sources)):
+        hidden = hidden_rows(sources[s][...], table_ref)
+        hidden_ref[s * block : (s + 1) * block, :] = hidden
+        normed_ref[s * block : (s + 1) * block, :] = modulated(hidden, mod_ref)
+    others = slice(block, tokens)
+    project(normed_ref[others, :], qkv_ref, gain_ref, query_ref, key_ref, value_ref, others)
 
     chunk = 256
-    first = lax.broadcasted_iota(I32, (chunk, 128), 1) < HEAD
+    first = lax.broadcasted_iota(I32, (tokens, 128), 1) < HEAD
     for pair in range(inner // 128):
         lanes = slice(pair * 128, (pair + 1) * 128)
-        for q in range(tokens // chunk):
-            here = slice(q * chunk, (q + 1) * chunk)
-            query = query_ref[here, lanes]
-            parts = []
-            for half in range(2):
-                kept = jnp.where(first == (half == 0), query, jnp.zeros_like(query))
-                scores = dot_abt(kept, key_ref[:, lanes])
-                weights = jnp.exp(scores).astype(BF16)
-                sums = dot_ab(weights, value_ref[pair])
-                parts.append(sums[:, 0:128] / sums[:, 128:256])
-            att_ref[here, lanes] = jnp.where(first, parts[0], parts[1]).astype(BF16)
+        for half in range(2):
+            keys = key_ref[:, lanes]
+            keys = jnp.where(first == (half == 0), keys, jnp.zeros_like(keys))
+            dims = slice(pair * 128 + half * HEAD, pair * 128 + (half + 1) * HEAD)
+            values = jnp.concatenate(
+                [value_ref[dims, :], jnp.ones((16, tokens), BF16)], axis=0
+            )
+            for q in range(tokens // chunk):
+                here = slice(q * chunk, (q + 1) * chunk)
+                scores = dot_abt(keys, query_ref[here, lanes])
+                sums = dot_ab(values, jnp.exp(scores).astype(BF16))
+                att_ref[dims, here] = (sums[0:HEAD] / sums[HEAD : HEAD + 1]).astype(BF16)
 
     gate = mod_ref[2]
     head = head_ref[...]
     offset = jnp.sum(head * mod_ref[3], axis=1, keepdims=True)
     head_high, head_low = split_two(head * (1.0 + mod_ref[4]))
     heads = jnp.concatenate([head_high, head_low], axis=0).astype(BF16)
-    for s in range(tokens // block):
+    ones = jnp.ones((16, width), BF16)
+    for s in range(len(sources)):
         here = slice(s * block, (s + 1) * block)
-        hidden = hidden_ref[here, :] + gate * dot_ab(att_ref[here, :], out_ref[...])
+        hidden = hidden_ref[here, :] + gate * dot_atb(att_ref[:, here], out_ref[...])
         center = hidden - jnp.mean(hidden, axis=1, keepdims=True)
-        inverse = lax.rsqrt(jnp.mean(center * center, axis=1, keepdims=True) + EPSILON)
-        final = center * inverse
-        final_high, final_low = split_two(final)
-        both = dot_abt(heads, final_high.astype(BF16))
-        rest = dot_abt(heads, final_low.astype(BF16))
-        vel_ref[:, here] = both[0:LAT] + both[LAT:] + rest[0:LAT] + offset
+        high = center.astype(BF16)
+        low = (center - high.astype(F32)).astype(BF16)
+        both = dot_abt(heads, high)
+        rest = dot_abt(heads, low)
+        square = dot_abt(ones, (center * center).astype(BF16))
+        inverse = lax.rsqrt(square[0:LAT] * (1.0 / width) + EPSILON)
+        vel_ref[places[s]] = (both[0:LAT] + both[LAT:] + rest[0:LAT]) * inverse + offset
 
 
 def decode_kernel(
@@ -247,25 +285,13 @@
     mine_ref,
     other_ref,
     time_ref,
-    proj_hbm,
-    map_hbm,
-    weight_hbm,
-    owned_ref,
-    fine_ref,
     proj_ref,
     map_ref,
     weight_ref,
+    owned_ref,
+    fine_ref,
     product_ref,
-    sems,
 ):
-    copies = [
-        pltpu.make_async_copy(source, target, sems.at[i])
-        for i, (source, target) in enumerate(
-            ((proj_hbm, proj_ref), (weight_hbm, weight_ref), (map_hbm, map_ref))
-        )
-    ]
-    for copy in copies:
-        copy.start()
     me = lax.axis_index("seq")
     is_cond = lax.axis_index("pair") == 0
     count, _, block = blocks_ref.shape
@@ -276,11 +302,14 @@
     table_rows = product_ref.shape[1]
     halo = (table_rows - slots) // 2
 
-    mine, other = mine_ref[...], other_ref[...]
-    cond = jnp.where(is_cond, mine, other)
-    uncond = jnp.where(is_cond, other, mine)
-    latents = jnp.concatenate([blocks_ref[s, 0:LAT, :] for s in range(count)], axis=1)
-    clean = latents - time_ref[0] * (uncond + GUIDANCE * (cond - uncond))
+    cleans = []
+    for s in range(count):
+        mine, other = mine_ref[s], other_ref[s]
+        cond = jnp.where(is_cond, mine, other)
+        uncond = jnp.where(is_cond, other, mine)
+        guided = uncond + GUIDANCE * (cond - uncond)
+        cleans.append(blocks_ref[s, 0:LAT, :] - time_ref[0] * guided)
+    clean = jnp.concatenate(cleans, axis=1)
 
     owners = jnp.concatenate(
         [blocks_ref[s, ROW_OWNER : ROW_OWNER + 1, :] for s in range(count)], axis=0
@@ -312,7 +341,6 @@
     table = spread[0:LAT] + spread[LAT : 2 * LAT] + spread[2 * LAT :]
     owned_ref[...] = table[:, 0:slots]
 
-    copies[0].wait()
     proj_high, proj_low = split_two(proj_ref[...])
     table_high, table_low = split_two(table)
     left = jnp.concatenate([proj_high, proj_high, proj_low, jnp.zeros_like(proj_low)], axis=0)
@@ -320,12 +348,10 @@
     before = dot_atb(left.astype(BF16), right.astype(BF16))
     features = (0.5 * before * (1.0 + jnp.tanh(0.5 * before))).astype(BF16)
 
-    copies[1].wait()
     step = 9 * out_channels
     for k in range(0, offsets * out_channels, step):
         product_ref[k : k + step] = dot_ab(weight_ref[k : k + step], features).astype(BF16)
 
-    copies[2].wait()
     fine = map_ref.shape[2]
     width = 256
     table_ids = lax.broadcasted_iota(I32, (table_rows, width), 0)
@@ -361,37 +387,34 @@
     far = seq_swap(packed, (3, 3))
     swapped = swap_pair(mixed)
     pos = jnp.asarray(position_parts(width))
-    return pl.pallas_call(
-        velocity_kernel,
+    held = pl.pallas_call(
+        own_kernel,
         out_shape=(
-            pltpu.VMEM((LAT, tokens), F32),
-            pltpu.VMEM((count, PACK_ROWS, block), F32),
-        ),
-        in_specs=[VMEM] * 4 + [HBM] * 7,
-        out_specs=(VMEM, VMEM),
-        scratch_shapes=[
             pltpu.VMEM((5, 1, width), F32),
-            pltpu.VMEM(in_proj.shape, F32),
             pltpu.VMEM(qkv_proj.shape, BF16),
             pltpu.VMEM(norm_gain.shape, F32),
             pltpu.VMEM(out_proj.shape, BF16),
             pltpu.VMEM((LAT, width), F32),
             pltpu.VMEM((pos.shape[0] + 32, width), BF16),
-            pltpu.VMEM((tokens, width), F32),
-            pltpu.VMEM((tokens, width), BF16),
-            pltpu.VMEM((tokens, inner), BF16),
-            pltpu.VMEM((tokens, inner), BF16),
-            pltpu.VMEM((inner // 128, tokens, 256), BF16),
-            pltpu.VMEM((tokens, inner), BF16),
+            pltpu.VMEM((block, width), F32),
+            pltpu.VMEM((block, inner), BF16),
+            pltpu.VMEM((block, inner), BF16),
+            pltpu.VMEM((inner, block), BF16),
+        ),
+        in_specs=[VMEM] * 2 + [HBM] * 7,
+        out_specs=(VMEM,) * 10,
+        scratch_shapes=[
+            pltpu.VMEM(in_proj.shape, F32),
             pltpu.SemaphoreType.DMA((7,)),
         ],
         compiler_params=pltpu.CompilerParams(vmem_limit_bytes=VMEM_GRANT),
-        name="velocity",
+        cost_estimate=pl.CostEstimate(
+            flops=2 * block * width * 4 * inner, bytes_accessed=6 << 20, transcendentals=0
+        ),
+        name="own_block",
     )(
         packed,
         mixed,
-        swapped,
-        far,
         *in_hbm(
             modulation[0, 0][:, None, :],
             in_proj,
@@ -402,6 +425,25 @@
             pos,
         ),
     )
+    return pl.pallas_call(
+        velocity_kernel,
+        out_shape=(
+            pltpu.VMEM((count, LAT, block), F32),
+            pltpu.VMEM((count, PACK_ROWS, block), F32),
+        ),
+        in_specs=[VMEM] * 14,
+        out_specs=(VMEM, VMEM),
+        scratch_shapes=[
+            pltpu.VMEM((tokens, width), F32),
+            pltpu.VMEM((tokens, width), BF16),
+            pltpu.VMEM((tokens, inner), BF16),
+            pltpu.VMEM((tokens, inner), BF16),
+            pltpu.VMEM((inner, tokens), BF16),
+            pltpu.VMEM((inner, tokens), BF16),
+        ],
+        compiler_params=pltpu.CompilerParams(vmem_limit_bytes=VMEM_GRANT),
+        name="velocity",
+    )(packed, mixed, swapped, far, *held)
 
 
 def layer_norm(values):
@@ -475,7 +517,7 @@
     hidden = hidden + mod_rows[2] * jnp.dot(attended, out_proj, preferred_element_type=F32)
     final = layer_norm(hidden) * (1.0 + mod_rows[4]) + mod_rows[3]
     velocity = jnp.dot(final, head_proj, precision=TOP_PRECISION).T
-    return lax.all_gather(velocity, "seq", axis=1, tiled=True)
+    return lax.all_gather(velocity, "seq", axis=0)
 
 
 def per_device(
@@ -544,15 +586,9 @@
             jax.ShapeDtypeStruct((LAT, slots), F32),
             jax.ShapeDtypeStruct((out_channels, fine), BF16),
         ),
-        in_specs=[VMEM, VMEM, VMEM, SMEM, HBM, HBM, HBM],
+        in_specs=[VMEM, VMEM, VMEM, SMEM, VMEM, VMEM, VMEM],
         out_specs=(VMEM, VMEM),
-        scratch_shapes=[
-            pltpu.VMEM(decoder_projection.shape, F32),
-            pltpu.VMEM((offsets, 1, fine), I32),
-            pltpu.VMEM((offsets * out_channels, decoder_projection.shape[1]), BF16),
-            pltpu.VMEM((offsets * out_channels, table_rows), BF16),
-            pltpu.SemaphoreType.DMA((3,)),
-        ],
+        scratch_shapes=[pltpu.VMEM((offsets * out_channels, table_rows), BF16)],
         compiler_params=pltpu.CompilerParams(vmem_limit_bytes=VMEM_GRANT),
         name="decode",
     )(
@@ -560,11 +596,9 @@
         velocity,
         partner,
         step_time,
-        *in_hbm(
-            decoder_projection,
-            kernel_map.reshape(offsets, 1, fine),
-            jnp.swapaxes(conv_weight, 1, 2).reshape(offsets * out_channels, -1),
-        ),
+        decoder_projection,
+        kernel_map.reshape(offsets, 1, fine),
+        jnp.swapaxes(conv_weight, 1, 2).reshape(offsets * out_channels, -1),
     )
     return (owned[None, None], decoded.T[None, None])
 

time: 32.6 us -> 31 us (0.951)
  waiting for transfers between devices: 3.5 us -> 0.2 us
  Pallas kernels: 22 us -> 23.1 us
  starting transfers between devices: 5.64 us -> 6.1 us
    pallas_call x1 -> x2, Pallas kernels: 10.7 us -> 14.1 us  [the longest x1 10.4 us: whole_asset_velocity(): pl.pallas_call(velocity_kernel, out_shape=(pltpu.VMEM((count, LAT, block)...]
    ppermute x2, waiting for transfers between devices: 2.97 us -> 0.01 us  [seq_swap(): return lax.ppermute(x, ('pair', 'seq'), routes)]
    pallas_call x1, Pallas kernels: 10.5 us -> 8.28 us  [per_device(): pl.pallas_call(decode_kernel, out_shape=(jax.ShapeDtypeStruct((LAT, slots...]
    ppermute x2, starting transfers between devices: 0.07 us -> 0.53 us  [swap_pair(): return lax.ppermute(x, 'pair', [(0, 1), (1, 0)])]
    ppermute x2, waiting for transfers between devices: 0.53 us -> 0.19 us  [swap_pair(): return lax.ppermute(x, 'pair', [(0, 1), (1, 0)])]
  transfers between devices with their start and end apart: 4 -> 4, of which waited for: 2 -> 1; matrix products, arithmetic and copies ran while one was open for 0% -> 0% of each run, Pallas kernels for 0% -> 12%
where the time goes in v3:
time: 31 us; the launch traced here: 30.8 us
  Pallas kernels  23.1 us (75%)
  starting transfers between devices  6.1 us (20%)
  between operations  1.34 us (4%)
    pallas_call x1, Pallas kernels, whole_asset_velocity(): pl.pallas_call(velocity_kernel, out_shape=(pltpu.VMEM((count, LAT, block)...  10.4 us
    pallas_call x1, Pallas kernels, per_device(): pl.pallas_call(decode_kernel, out_shape=(jax.ShapeDtypeStruct((LAT, slots...  8.28 us
    ppermute x2, starting transfers between devices, seq_swap(): return lax.ppermute(x, ('pair', 'seq'), routes)  5.56 us
    pallas_call x1, Pallas kernels, whole_asset_velocity(): pl.pallas_call(own_kernel, out_shape=(pltpu.VMEM((5, 1, width), F32), plt...  3.64 us
    pallas_call x1, Pallas kernels, per_device(): pl.pallas_call(pack_kernel, out_shape=pltpu.VMEM((PACK_ROWS, block), F32)...  0.77 us
  transfers between devices with their start and end apart: 4, of which 1 were waited for; matrix products, arithmetic and copies ran while one was open for 0% of the time, Pallas kernels for 12%

profile of v3, /device:TPU:0, one launch (start us, length us, event | category | flops | bytes accessed | tf_op | source)
XLA Modules:
  0.0 30.8 jit_solution(18078502730640531977)
XLA Ops:
  0.6 0.8 %pack.1.own_ref = f32[16,128]{1,0:T(8,128)S(1)} custom-call(f32[8,128]{1,0:T(8,128)} %bitcast.18, s32[3,1,128]{2,1,0:T(1,128)} %bitcast.19, s32[1,128]{1,0:T(1,128)} %bitcast.21, s32[2,8]{1,0:T(2,128)} %bitcast.20), custom_call_target="tpu_custom_call" | custom-call | tf_op jit(solution)/shard_map/pack/pallas_call | solution.py:541
  1.4 3.1 %collective-permute-start = (f32[16,128]{1,0:T(8,128)S(1)}, f32[16,128]{1,0:T(8,128)S(1)}, u32[]{:S(2)}, u32[]{:S(2)}) collective-permute-start(f32[16,128]{1,0:T(8,128)S(1)} %pack.1.own_ref), channel_id=1, source_target_pairs={{4,0},{0,4},{12,8},{8,12},{24,16},{28,20},{16,24},{20,28},{5,1},{1... | collective-permute-start | bytes 24584 | tf_op jit(solution)/shard_map/ppermute | solution.py:377
  4.5 2.5 %collective-permute-start.2 = (f32[16,128]{1,0:T(8,128)S(1)}, f32[16,128]{1,0:T(8,128)S(1)}, u32[]{:S(2)}, u32[]{:S(2)}) collective-permute-start(f32[16,128]{1,0:T(8,128)S(1)} %pack.1.own_ref), channel_id=1, source_target_pairs={{12,0},{8,4},{4,8},{0,12},{28,16},{24,20},{20,24},{16,28},{13,1},{... | collective-permute-start | bytes 24584 | tf_op jit(solution)/shard_map/ppermute | solution.py:377
  7.0 0.0 collective-permute-done.later_ref.mixed_ref
  7.0 0.0 collective-permute-start.1
  7.0 3.6 %own_block.1 = (f32[5,1,1024]{2,1,0:T(1,128)S(1)}, bf16[1024,1536]{1,0:T(8,128)(2,1)S(1)}, f32[2,512]{1,0:T(2,128)S(1)}, bf16[512,1024]{1,0:T(8,128)(2,1)S(1)}, ...) custom-call(f32[16,128]{1,0:T(8,128)S(1)} %pack.1.own_ref, ...), custom_call_target="tpu_custom_call" | custom-call | flops 536870912 | bytes 6291456 | tf_op jit(solution)/shard_map/own_block/pallas_call | solution.py:390
  10.6 0.0 copy-start
  10.6 0.0 copy-start.1
  10.7 0.0 copy-start.2
  10.7 0.0 collective-permute-done.2.far_ref
  10.7 0.0 collective-permute-done.1.swapped_ref
  10.7 10.4 %velocity.1 = (f32[4,8,128]{2,1,0:T(8,128)S(1)}, f32[4,16,128]{2,1,0:T(8,128)S(1)}) custom-call(f32[16,128]{1,0:T(8,128)S(1)} %pack.1.own_ref, f32[16,128]{1,0:T(8,128)S(1)} %collective-permute-done.later_ref.mixed_ref, f32[16,128]{1,0:T(8,128)S(1)} %collective-permute-done.1.swapped_ref, f32[16,128]{1,0:T(8,128)S(1)} %collective-permute-done.2.far_ref, ...), custom_call_target="tpu_custom_call" | custom-call | tf_op jit(solution)/shard_map/velocity/pallas_call | solution.py:428
  21.1 0.5 %collective-permute-start.3 = (f32[4,8,128]{2,1,0:T(8,128)S(1)}, f32[4,8,128]{2,1,0:T(8,128)S(1)}, u32[]{:S(2)}, u32[]{:S(2)}) collective-permute-start(f32[4,8,128]{2,1,0:T(8,128)S(1)} %get-tuple-element.27.mine_ref), channel_id=1, source_target_pairs={{0,16},{16,0},{1,17},{17,1},{2,18},{18,2},{3,19},{19,3},{4,20},{20... | collective-permute-start | bytes 49160 | tf_op jit(solution)/shard_map/ppermute | solution.py:369
  22.3 0.2 collective-permute-done.3.other_ref
  22.5 0.0 copy-done
  22.5 0.0 copy-done.1
  22.5 0.0 copy-done.2
  22.5 8.3 %decode.1 = (f32[8,256]{1,0:T(8,128)}, bf16[96,1024]{1,0:T(8,128)(2,1)}) custom-call(f32[4,16,128]{2,1,0:T(8,128)S(1)} %get-tuple-element.26.blocks_ref, f32[4,8,128]{2,1,0:T(8,128)S(1)} %get-tuple-element.27.mine_ref, f32[4,8,128]{2,1,0:T(8,128)S(1)} %collective-permute-done.3.other_ref, f32[1]{0:T(128)S(6)} %copy.17.time_ref, f32[8,768]{1,0:T(8,128)S(1)} %copy-done.2, ...), custom_call_target="tpu_custom_call" | custom-call | tf_op jit(solution)/shard_map/decode/pallas_call | solution.py:583
Async XLA Ops:
  1.4 5.6 %collective-permute-start = (f32[16,128]{1,0:T(8,128)S(1)}, f32[16,128]{1,0:T(8,128)S(1)}, u32[]{:S(2)}, u32[]{:S(2)}) collective-permute-start(f32[16,128]{1,0:T(8,128)S(1)} %pack.1.own_ref), channel_id=1, source_target_pairs={{4,0},{0,4},{12,8},{8,12},{24,16},{28,20},{16,24},{20,28},{5,1},{1... | collective-permute-start | bytes 24584 | tf_op jit(solution)/shard_map/ppermute | solution.py:377
  4.5 6.2 %collective-permute-start.2 = (f32[16,128]{1,0:T(8,128)S(1)}, f32[16,128]{1,0:T(8,128)S(1)}, u32[]{:S(2)}, u32[]{:S(2)}) collective-permute-start(f32[16,128]{1,0:T(8,128)S(1)} %pack.1.own_ref), channel_id=1, source_target_pairs={{12,0},{8,4},{4,8},{0,12},{28,16},{24,20},{20,24},{16,28},{13,1},{... | collective-permute-start | bytes 24584 | tf_op jit(solution)/shard_map/ppermute | solution.py:377
  7.0 3.7 %collective-permute-start.1 = (f32[16,128]{1,0:T(8,128)S(1)}, f32[16,128]{1,0:T(8,128)S(1)}, u32[]{:S(2)}, u32[]{:S(2)}) collective-permute-start(f32[16,128]{1,0:T(8,128)S(1)} %collective-permute-done.later_ref.mixed_ref), channel_id=1, source_target_pairs={{0,16},{16,0},{1,17},{17,1},{2,18},{18,2},{3,19},{19,3},{4,20},{20... | collective-permute-start | bytes 24584 | tf_op jit(solution)/shard_map/ppermute | solution.py:369
  10.6 11.9 %copy-start = (bf16[27,768,96]{1,2,0:T(8,128)(2,1)S(1)}, bf16[27,768,96]{1,2,0:T(8,128)(2,1)}, u32[]{:S(2)}) copy-start(bf16[27,768,96]{1,2,0:T(8,128)(2,1)} %param.28) | copy-start | bytes 11943940
  10.6 11.8 %copy-start.1 = (s32[1,1,27,1024]{3,1,2,0:T(1,128)S(1)}, s32[1,1,27,1024]{3,1,2,0:T(1,128)}, u32[]{:S(2)}) copy-start(s32[1,1,27,1024]{3,1,2,0:T(1,128)} %param.27) | copy-start | bytes 331780
  10.7 11.8 %copy-start.2 = (f32[8,768]{1,0:T(8,128)S(1)}, f32[8,768]{1,0:T(8,128)}, u32[]{:S(2)}) copy-start(f32[8,768]{1,0:T(8,128)} %proj_ref.1) | copy-start | bytes 73732
  21.1 1.4 %collective-permute-start.3 = (f32[4,8,128]{2,1,0:T(8,128)S(1)}, f32[4,8,128]{2,1,0:T(8,128)S(1)}, u32[]{:S(2)}, u32[]{:S(2)}) collective-permute-start(f32[4,8,128]{2,1,0:T(8,128)S(1)} %get-tuple-element.27.mine_ref), channel_id=1, source_target_pairs={{0,16},{16,0},{1,17},{17,1},{2,18},{18,2},{3,19},{19,3},{4,20},{20... | collective-permute-start | bytes 49160 | tf_op jit(solution)/shard_map/ppermute | solution.py:369

commit v4 on v3

--- a/solution.py
+++ b/solution.py
@@ -128,11 +128,13 @@
         == lax.broadcasted_iota(I32, (group, group), 1) // HEAD
     )
     averager = jnp.where(same_head, 1.0 / HEAD, 0.0).astype(BF16)
-    for j in range(3 * inner // group):
-        projected = dot_ab(normed, qkv_ref[:, j * group : (j + 1) * group])
+
+    def finish(j, projected):
         which, col = divmod(j * group, inner)
         if which == 2:
-            value_ref[col : col + group, rows] = projected.astype(BF16).T
+            for half in range(group // 128):
+                lanes = slice(half * 128, (half + 1) * 128)
+                value_ref[col // 128 + half, rows, 0:128] = projected[:, lanes].astype(BF16)
         else:
             square = dot_ab((projected * projected).astype(BF16), averager)
             gains = gain_ref[which : which + 1, col : col + group]
@@ -140,6 +142,14 @@
                 gains = gains * (HEAD**-0.5)
             result = (projected * lax.rsqrt(square + EPSILON) * gains).astype(BF16)
             (query_ref, key_ref)[which][rows, col : col + group] = result
+
+    previous = None
+    for j in range(3 * inner // group):
+        projected = dot_ab(normed, qkv_ref[:, j * group : (j + 1) * group])
+        if previous is not None:
+            finish(*previous)
+        previous = (j, projected)
+    finish(*previous)
 
 
 def own_kernel(
@@ -236,30 +246,38 @@
     hidden_ref[0:block, :] = own_hidden_ref[...]
     query_ref[0:block, :] = own_query_ref[...]
     key_ref[0:block, :] = own_key_ref[...]
-    value_ref[:, 0:block] = own_value_ref[...]
+    for pair in range(inner // 128):
+        value_ref[pair, 0:block, 0:128] = own_value_ref[pair]
+    value_ref[:, :, 128:256] = jnp.ones((inner // 128, tokens, 128), BF16)
+    ready = hidden_rows(sources[1][...], table_ref)
     for s in range(1, len(sources)):
-        hidden = hidden_rows(sources[s][...], table_ref)
+        hidden = ready
+        if s + 1 < len(sources):
+            ready = hidden_rows(sources[s + 1][...], table_ref)
         hidden_ref[s * block : (s + 1) * block, :] = hidden
         normed_ref[s * block : (s + 1) * block, :] = modulated(hidden, mod_ref)
     others = slice(block, tokens)
     project(normed_ref[others, :], qkv_ref, gain_ref, query_ref, key_ref, value_ref, others)
 
     chunk = 256
-    first = lax.broadcasted_iota(I32, (tokens, 128), 1) < HEAD
-    for pair in range(inner // 128):
+    first = lax.broadcasted_iota(I32, (chunk, 128), 1) < HEAD
+    todo = [(pair, q, half) for pair in range(inner // 128) for q in range(tokens // chunk) for half in range(2)]
+    def score(pair, q, half):
         lanes = slice(pair * 128, (pair + 1) * 128)
-        for half in range(2):
-            keys = key_ref[:, lanes]
-            keys = jnp.where(first == (half == 0), keys, jnp.zeros_like(keys))
-            dims = slice(pair * 128 + half * HEAD, pair * 128 + (half + 1) * HEAD)
-            values = jnp.concatenate(
-                [value_ref[dims, :], jnp.ones((16, tokens), BF16)], axis=0
-            )
-            for q in range(tokens // chunk):
-                here = slice(q * chunk, (q + 1) * chunk)
-                scores = dot_abt(keys, query_ref[here, lanes])
-                sums = dot_ab(values, jnp.exp(scores).astype(BF16))
-                att_ref[dims, here] = (sums[0:HEAD] / sums[HEAD : HEAD + 1]).astype(BF16)
+        query = query_ref[q * chunk : (q + 1) * chunk, lanes]
+        kept = jnp.where(first == (half == 0), query, jnp.zeros_like(query))
+        return dot_abt(kept, key_ref[:, lanes])
+    ready = score(*todo[0])
+    parts = []
+    for at, (pair, q, half) in enumerate(todo):
+        scores = ready
+        if at + 1 < len(todo):
+            ready = score(*todo[at + 1])
+        sums = dot_ab(jnp.exp(scores).astype(BF16), value_ref[pair])
+        parts.append(sums[:, 0:128] / sums[:, 128:256])
+        if half == 1:
+            att_ref[q * chunk : (q + 1) * chunk, pair * 128 : (pair + 1) * 128] = jnp.where(first, parts[0], parts[1]).astype(BF16)
+            parts = []
 
     gate = mod_ref[2]
     head = head_ref[...]
@@ -267,17 +285,34 @@
     head_high, head_low = split_two(head * (1.0 + mod_ref[4]))
     heads = jnp.concatenate([head_high, head_low], axis=0).astype(BF16)
     ones = jnp.ones((16, width), BF16)
-    for s in range(len(sources)):
-        here = slice(s * block, (s + 1) * block)
-        hidden = hidden_ref[here, :] + gate * dot_atb(att_ref[:, here], out_ref[...])
+    step = 128
+    def attended(q):
+        return dot_ab(att_ref[q * step : (q + 1) * step, :], out_ref[...])
+    def middle(q, product):
+        hidden = hidden_ref[q * step : (q + 1) * step, :] + gate * product
         center = hidden - jnp.mean(hidden, axis=1, keepdims=True)
         high = center.astype(BF16)
         low = (center - high.astype(F32)).astype(BF16)
+        return high, low
+    def last(q, high, low):
         both = dot_abt(heads, high)
         rest = dot_abt(heads, low)
-        square = dot_abt(ones, (center * center).astype(BF16))
+        square = dot_abt(ones, high * high)
         inverse = lax.rsqrt(square[0:LAT] * (1.0 / width) + EPSILON)
-        vel_ref[places[s]] = (both[0:LAT] + both[LAT:] + rest[0:LAT]) * inverse + offset
+        velocity = (both[0:LAT] + both[LAT:] + rest[0:LAT]) * inverse + offset
+        for i in range(step // block):
+            vel_ref[places[q * (step // block) + i]] = velocity[:, i * block : (i + 1) * block]
+    count = tokens // step
+    product = attended(0)
+    waiting = None
+    for q in range(count):
+        following = attended(q + 1) if q + 1 < count else None
+        centered = middle(q, product)
+        if waiting is not None:
+            last(*waiting)
+        waiting = (q, *centered)
+        product = following
+    last(*waiting)
 
 
 def decode_kernel(
@@ -383,8 +418,8 @@
     tokens = count * block
     width = in_proj.shape[1]
     inner = out_proj.shape[0]
+    far = seq_swap(packed, (3, 3))
     mixed = seq_swap(packed, (1, 2))
-    far = seq_swap(packed, (3, 3))
     swapped = swap_pair(mixed)
     pos = jnp.asarray(position_parts(width))
     held = pl.pallas_call(
@@ -399,7 +434,7 @@
             pltpu.VMEM((block, width), F32),
             pltpu.VMEM((block, inner), BF16),
             pltpu.VMEM((block, inner), BF16),
-            pltpu.VMEM((inner, block), BF16),
+            pltpu.VMEM((inner // 128, block, 128), BF16),
         ),
         in_specs=[VMEM] * 2 + [HBM] * 7,
         out_specs=(VMEM,) * 10,
@@ -438,8 +473,8 @@
             pltpu.VMEM((tokens, width), BF16),
             pltpu.VMEM((tokens, inner), BF16),
             pltpu.VMEM((tokens, inner), BF16),
-            pltpu.VMEM((inner, tokens), BF16),
-            pltpu.VMEM((inner, tokens), BF16),
+            pltpu.VMEM((inner // 128, tokens, 256), BF16),
+            pltpu.VMEM((tokens, inner), BF16),
         ],
         compiler_params=pltpu.CompilerParams(vmem_limit_bytes=VMEM_GRANT),
         name="velocity",

time: 31 us -> 26 us (0.84)
  Pallas kernels: 23.1 us -> 18.2 us
    pallas_call x1, Pallas kernels: 10.4 us -> 6.18 us  [whole_asset_velocity(): pl.pallas_call(velocity_kernel, out_shape=(pltpu.VMEM((count, LAT, block)...]
    pallas_call x1, Pallas kernels: 3.64 us -> 3.14 us  [whole_asset_velocity(): pl.pallas_call(own_kernel, out_shape=(pltpu.VMEM((5, 1, width), F32), plt...]
where the time goes in v4:
time: 26 us; the launch traced here: 25.8 us
  Pallas kernels  18.2 us (70%)
  starting transfers between devices  6.1 us (23%)
  between operations  1.34 us (5%)
    pallas_call x1, Pallas kernels, per_device(): pl.pallas_call(decode_kernel, out_shape=(jax.ShapeDtypeStruct((LAT, slots...  8.09 us
    pallas_call x1, Pallas kernels, whole_asset_velocity(): pl.pallas_call(velocity_kernel, out_shape=(pltpu.VMEM((count, LAT, block)...  6.18 us
    ppermute x2, starting transfers between devices, seq_swap(): return lax.ppermute(x, ('pair', 'seq'), routes)  5.56 us
    pallas_call x1, Pallas kernels, whole_asset_velocity(): pl.pallas_call(own_kernel, out_shape=(pltpu.VMEM((5, 1, width), F32), plt...  3.14 us
    pallas_call x1, Pallas kernels, per_device(): pl.pallas_call(pack_kernel, out_shape=pltpu.VMEM((PACK_ROWS, block), F32)...  0.77 us
    ppermute x2, starting transfers between devices, swap_pair(): return lax.ppermute(x, 'pair', [(0, 1), (1, 0)])  0.54 us
  transfers between devices with their start and end apart: 4, of which 1 were waited for; matrix products, arithmetic and copies ran while one was open for 0% of the time, Pallas kernels for 12%

profile of v4, /device:TPU:0, one launch (start us, length us, event | category | flops | bytes accessed | tf_op | source)
XLA Modules:
  0.0 25.8 jit_solution(6284550991220733025)
XLA Ops:
  0.6 0.8 %pack.1.own_ref = f32[16,128]{1,0:T(8,128)S(1)} custom-call(f32[8,128]{1,0:T(8,128)} %bitcast.18, s32[3,1,128]{2,1,0:T(1,128)} %bitcast.19, s32[1,128]{1,0:T(1,128)} %bitcast.21, s32[2,8]{1,0:T(2,128)} %bitcast.20), custom_call_target="tpu_custom_call" | custom-call | tf_op jit(solution)/shard_map/pack/pallas_call | solution.py:576
  1.4 3.1 %collective-permute-start = (f32[16,128]{1,0:T(8,128)S(1)}, f32[16,128]{1,0:T(8,128)S(1)}, u32[]{:S(2)}, u32[]{:S(2)}) collective-permute-start(f32[16,128]{1,0:T(8,128)S(1)} %pack.1.own_ref), channel_id=1, source_target_pairs={{4,0},{0,4},{12,8},{8,12},{24,16},{28,20},{16,24},{20,28},{5,1},{1... | collective-permute-start | bytes 24584 | tf_op jit(solution)/shard_map/ppermute | solution.py:412
  4.5 2.5 %collective-permute-start.2 = (f32[16,128]{1,0:T(8,128)S(1)}, f32[16,128]{1,0:T(8,128)S(1)}, u32[]{:S(2)}, u32[]{:S(2)}) collective-permute-start(f32[16,128]{1,0:T(8,128)S(1)} %pack.1.own_ref), channel_id=1, source_target_pairs={{12,0},{8,4},{4,8},{0,12},{28,16},{24,20},{20,24},{16,28},{13,1},{... | collective-permute-start | bytes 24584 | tf_op jit(solution)/shard_map/ppermute | solution.py:412
  7.0 0.0 collective-permute-done.later_ref.mixed_ref
  7.0 0.0 collective-permute-start.1
  7.0 3.1 %own_block.1 = (f32[5,1,1024]{2,1,0:T(1,128)S(1)}, bf16[1024,1536]{1,0:T(8,128)(2,1)S(1)}, f32[2,512]{1,0:T(2,128)S(1)}, bf16[512,1024]{1,0:T(8,128)(2,1)S(1)}, ...) custom-call(f32[16,128]{1,0:T(8,128)S(1)} %pack.1.own_ref, ...), custom_call_target="tpu_custom_call" | custom-call | flops 536870912 | bytes 6291456 | tf_op jit(solution)/shard_map/own_block/pallas_call | solution.py:425
  10.1 0.0 copy-start
  10.1 0.0 copy-start.1
  10.1 0.0 copy-start.2
  10.2 0.0 collective-permute-done.2.far_ref
  10.2 0.0 collective-permute-done.1.swapped_ref
  10.2 6.2 %velocity.1 = (f32[4,8,128]{2,1,0:T(8,128)S(1)}, f32[4,16,128]{2,1,0:T(8,128)S(1)}) custom-call(f32[16,128]{1,0:T(8,128)S(1)} %pack.1.own_ref, f32[16,128]{1,0:T(8,128)S(1)} %collective-permute-done.later_ref.mixed_ref, f32[16,128]{1,0:T(8,128)S(1)} %collective-permute-done.1.swapped_ref, f32[16,128]{1,0:T(8,128)S(1)} %collective-permute-done.2.far_ref, ...), custom_call_target="tpu_custom_call" | custom-call | tf_op jit(solution)/shard_map/velocity/pallas_call | solution.py:463
  16.4 0.5 %collective-permute-start.3 = (f32[4,8,128]{2,1,0:T(8,128)S(1)}, f32[4,8,128]{2,1,0:T(8,128)S(1)}, u32[]{:S(2)}, u32[]{:S(2)}) collective-permute-start(f32[4,8,128]{2,1,0:T(8,128)S(1)} %get-tuple-element.27.mine_ref), channel_id=1, source_target_pairs={{0,16},{16,0},{1,17},{17,1},{2,18},{18,2},{3,19},{19,3},{4,20},{20... | collective-permute-start | bytes 49160 | tf_op jit(solution)/shard_map/ppermute | solution.py:404
  17.6 0.2 collective-permute-done.3.other_ref
  17.7 0.0 copy-done
  17.7 0.0 copy-done.1
  17.7 0.0 copy-done.2
  17.7 8.1 %decode.1 = (f32[8,256]{1,0:T(8,128)}, bf16[96,1024]{1,0:T(8,128)(2,1)}) custom-call(f32[4,16,128]{2,1,0:T(8,128)S(1)} %get-tuple-element.26.blocks_ref, f32[4,8,128]{2,1,0:T(8,128)S(1)} %get-tuple-element.27.mine_ref, f32[4,8,128]{2,1,0:T(8,128)S(1)} %collective-permute-done.3.other_ref, f32[1]{0:T(128)S(6)} %copy.17.time_ref, f32[8,768]{1,0:T(8,128)S(1)} %copy-done.2, ...), custom_call_target="tpu_custom_call" | custom-call | tf_op jit(solution)/shard_map/decode/pallas_call | solution.py:618
Async XLA Ops:
  1.4 5.6 %collective-permute-start = (f32[16,128]{1,0:T(8,128)S(1)}, f32[16,128]{1,0:T(8,128)S(1)}, u32[]{:S(2)}, u32[]{:S(2)}) collective-permute-start(f32[16,128]{1,0:T(8,128)S(1)} %pack.1.own_ref), channel_id=1, source_target_pairs={{4,0},{0,4},{12,8},{8,12},{24,16},{28,20},{16,24},{20,28},{5,1},{1... | collective-permute-start | bytes 24584 | tf_op jit(solution)/shard_map/ppermute | solution.py:412
  4.5 5.7 %collective-permute-start.2 = (f32[16,128]{1,0:T(8,128)S(1)}, f32[16,128]{1,0:T(8,128)S(1)}, u32[]{:S(2)}, u32[]{:S(2)}) collective-permute-start(f32[16,128]{1,0:T(8,128)S(1)} %pack.1.own_ref), channel_id=1, source_target_pairs={{12,0},{8,4},{4,8},{0,12},{28,16},{24,20},{20,24},{16,28},{13,1},{... | collective-permute-start | bytes 24584 | tf_op jit(solution)/shard_map/ppermute | solution.py:412
  7.0 3.2 %collective-permute-start.1 = (f32[16,128]{1,0:T(8,128)S(1)}, f32[16,128]{1,0:T(8,128)S(1)}, u32[]{:S(2)}, u32[]{:S(2)}) collective-permute-start(f32[16,128]{1,0:T(8,128)S(1)} %collective-permute-done.later_ref.mixed_ref), channel_id=1, source_target_pairs={{0,16},{16,0},{1,17},{17,1},{2,18},{18,2},{3,19},{19,3},{4,20},{20... | collective-permute-start | bytes 24584 | tf_op jit(solution)/shard_map/ppermute | solution.py:404
  10.1 7.6 %copy-start = (bf16[27,768,96]{1,2,0:T(8,128)(2,1)S(1)}, bf16[27,768,96]{1,2,0:T(8,128)(2,1)}, u32[]{:S(2)}) copy-start(bf16[27,768,96]{1,2,0:T(8,128)(2,1)} %param.28) | copy-start | bytes 11943940
  10.1 7.6 %copy-start.1 = (s32[1,1,27,1024]{3,1,2,0:T(1,128)S(1)}, s32[1,1,27,1024]{3,1,2,0:T(1,128)}, u32[]{:S(2)}) copy-start(s32[1,1,27,1024]{3,1,2,0:T(1,128)} %param.27) | copy-start | bytes 331780
  10.1 7.6 %copy-start.2 = (f32[8,768]{1,0:T(8,128)S(1)}, f32[8,768]{1,0:T(8,128)}, u32[]{:S(2)}) copy-start(f32[8,768]{1,0:T(8,128)} %proj_ref.1) | copy-start | bytes 73732
  16.4 1.4 %collective-permute-start.3 = (f32[4,8,128]{2,1,0:T(8,128)S(1)}, f32[4,8,128]{2,1,0:T(8,128)S(1)}, u32[]{:S(2)}, u32[]{:S(2)}) collective-permute-start(f32[4,8,128]{2,1,0:T(8,128)S(1)} %get-tuple-element.27.mine_ref), channel_id=1, source_target_pairs={{0,16},{16,0},{1,17},{17,1},{2,18},{18,2},{3,19},{19,3},{4,20},{20... | collective-permute-start | bytes 49160 | tf_op jit(solution)/shard_map/ppermute | solution.py:404

commit v5 on v4

--- a/solution.py
+++ b/solution.py
@@ -21,6 +21,9 @@
 F32 = jnp.float32
 BF16 = jnp.bfloat16
 I32 = jnp.int32
+F8 = jnp.float8_e4m3fn
+CODE_TOP = 256.0
+TINY = 1e-30
 
 ROW_COORD = 8
 ROW_OWNER = 11
@@ -325,7 +328,7 @@
     weight_ref,
     owned_ref,
     fine_ref,
-    product_ref,
+    code_ref,
 ):
     me = lax.axis_index("seq")
     is_cond = lax.axis_index("pair") == 0
@@ -334,7 +337,7 @@
     capacity = slots // count
     offsets = map_ref.shape[0]
     out_channels = fine_ref.shape[0]
-    table_rows = product_ref.shape[1]
+    table_rows = code_ref.shape[2]
     halo = (table_rows - slots) // 2
 
     cleans = []
@@ -383,21 +386,69 @@
     before = dot_atb(left.astype(BF16), right.astype(BF16))
     features = (0.5 * before * (1.0 + jnp.tanh(0.5 * before))).astype(BF16)
 
-    step = 9 * out_channels
-    for k in range(0, offsets * out_channels, step):
-        product_ref[k : k + step] = dot_ab(weight_ref[k : k + step], features).astype(BF16)
+    count = 3
+    groups = [range(k, min(k + count, offsets)) for k in range(0, offsets, count)]
+
+    def multiply(group):
+        rows = weight_ref[group[0] * out_channels : (group[-1] + 1) * out_channels]
+        return dot_ab(rows, features)
+
+    def code(group, product):
+        top = jnp.max(jnp.abs(product), axis=0, keepdims=True)
+        top = jnp.maximum(jnp.max(top, axis=1, keepdims=True), TINY)
+        scaled = product * (CODE_TOP / top)
+        high = scaled.astype(F8)
+        low = (scaled - high.astype(F32)).astype(F8)
+        for i, k in enumerate(group):
+            rows = slice(i * out_channels, (i + 1) * out_channels)
+            code_ref[k, 0:out_channels] = high[rows]
+            code_ref[k, out_channels : 2 * out_channels] = low[rows]
+        return top * (1.0 / CODE_TOP)
+
+    units = []
+    ready = multiply(groups[0])
+    for i, group in enumerate(groups):
+        product = ready
+        if i + 1 < len(groups):
+            ready = multiply(groups[i + 1])
+        units.append(code(group, product))
 
     fine = map_ref.shape[2]
     width = 256
-    table_ids = lax.broadcasted_iota(I32, (table_rows, width), 0)
+    table_ids = lax.broadcasted_iota(jnp.int16, (table_rows, width), 0)
+    one = jnp.ones((table_rows, width), F8)
+    zero = jnp.zeros((table_rows, width), F8)
     for f in range(fine // width):
         here = slice(f * width, (f + 1) * width)
         total = jnp.zeros((out_channels, width), F32)
-        for k in range(offsets):
-            chosen = (table_ids == map_ref[k, :, here]).astype(F32).astype(BF16)
-            products = product_ref[k * out_channels : (k + 1) * out_channels]
-            total = total + dot_ab(products, chosen)
+        for group, unit in zip(groups, units):
+            part = jnp.zeros((2 * out_channels, width), F32)
+            for k in group:
+                index = jnp.broadcast_to(map_ref[k, :, here], (16, width)).astype(jnp.int16)
+                index = jnp.broadcast_to(index[None], (table_rows // 16, 16, width))
+                chosen = jnp.where(table_ids == index.reshape(table_rows, width), one, zero)
+                part = part + dot_ab(code_ref[k], chosen)
+            total = total + (part[0:out_channels] + part[out_channels:]) * unit
         fine_ref[:, here] = total.astype(BF16)
+
+
+def decode_call(blocks, velocity, partner, step_time, decoder_projection, index_rows, weights):
+    offsets, _, fine = index_rows.shape
+    out_channels = weights.shape[0] // offsets
+    slots = fine // 4
+    table_rows = 2 * slots
+    return pl.pallas_call(
+        decode_kernel,
+        out_shape=(
+            jax.ShapeDtypeStruct((LAT, slots), F32),
+            jax.ShapeDtypeStruct((out_channels, fine), BF16),
+        ),
+        in_specs=[VMEM, VMEM, VMEM, SMEM, VMEM, VMEM, VMEM],
+        out_specs=(VMEM, VMEM),
+        scratch_shapes=[pltpu.VMEM((offsets, 2 * out_channels, table_rows), F8)],
+        compiler_params=pltpu.CompilerParams(vmem_limit_bytes=VMEM_GRANT),
+        name="decode",
+    )(blocks, velocity, partner, step_time, decoder_projection, index_rows, weights)
 
 
 def swap_pair(x):
@@ -613,20 +664,7 @@
     partner = swap_pair(velocity)
     offsets, _, out_channels = conv_weight.shape
     fine = kernel_map.shape[3]
-    slots = fine // 4
-    table_rows = slots + 2 * border_blocks.shape[3] * BLK
-    owned, decoded = pl.pallas_call(
-        decode_kernel,
-        out_shape=(
-            jax.ShapeDtypeStruct((LAT, slots), F32),
-            jax.ShapeDtypeStruct((out_channels, fine), BF16),
-        ),
-        in_specs=[VMEM, VMEM, VMEM, SMEM, VMEM, VMEM, VMEM],
-        out_specs=(VMEM, VMEM),
-        scratch_shapes=[pltpu.VMEM((offsets * out_channels, table_rows), BF16)],
-        compiler_params=pltpu.CompilerParams(vmem_limit_bytes=VMEM_GRANT),
-        name="decode",
-    )(
+    owned, decoded = decode_call(
         blocks,
         velocity,
         partner,

time: 26 us -> 24.7 us (0.950)
  Pallas kernels: 18.2 us -> 16.8 us
    pallas_call x1, Pallas kernels: 8.09 us -> 6.76 us  [decode_call(): pl.pallas_call(decode_kernel, out_shape=(jax.ShapeDtypeStruct((LAT, slots...]
  transfers between devices with their start and end apart: 4 -> 4, of which waited for: 1 -> 1; matrix products, arithmetic and copies ran while one was open for 0% -> 0% of each run, Pallas kernels for 12% -> 13%
where the time goes in v5:
time: 24.7 us; the launch traced here: 24.5 us
  Pallas kernels  16.8 us (68%)
  starting transfers between devices  6.1 us (25%)
  between operations  1.34 us (5%)
    pallas_call x1, Pallas kernels, decode_call(): pl.pallas_call(decode_kernel, out_shape=(jax.ShapeDtypeStruct((LAT, slots...  6.76 us
    pallas_call x1, Pallas kernels, whole_asset_velocity(): pl.pallas_call(velocity_kernel, out_shape=(pltpu.VMEM((count, LAT, block)...  6.18 us
    ppermute x2, starting transfers between devices, seq_swap(): return lax.ppermute(x, ('pair', 'seq'), routes)  5.56 us
    pallas_call x1, Pallas kernels, whole_asset_velocity(): pl.pallas_call(own_kernel, out_shape=(pltpu.VMEM((5, 1, width), F32), plt...  3.14 us
    pallas_call x1, Pallas kernels, per_device(): pl.pallas_call(pack_kernel, out_shape=pltpu.VMEM((PACK_ROWS, block), F32)...  0.77 us
    ppermute x2, starting transfers between devices, swap_pair(): return lax.ppermute(x, 'pair', [(0, 1), (1, 0)])  0.54 us
  transfers between devices with their start and end apart: 4, of which 1 were waited for; matrix products, arithmetic and copies ran while one was open for 0% of the time, Pallas kernels for 13%

profile of v5, /device:TPU:0, one launch (start us, length us, event | category | flops | bytes accessed | tf_op | source)
XLA Modules:
  0.0 24.5 jit_solution(3537147544387541443)
XLA Ops:
  0.6 0.8 %pack.1.own_ref = f32[16,128]{1,0:T(8,128)S(1)} custom-call(f32[8,128]{1,0:T(8,128)} %bitcast.18, s32[3,1,128]{2,1,0:T(1,128)} %bitcast.19, s32[1,128]{1,0:T(1,128)} %bitcast.21, s32[2,8]{1,0:T(2,128)} %bitcast.20), custom_call_target="tpu_custom_call" | custom-call | tf_op jit(solution)/shard_map/pack/pallas_call | solution.py:627
  1.4 3.1 %collective-permute-start = (f32[16,128]{1,0:T(8,128)S(1)}, f32[16,128]{1,0:T(8,128)S(1)}, u32[]{:S(2)}, u32[]{:S(2)}) collective-permute-start(f32[16,128]{1,0:T(8,128)S(1)} %pack.1.own_ref), channel_id=1, source_target_pairs={{4,0},{0,4},{12,8},{8,12},{24,16},{28,20},{16,24},{20,28},{5,1},{1... | collective-permute-start | bytes 24584 | tf_op jit(solution)/shard_map/ppermute | solution.py:463
  4.5 2.5 %collective-permute-start.2 = (f32[16,128]{1,0:T(8,128)S(1)}, f32[16,128]{1,0:T(8,128)S(1)}, u32[]{:S(2)}, u32[]{:S(2)}) collective-permute-start(f32[16,128]{1,0:T(8,128)S(1)} %pack.1.own_ref), channel_id=1, source_target_pairs={{12,0},{8,4},{4,8},{0,12},{28,16},{24,20},{20,24},{16,28},{13,1},{... | collective-permute-start | bytes 24584 | tf_op jit(solution)/shard_map/ppermute | solution.py:463
  7.0 0.0 collective-permute-done.later_ref.mixed_ref
  7.0 0.0 collective-permute-start.1
  7.0 3.1 %own_block.1 = (f32[5,1,1024]{2,1,0:T(1,128)S(1)}, bf16[1024,1536]{1,0:T(8,128)(2,1)S(1)}, f32[2,512]{1,0:T(2,128)S(1)}, bf16[512,1024]{1,0:T(8,128)(2,1)S(1)}, ...) custom-call(f32[16,128]{1,0:T(8,128)S(1)} %pack.1.own_ref, ...), custom_call_target="tpu_custom_call" | custom-call | flops 536870912 | bytes 6291456 | tf_op jit(solution)/shard_map/own_block/pallas_call | solution.py:476
  10.1 0.0 copy-start
  10.1 0.0 copy-start.1
  10.1 0.0 copy-start.2
  10.2 0.0 collective-permute-done.2.far_ref
  10.2 0.0 collective-permute-done.1.swapped_ref
  10.2 6.2 %velocity.1 = (f32[4,8,128]{2,1,0:T(8,128)S(1)}, f32[4,16,128]{2,1,0:T(8,128)S(1)}) custom-call(f32[16,128]{1,0:T(8,128)S(1)} %pack.1.own_ref, f32[16,128]{1,0:T(8,128)S(1)} %collective-permute-done.later_ref.mixed_ref, f32[16,128]{1,0:T(8,128)S(1)} %collective-permute-done.1.swapped_ref, f32[16,128]{1,0:T(8,128)S(1)} %collective-permute-done.2.far_ref, ...), custom_call_target="tpu_custom_call" | custom-call | tf_op jit(solution)/shard_map/velocity/pallas_call | solution.py:514
  16.4 0.5 %collective-permute-start.3 = (f32[4,8,128]{2,1,0:T(8,128)S(1)}, f32[4,8,128]{2,1,0:T(8,128)S(1)}, u32[]{:S(2)}, u32[]{:S(2)}) collective-permute-start(f32[4,8,128]{2,1,0:T(8,128)S(1)} %get-tuple-element.27.mine_ref), channel_id=1, source_target_pairs={{0,16},{16,0},{1,17},{17,1},{2,18},{18,2},{3,19},{19,3},{4,20},{20... | collective-permute-start | bytes 49160 | tf_op jit(solution)/shard_map/ppermute | solution.py:455
  17.6 0.2 collective-permute-done.3.other_ref
  17.7 0.0 copy-done
  17.7 0.0 copy-done.1
  17.7 0.0 copy-done.2
  17.7 6.8 %decode.1 = (f32[8,256]{1,0:T(8,128)}, bf16[96,1024]{1,0:T(8,128)(2,1)}) custom-call(f32[4,16,128]{2,1,0:T(8,128)S(1)} %get-tuple-element.26.blocks_ref, f32[4,8,128]{2,1,0:T(8,128)S(1)} %get-tuple-element.27.mine_ref, f32[4,8,128]{2,1,0:T(8,128)S(1)} %collective-permute-done.3.other_ref, f32[1]{0:T(128)S(6)} %copy.17.time_ref, f32[8,768]{1,0:T(8,128)S(1)} %copy-done.2, ...), custom_call_target="tpu_custom_call" | custom-call | tf_op jit(solution)/shard_map/decode/pallas_call | solution.py:440
Async XLA Ops:
  1.4 5.6 %collective-permute-start = (f32[16,128]{1,0:T(8,128)S(1)}, f32[16,128]{1,0:T(8,128)S(1)}, u32[]{:S(2)}, u32[]{:S(2)}) collective-permute-start(f32[16,128]{1,0:T(8,128)S(1)} %pack.1.own_ref), channel_id=1, source_target_pairs={{4,0},{0,4},{12,8},{8,12},{24,16},{28,20},{16,24},{20,28},{5,1},{1... | collective-permute-start | bytes 24584 | tf_op jit(solution)/shard_map/ppermute | solution.py:463
  4.5 5.7 %collective-permute-start.2 = (f32[16,128]{1,0:T(8,128)S(1)}, f32[16,128]{1,0:T(8,128)S(1)}, u32[]{:S(2)}, u32[]{:S(2)}) collective-permute-start(f32[16,128]{1,0:T(8,128)S(1)} %pack.1.own_ref), channel_id=1, source_target_pairs={{12,0},{8,4},{4,8},{0,12},{28,16},{24,20},{20,24},{16,28},{13,1},{... | collective-permute-start | bytes 24584 | tf_op jit(solution)/shard_map/ppermute | solution.py:463
  7.0 3.2 %collective-permute-start.1 = (f32[16,128]{1,0:T(8,128)S(1)}, f32[16,128]{1,0:T(8,128)S(1)}, u32[]{:S(2)}, u32[]{:S(2)}) collective-permute-start(f32[16,128]{1,0:T(8,128)S(1)} %collective-permute-done.later_ref.mixed_ref), channel_id=1, source_target_pairs={{0,16},{16,0},{1,17},{17,1},{2,18},{18,2},{3,19},{19,3},{4,20},{20... | collective-permute-start | bytes 24584 | tf_op jit(solution)/shard_map/ppermute | solution.py:455
  10.1 7.6 %copy-start = (bf16[27,768,96]{1,2,0:T(8,128)(2,1)S(1)}, bf16[27,768,96]{1,2,0:T(8,128)(2,1)}, u32[]{:S(2)}) copy-start(bf16[27,768,96]{1,2,0:T(8,128)(2,1)} %param.28) | copy-start | bytes 11943940
  10.1 7.6 %copy-start.1 = (s32[1,1,27,1024]{3,1,2,0:T(1,128)S(1)}, s32[1,1,27,1024]{3,1,2,0:T(1,128)}, u32[]{:S(2)}) copy-start(s32[1,1,27,1024]{3,1,2,0:T(1,128)} %param.27) | copy-start | bytes 331780
  10.1 7.6 %copy-start.2 = (f32[8,768]{1,0:T(8,128)S(1)}, f32[8,768]{1,0:T(8,128)}, u32[]{:S(2)}) copy-start(f32[8,768]{1,0:T(8,128)} %proj_ref.1) | copy-start | bytes 73732
  16.4 1.4 %collective-permute-start.3 = (f32[4,8,128]{2,1,0:T(8,128)S(1)}, f32[4,8,128]{2,1,0:T(8,128)S(1)}, u32[]{:S(2)}, u32[]{:S(2)}) collective-permute-start(f32[4,8,128]{2,1,0:T(8,128)S(1)} %get-tuple-element.27.mine_ref), channel_id=1, source_target_pairs={{0,16},{16,0},{1,17},{17,1},{2,18},{18,2},{3,19},{19,3},{4,20},{20... | collective-permute-start | bytes 49160 | tf_op jit(solution)/shard_map/ppermute | solution.py:455

commit v6 on v5

--- a/solution.py
+++ b/solution.py
@@ -318,36 +318,13 @@
     last(*waiting)
 
 
-def decode_kernel(
-    blocks_ref,
-    mine_ref,
-    other_ref,
-    time_ref,
-    proj_ref,
-    map_ref,
-    weight_ref,
-    owned_ref,
-    fine_ref,
-    code_ref,
-):
+def route_kernel(blocks_ref, picks_ref):
     me = lax.axis_index("seq")
-    is_cond = lax.axis_index("pair") == 0
     count, _, block = blocks_ref.shape
-    slots = owned_ref.shape[1]
+    table_rows = picks_ref.shape[0]
+    slots = table_rows // 2
     capacity = slots // count
-    offsets = map_ref.shape[0]
-    out_channels = fine_ref.shape[0]
-    table_rows = code_ref.shape[2]
     halo = (table_rows - slots) // 2
-
-    cleans = []
-    for s in range(count):
-        mine, other = mine_ref[s], other_ref[s]
-        cond = jnp.where(is_cond, mine, other)
-        uncond = jnp.where(is_cond, other, mine)
-        guided = uncond + GUIDANCE * (cond - uncond)
-        cleans.append(blocks_ref[s, 0:LAT, :] - time_ref[0] * guided)
-    clean = jnp.concatenate(cleans, axis=1)
 
     owners = jnp.concatenate(
         [blocks_ref[s, ROW_OWNER : ROW_OWNER + 1, :] for s in range(count)], axis=0
@@ -364,18 +341,49 @@
         targets.append(jnp.concatenate([slot_of[s : s + 1] for s in range(count)], axis=1))
     tokens = count * block
     rows = lax.broadcasted_iota(I32, (slots, tokens), 0)
-    picks = [(rows == targets[0]).astype(F32).astype(BF16)]
+    picks_ref[0:slots] = (rows == targets[0]).astype(F32).astype(BF16)
     small = lax.broadcasted_iota(I32, (BLK, tokens), 0)
     for step, direction in ((-1, 1), (1, 0)):
         source = jnp.clip(me + step, 0, count - 1)
         border = blocks_ref[source, ROW_BORDER : ROW_BORDER + 2, :].astype(I32)
         target = targets[1 if step < 0 else 2]
+        start = slots + (0 if step < 0 else halo)
         for i in range(halo // BLK):
             wanted = border[direction : direction + 1, i : i + 1] * BLK
-            picks.append((small + wanted == target).astype(F32).astype(BF16))
-    picks = jnp.concatenate(picks, axis=0)
+            here = slice(start + i * BLK, start + (i + 1) * BLK)
+            picks_ref[here] = (small + wanted == target).astype(F32).astype(BF16)
+
+
+def decode_kernel(
+    blocks_ref,
+    picks_ref,
+    mine_ref,
+    other_ref,
+    time_ref,
+    proj_ref,
+    map_ref,
+    weight_ref,
+    owned_ref,
+    fine_ref,
+    code_ref,
+):
+    is_cond = lax.axis_index("pair") == 0
+    slots = owned_ref.shape[1]
+    offsets = map_ref.shape[0]
+    out_channels = fine_ref.shape[0]
+    table_rows = code_ref.shape[2]
+
+    cleans = []
+    for s in range(blocks_ref.shape[0]):
+        mine, other = mine_ref[s], other_ref[s]
+        cond = jnp.where(is_cond, mine, other)
+        uncond = jnp.where(is_cond, other, mine)
+        guided = uncond + GUIDANCE * (cond - uncond)
+        cleans.append(blocks_ref[s, 0:LAT, :] - time_ref[0] * guided)
+    clean = jnp.concatenate(cleans, axis=1)
+
     parts = jnp.concatenate(split_three(clean), axis=0).astype(BF16)
-    spread = dot_abt(parts, picks)
+    spread = dot_abt(parts, picks_ref[...])
     table = spread[0:LAT] + spread[LAT : 2 * LAT] + spread[2 * LAT :]
     owned_ref[...] = table[:, 0:slots]
 
@@ -432,23 +440,38 @@
         fine_ref[:, here] = total.astype(BF16)
 
 
-def decode_call(blocks, velocity, partner, step_time, decoder_projection, index_rows, weights):
+def route_call(blocks, table_rows):
+    count, _, block = blocks.shape
+    return pl.pallas_call(
+        route_kernel,
+        out_shape=pltpu.VMEM((table_rows, count * block), BF16),
+        in_specs=[VMEM],
+        out_specs=VMEM,
+        compiler_params=pltpu.CompilerParams(vmem_limit_bytes=VMEM_GRANT),
+        cost_estimate=pl.CostEstimate(flops=0, bytes_accessed=1 << 20, transcendentals=0),
+        name="route",
+    )(blocks)
+
+
+def decode_call(
+    blocks, picks, velocity, partner, step_time, decoder_projection, index_rows, weights
+):
     offsets, _, fine = index_rows.shape
     out_channels = weights.shape[0] // offsets
     slots = fine // 4
-    table_rows = 2 * slots
+    table_rows = picks.shape[0]
     return pl.pallas_call(
         decode_kernel,
         out_shape=(
             jax.ShapeDtypeStruct((LAT, slots), F32),
             jax.ShapeDtypeStruct((out_channels, fine), BF16),
         ),
-        in_specs=[VMEM, VMEM, VMEM, SMEM, VMEM, VMEM, VMEM],
+        in_specs=[VMEM, VMEM, VMEM, VMEM, SMEM, VMEM, VMEM, VMEM],
         out_specs=(VMEM, VMEM),
         scratch_shapes=[pltpu.VMEM((offsets, 2 * out_channels, table_rows), F8)],
         compiler_params=pltpu.CompilerParams(vmem_limit_bytes=VMEM_GRANT),
         name="decode",
-    )(blocks, velocity, partner, step_time, decoder_projection, index_rows, weights)
+    )(blocks, picks, velocity, partner, step_time, decoder_projection, index_rows, weights)
 
 
 def swap_pair(x):
@@ -662,10 +685,12 @@
             head_proj,
         )
     partner = swap_pair(velocity)
+    picks = route_call(blocks, kernel_map.shape[3] // 2)
     offsets, _, out_channels = conv_weight.shape
     fine = kernel_map.shape[3]
     owned, decoded = decode_call(
         blocks,
+        picks,
         velocity,
         partner,
         step_time,

time: 24.7 us -> 24.7 us (level)
    pallas_call x0 -> x1, Pallas kernels: none -> 0.29 us  [route_call(): pl.pallas_call(route_kernel, out_shape=pltpu.VMEM((table_rows, count * bl...]
  transfers between devices with their start and end apart: 4 -> 4, of which waited for: 1 -> 0; matrix products, arithmetic and copies ran while one was open for 0% -> 0% of each run, Pallas kernels for 13% -> 14%
where the time goes in v6:
time: 24.7 us; the launch traced here: 24.5 us
  Pallas kernels  17 us (69%)
  starting transfers between devices  6.1 us (25%)
  between operations  1.38 us (6%)
    pallas_call x1, Pallas kernels, decode_call(): pl.pallas_call(decode_kernel, out_shape=(jax.ShapeDtypeStruct((LAT, slots...  6.59 us
    pallas_call x1, Pallas kernels, whole_asset_velocity(): pl.pallas_call(velocity_kernel, out_shape=(pltpu.VMEM((count, LAT, block)...  6.18 us
    ppermute x2, starting transfers between devices, seq_swap(): return lax.ppermute(x, ('pair', 'seq'), routes)  5.56 us
    pallas_call x1, Pallas kernels, whole_asset_velocity(): pl.pallas_call(own_kernel, out_shape=(pltpu.VMEM((5, 1, width), F32), plt...  3.14 us
    pallas_call x1, Pallas kernels, per_device(): pl.pallas_call(pack_kernel, out_shape=pltpu.VMEM((PACK_ROWS, block), F32)...  0.77 us
    ppermute x2, starting transfers between devices, swap_pair(): return lax.ppermute(x, 'pair', [(0, 1), (1, 0)])  0.54 us
  transfers between devices with their start and end apart: 4, of which 0 were waited for; matrix products, arithmetic and copies ran while one was open for 0% of the time, Pallas kernels for 14%

profile of v6, /device:TPU:0, one launch (start us, length us, event | category | flops | bytes accessed | tf_op | source)
XLA Modules:
  0.0 24.5 jit_solution(5635663440279331595)
XLA Ops:
  0.6 0.8 %pack.1.own_ref = f32[16,128]{1,0:T(8,128)S(1)} custom-call(f32[8,128]{1,0:T(8,128)} %bitcast.18, s32[3,1,128]{2,1,0:T(1,128)} %bitcast.19, s32[1,128]{1,0:T(1,128)} %bitcast.21, s32[2,8]{1,0:T(2,128)} %bitcast.20), custom_call_target="tpu_custom_call" | custom-call | tf_op jit(solution)/shard_map/pack/pallas_call | solution.py:650
  1.4 3.1 %collective-permute-start = (f32[16,128]{1,0:T(8,128)S(1)}, f32[16,128]{1,0:T(8,128)S(1)}, u32[]{:S(2)}, u32[]{:S(2)}) collective-permute-start(f32[16,128]{1,0:T(8,128)S(1)} %pack.1.own_ref), channel_id=1, source_target_pairs={{4,0},{0,4},{12,8},{8,12},{24,16},{28,20},{16,24},{20,28},{5,1},{1... | collective-permute-start | bytes 24584 | tf_op jit(solution)/shard_map/ppermute | solution.py:486
  4.5 2.5 %collective-permute-start.2 = (f32[16,128]{1,0:T(8,128)S(1)}, f32[16,128]{1,0:T(8,128)S(1)}, u32[]{:S(2)}, u32[]{:S(2)}) collective-permute-start(f32[16,128]{1,0:T(8,128)S(1)} %pack.1.own_ref), channel_id=1, source_target_pairs={{12,0},{8,4},{4,8},{0,12},{28,16},{24,20},{20,24},{16,28},{13,1},{... | collective-permute-start | bytes 24584 | tf_op jit(solution)/shard_map/ppermute | solution.py:486
  7.0 0.0 collective-permute-done.later_ref.mixed_ref
  7.0 0.0 collective-permute-start.1
  7.0 3.1 %own_block.1 = (f32[5,1,1024]{2,1,0:T(1,128)S(1)}, bf16[1024,1536]{1,0:T(8,128)(2,1)S(1)}, f32[2,512]{1,0:T(2,128)S(1)}, bf16[512,1024]{1,0:T(8,128)(2,1)S(1)}, ...) custom-call(f32[16,128]{1,0:T(8,128)S(1)} %pack.1.own_ref, ...), custom_call_target="tpu_custom_call" | custom-call | flops 536870912 | bytes 6291456 | tf_op jit(solution)/shard_map/own_block/pallas_call | solution.py:499
  10.1 0.0 collective-permute-done.2.far_ref
  10.1 0.0 collective-permute-done.1.swapped_ref
  10.1 0.0 copy-start
  10.2 0.0 copy-start.1
  10.2 0.0 copy-start.2
  10.2 6.2 %velocity.1 = (f32[4,8,128]{2,1,0:T(8,128)S(1)}, f32[4,16,128]{2,1,0:T(8,128)S(1)}) custom-call(f32[16,128]{1,0:T(8,128)S(1)} %pack.1.own_ref, f32[16,128]{1,0:T(8,128)S(1)} %collective-permute-done.later_ref.mixed_ref, f32[16,128]{1,0:T(8,128)S(1)} %collective-permute-done.1.swapped_ref, f32[16,128]{1,0:T(8,128)S(1)} %collective-permute-done.2.far_ref, ...), custom_call_target="tpu_custom_call" | custom-call | tf_op jit(solution)/shard_map/velocity/pallas_call | solution.py:537
  16.4 0.5 %collective-permute-start.3 = (f32[4,8,128]{2,1,0:T(8,128)S(1)}, f32[4,8,128]{2,1,0:T(8,128)S(1)}, u32[]{:S(2)}, u32[]{:S(2)}) collective-permute-start(f32[4,8,128]{2,1,0:T(8,128)S(1)} %get-tuple-element.27.mine_ref), channel_id=1, source_target_pairs={{0,16},{16,0},{1,17},{17,1},{2,18},{18,2},{3,19},{19,3},{4,20},{20... | collective-permute-start | bytes 49160 | tf_op jit(solution)/shard_map/ppermute | solution.py:478
  17.6 0.3 %route.1.picks_ref = bf16[512,512]{1,0:T(8,128)(2,1)S(1)} custom-call(f32[4,16,128]{2,1,0:T(8,128)S(1)} %get-tuple-element.26.blocks_ref), custom_call_target="tpu_custom_call" | custom-call | bytes 1048576 | tf_op jit(solution)/shard_map/route/pallas_call | solution.py:445
  17.8 0.0 collective-permute-done.3.other_ref
  17.9 0.0 copy-done
  17.9 0.0 copy-done.1
  17.9 0.0 copy-done.2
  17.9 6.6 %decode.1 = (f32[8,256]{1,0:T(8,128)}, bf16[96,1024]{1,0:T(8,128)(2,1)}) custom-call(f32[4,16,128]{2,1,0:T(8,128)S(1)} %get-tuple-element.26.blocks_ref, bf16[512,512]{1,0:T(8,128)(2,1)S(1)} %route.1.picks_ref, f32[4,8,128]{2,1,0:T(8,128)S(1)} %get-tuple-element.27.mine_ref, f32[4,8,128]{2,1,0:T(8,128)S(1)} %collective-permute-done.3.other_ref, ...), custom_call_target="tpu_custom_call" | custom-call | tf_op jit(solution)/shard_map/decode/pallas_call | solution.py:463
Async XLA Ops:
  1.4 5.6 %collective-permute-start = (f32[16,128]{1,0:T(8,128)S(1)}, f32[16,128]{1,0:T(8,128)S(1)}, u32[]{:S(2)}, u32[]{:S(2)}) collective-permute-start(f32[16,128]{1,0:T(8,128)S(1)} %pack.1.own_ref), channel_id=1, source_target_pairs={{4,0},{0,4},{12,8},{8,12},{24,16},{28,20},{16,24},{20,28},{5,1},{1... | collective-permute-start | bytes 24584 | tf_op jit(solution)/shard_map/ppermute | solution.py:486
  4.5 5.6 %collective-permute-start.2 = (f32[16,128]{1,0:T(8,128)S(1)}, f32[16,128]{1,0:T(8,128)S(1)}, u32[]{:S(2)}, u32[]{:S(2)}) collective-permute-start(f32[16,128]{1,0:T(8,128)S(1)} %pack.1.own_ref), channel_id=1, source_target_pairs={{12,0},{8,4},{4,8},{0,12},{28,16},{24,20},{20,24},{16,28},{13,1},{... | collective-permute-start | bytes 24584 | tf_op jit(solution)/shard_map/ppermute | solution.py:486
  7.0 3.2 %collective-permute-start.1 = (f32[16,128]{1,0:T(8,128)S(1)}, f32[16,128]{1,0:T(8,128)S(1)}, u32[]{:S(2)}, u32[]{:S(2)}) collective-permute-start(f32[16,128]{1,0:T(8,128)S(1)} %collective-permute-done.later_ref.mixed_ref), channel_id=1, source_target_pairs={{0,16},{16,0},{1,17},{17,1},{2,18},{18,2},{3,19},{19,3},{4,20},{20... | collective-permute-start | bytes 24584 | tf_op jit(solution)/shard_map/ppermute | solution.py:478
  10.1 7.7 %copy-start = (bf16[27,768,96]{1,2,0:T(8,128)(2,1)S(1)}, bf16[27,768,96]{1,2,0:T(8,128)(2,1)}, u32[]{:S(2)}) copy-start(bf16[27,768,96]{1,2,0:T(8,128)(2,1)} %param.28) | copy-start | bytes 11943940
  10.2 7.7 %copy-start.1 = (s32[1,1,27,1024]{3,1,2,0:T(1,128)S(1)}, s32[1,1,27,1024]{3,1,2,0:T(1,128)}, u32[]{:S(2)}) copy-start(s32[1,1,27,1024]{3,1,2,0:T(1,128)} %param.27) | copy-start | bytes 331780
  10.2 7.7 %copy-start.2 = (f32[8,768]{1,0:T(8,128)S(1)}, f32[8,768]{1,0:T(8,128)}, u32[]{:S(2)}) copy-start(f32[8,768]{1,0:T(8,128)} %proj_ref.1) | copy-start | bytes 73732
  16.4 1.5 %collective-permute-start.3 = (f32[4,8,128]{2,1,0:T(8,128)S(1)}, f32[4,8,128]{2,1,0:T(8,128)S(1)}, u32[]{:S(2)}, u32[]{:S(2)}) collective-permute-start(f32[4,8,128]{2,1,0:T(8,128)S(1)} %get-tuple-element.27.mine_ref), channel_id=1, source_target_pairs={{0,16},{16,0},{1,17},{17,1},{2,18},{18,2},{3,19},{19,3},{4,20},{20... | collective-permute-start | bytes 49160 | tf_op jit(solution)/shard_map/ppermute | solution.py:478

commit v7 on v6

--- a/solution.py
+++ b/solution.py
@@ -157,7 +157,6 @@
 
 def own_kernel(
     own_ref,
-    later_ref,
     mod_hbm,
     in_hbm,
     qkv_hbm,
@@ -211,11 +210,30 @@
     copies[6].wait()
 
 
+def near_kernel(
+    near_ref,
+    later_ref,
+    mod_ref,
+    qkv_ref,
+    gain_ref,
+    table_ref,
+    hidden_ref,
+    query_ref,
+    key_ref,
+    value_ref,
+):
+    hidden = hidden_rows(near_ref[...], table_ref)
+    hidden_ref[...] = hidden
+    normed = modulated(hidden, mod_ref)
+    rows = slice(0, near_ref.shape[1])
+    project(normed, qkv_ref, gain_ref, query_ref, key_ref, value_ref, rows)
+
+
 def velocity_kernel(
     own_ref,
-    mixed_ref,
+    near_ref,
+    first_ref,
     swapped_ref,
-    far_ref,
     mod_ref,
     qkv_ref,
     gain_ref,
@@ -226,6 +244,10 @@
     own_query_ref,
     own_key_ref,
     own_value_ref,
+    near_hidden_ref,
+    near_query_ref,
+    near_key_ref,
+    near_value_ref,
     vel_ref,
     blocks_ref,
     hidden_ref,
@@ -241,34 +263,40 @@
     tokens = hidden_ref.shape[0]
     inner = out_ref.shape[0]
     block = own_ref.shape[1]
-    places = (me, me ^ (1 + side), me ^ (2 - side), me ^ 3)
-    sources = (own_ref, mixed_ref, swapped_ref, far_ref)
+    places = (me, me ^ 1, me ^ (3 - side), me ^ (2 + side))
+    sources = (own_ref, near_ref, first_ref, swapped_ref)
     for place, source in zip(places, sources):
         blocks_ref[place] = source[...]
 
-    hidden_ref[0:block, :] = own_hidden_ref[...]
-    query_ref[0:block, :] = own_query_ref[...]
-    key_ref[0:block, :] = own_key_ref[...]
-    for pair in range(inner // 128):
-        value_ref[pair, 0:block, 0:128] = own_value_ref[pair]
     value_ref[:, :, 128:256] = jnp.ones((inner // 128, tokens, 128), BF16)
-    ready = hidden_rows(sources[1][...], table_ref)
-    for s in range(1, len(sources)):
+    ready = hidden_rows(first_ref[...], table_ref)
+    done = (
+        (own_hidden_ref, own_query_ref, own_key_ref, own_value_ref),
+        (near_hidden_ref, near_query_ref, near_key_ref, near_value_ref),
+    )
+    for s, (hidden, query, key, value) in enumerate(done):
+        here = slice(s * block, (s + 1) * block)
+        hidden_ref[here, :] = hidden[...]
+        query_ref[here, :] = query[...]
+        key_ref[here, :] = key[...]
+        for pair in range(inner // 128):
+            value_ref[pair, here, 0:128] = value[pair]
+    for s in range(len(done), len(sources)):
         hidden = ready
         if s + 1 < len(sources):
             ready = hidden_rows(sources[s + 1][...], table_ref)
         hidden_ref[s * block : (s + 1) * block, :] = hidden
         normed_ref[s * block : (s + 1) * block, :] = modulated(hidden, mod_ref)
-    others = slice(block, tokens)
+    others = slice(len(done) * block, tokens)
     project(normed_ref[others, :], qkv_ref, gain_ref, query_ref, key_ref, value_ref, others)
 
     chunk = 256
-    first = lax.broadcasted_iota(I32, (chunk, 128), 1) < HEAD
+    even = lax.broadcasted_iota(I32, (chunk, 128), 1) < HEAD
     todo = [(pair, q, half) for pair in range(inner // 128) for q in range(tokens // chunk) for half in range(2)]
     def score(pair, q, half):
         lanes = slice(pair * 128, (pair + 1) * 128)
         query = query_ref[q * chunk : (q + 1) * chunk, lanes]
-        kept = jnp.where(first == (half == 0), query, jnp.zeros_like(query))
+        kept = jnp.where(even == (half == 0), query, jnp.zeros_like(query))
         return dot_abt(kept, key_ref[:, lanes])
     ready = score(*todo[0])
     parts = []
@@ -279,7 +307,7 @@
         sums = dot_ab(jnp.exp(scores).astype(BF16), value_ref[pair])
         parts.append(sums[:, 0:128] / sums[:, 128:256])
         if half == 1:
-            att_ref[q * chunk : (q + 1) * chunk, pair * 128 : (pair + 1) * 128] = jnp.where(first, parts[0], parts[1]).astype(BF16)
+            att_ref[q * chunk : (q + 1) * chunk, pair * 128 : (pair + 1) * 128] = jnp.where(even, parts[0], parts[1]).astype(BF16)
             parts = []
 
     gate = mod_ref[2]
@@ -492,9 +520,18 @@
     tokens = count * block
     width = in_proj.shape[1]
     inner = out_proj.shape[0]
-    far = seq_swap(packed, (3, 3))
-    mixed = seq_swap(packed, (1, 2))
-    swapped = swap_pair(mixed)
+    first = seq_swap(packed, (3, 2))
+    near = seq_swap(packed, (1, 1))
+    swapped = swap_pair(first)
+    block_shapes = (
+        pltpu.VMEM((block, width), F32),
+        pltpu.VMEM((block, inner), BF16),
+        pltpu.VMEM((block, inner), BF16),
+        pltpu.VMEM((inner // 128, block, 128), BF16),
+    )
+    block_cost = pl.CostEstimate(
+        flops=2 * block * width * 4 * inner, bytes_accessed=6 << 20, transcendentals=0
+    )
     pos = jnp.asarray(position_parts(width))
     held = pl.pallas_call(
         own_kernel,
@@ -505,25 +542,19 @@
             pltpu.VMEM(out_proj.shape, BF16),
             pltpu.VMEM((LAT, width), F32),
             pltpu.VMEM((pos.shape[0] + 32, width), BF16),
-            pltpu.VMEM((block, width), F32),
-            pltpu.VMEM((block, inner), BF16),
-            pltpu.VMEM((block, inner), BF16),
-            pltpu.VMEM((inner // 128, block, 128), BF16),
+            *block_shapes,
         ),
-        in_specs=[VMEM] * 2 + [HBM] * 7,
+        in_specs=[VMEM] + [HBM] * 7,
         out_specs=(VMEM,) * 10,
         scratch_shapes=[
             pltpu.VMEM(in_proj.shape, F32),
             pltpu.SemaphoreType.DMA((7,)),
         ],
         compiler_params=pltpu.CompilerParams(vmem_limit_bytes=VMEM_GRANT),
-        cost_estimate=pl.CostEstimate(
-            flops=2 * block * width * 4 * inner, bytes_accessed=6 << 20, transcendentals=0
-        ),
+        cost_estimate=block_cost,
         name="own_block",
     )(
         packed,
-        mixed,
         *in_hbm(
             modulation[0, 0][:, None, :],
             in_proj,
@@ -534,13 +565,24 @@
             pos,
         ),
     )
+    weights, own_state = held[:6], held[6:]
+    mod_rows, qkv_rows, gains, _, _, table = weights
+    near_state = pl.pallas_call(
+        near_kernel,
+        out_shape=block_shapes,
+        in_specs=[VMEM] * 6,
+        out_specs=(VMEM,) * 4,
+        compiler_params=pltpu.CompilerParams(vmem_limit_bytes=VMEM_GRANT),
+        cost_estimate=block_cost,
+        name="near_block",
+    )(near, first, mod_rows, qkv_rows, gains, table)
     return pl.pallas_call(
         velocity_kernel,
         out_shape=(
             pltpu.VMEM((count, LAT, block), F32),
             pltpu.VMEM((count, PACK_ROWS, block), F32),
         ),
-        in_specs=[VMEM] * 14,
+        in_specs=[VMEM] * 18,
         out_specs=(VMEM, VMEM),
         scratch_shapes=[
             pltpu.VMEM((tokens, width), F32),
@@ -552,7 +594,7 @@
         ],
         compiler_params=pltpu.CompilerParams(vmem_limit_bytes=VMEM_GRANT),
         name="velocity",
-    )(packed, mixed, swapped, far, *held)
+    )(packed, near, first, swapped, *weights, *own_state, *near_state)
 
 
 def layer_norm(values):

time: 24.7 us -> 25.2 us (1.020)
  starting transfers between devices: 6.1 us -> 5.29 us
  Pallas kernels: 17 us -> 17.7 us
  waiting for transfers between devices: 0.01 us -> 0.6 us
    pallas_call x0 -> x1, Pallas kernels: none -> 1.34 us  [whole_asset_velocity(): pl.pallas_call(near_kernel, out_shape=block_shapes, in_specs=[VMEM] * 6,...]
    pallas_call x1, Pallas kernels: 6.18 us -> 5.63 us  [whole_asset_velocity(): pl.pallas_call(velocity_kernel, out_shape=(pltpu.VMEM((count, LAT, block)...]
    ppermute x2, starting transfers between devices: 5.56 us -> 5.12 us  [seq_swap(): return lax.ppermute(x, ('pair', 'seq'), routes)]
    ppermute x2, waiting for transfers between devices: 0.01 us -> 0.43 us  [seq_swap(): return lax.ppermute(x, ('pair', 'seq'), routes)]
    ppermute x2, starting transfers between devices: 0.54 us -> 0.17 us  [swap_pair(): return lax.ppermute(x, 'pair', [(0, 1), (1, 0)])]
  transfers between devices with their start and end apart: 4 -> 4, of which waited for: 0 -> 2; matrix products, arithmetic and copies ran while one was open for 0% -> 0% of each run, Pallas kernels for 14% -> 19%
where the time goes in v7:
time: 25.2 us; the launch traced here: 25 us
  Pallas kernels  17.7 us (70%)
  starting transfers between devices  5.29 us (21%)
  between operations  1.37 us (5%)
  waiting for transfers between devices  0.6 us (2%)
    pallas_call x1, Pallas kernels, decode_call(): pl.pallas_call(decode_kernel, out_shape=(jax.ShapeDtypeStruct((LAT, slots...  6.58 us
    pallas_call x1, Pallas kernels, whole_asset_velocity(): pl.pallas_call(velocity_kernel, out_shape=(pltpu.VMEM((count, LAT, block)...  5.63 us
    ppermute x2, starting transfers between devices, seq_swap(): return lax.ppermute(x, ('pair', 'seq'), routes)  5.12 us
    pallas_call x1, Pallas kernels, whole_asset_velocity(): pl.pallas_call(own_kernel, out_shape=(pltpu.VMEM((5, 1, width), F32), plt...  3.12 us
    pallas_call x1, Pallas kernels, whole_asset_velocity(): pl.pallas_call(near_kernel, out_shape=block_shapes, in_specs=[VMEM] * 6,...  1.34 us
    pallas_call x1, Pallas kernels, per_device(): pl.pallas_call(pack_kernel, out_shape=pltpu.VMEM((PACK_ROWS, block), F32)...  0.77 us
  transfers between devices with their start and end apart: 4, of which 2 were waited for; matrix products, arithmetic and copies ran while one was open for 0% of the time, Pallas kernels for 19%

profile of v7, /device:TPU:0, one launch (start us, length us, event | category | flops | bytes accessed | tf_op | source)
XLA Modules:
  0.0 25.0 jit_solution(4525904889429360613)
XLA Ops:
  0.6 0.8 %pack.1.own_ref = f32[16,128]{1,0:T(8,128)S(1)} custom-call(f32[8,128]{1,0:T(8,128)} %bitcast.18, s32[3,1,128]{2,1,0:T(1,128)} %bitcast.19, s32[1,128]{1,0:T(1,128)} %bitcast.21, s32[2,8]{1,0:T(2,128)} %bitcast.20), custom_call_target="tpu_custom_call" | custom-call | tf_op jit(solution)/shard_map/pack/pallas_call | solution.py:692
  1.4 5.1 %collective-permute-start.1 = (f32[16,128]{1,0:T(8,128)S(1)}, f32[16,128]{1,0:T(8,128)S(1)}, u32[]{:S(2)}, u32[]{:S(2)}) collective-permute-start(f32[16,128]{1,0:T(8,128)S(1)} %pack.1.own_ref), channel_id=1, source_target_pairs={{12,0},{8,4},{4,8},{0,12},{24,16},{28,20},{16,24},{20,28},{13,1},{... | collective-permute-start | bytes 24584 | tf_op jit(solution)/shard_map/ppermute | solution.py:514
  6.5 0.0 collective-permute-start
  6.5 3.1 %own_block.1 = (f32[5,1,1024]{2,1,0:T(1,128)S(1)}, bf16[1024,1536]{1,0:T(8,128)(2,1)S(1)}, f32[2,512]{1,0:T(2,128)S(1)}, bf16[512,1024]{1,0:T(8,128)(2,1)S(1)}, ...) custom-call(f32[16,128]{1,0:T(8,128)S(1)} %pack.1.own_ref, ...), custom_call_target="tpu_custom_call" | custom-call | flops 536870912 | bytes 6291456 | tf_op jit(solution)/shard_map/own_block/pallas_call | solution.py:536
  9.7 0.0 collective-permute-done.1.later_ref.first_ref
  9.7 0.1 collective-permute-start.2
  9.7 0.4 %collective-permute-done.near_ref = f32[16,128]{1,0:T(8,128)S(1)} collective-permute-done((f32[16,128]{1,0:T(8,128)S(1)}, f32[16,128]{1,0:T(8,128)S(1)}, u32[]{:S(2)}, u32[]{:S(2)}) %collective-permute-start) | collective-permute-done | bytes 8224 | tf_op jit(solution)/shard_map/ppermute | solution.py:514
  10.2 1.3 %near_block.1 = (f32[128,1024]{1,0:T(8,128)S(1)}, bf16[128,512]{1,0:T(8,128)(2,1)S(1)}, bf16[128,512]{1,0:T(8,128)(2,1)S(1)}, bf16[4,128,128]{2,1,0:T(8,128)(2,1)S(1)}) custom-call(f32[16,128]{1,0:T(8,128)S(1)} %collective-permute-done.near_ref, f32[16,128]{1,0:T(8,128)S(1)} %collective-permute-done.1.later_ref.first_ref, ...), custom_call_target="tpu_custom_call" | custom-call | flops 536870912 | bytes 6291456 | tf_op jit(solution)/shard_map/near_block/pallas_call | solution.py:570
  11.5 0.0 collective-permute-done.2.swapped_ref
  11.5 0.0 copy-start
  11.5 0.0 copy-start.1
  11.6 0.0 copy-start.2
  11.6 5.6 %velocity.1 = (f32[4,8,128]{2,1,0:T(8,128)S(1)}, f32[4,16,128]{2,1,0:T(8,128)S(1)}) custom-call(f32[16,128]{1,0:T(8,128)S(1)} %pack.1.own_ref, f32[16,128]{1,0:T(8,128)S(1)} %collective-permute-done.near_ref, f32[16,128]{1,0:T(8,128)S(1)} %collective-permute-done.1.later_ref.first_ref, f32[16,128]{1,0:T(8,128)S(1)} %collective-permute-done.2.swapped_ref, ...), custom_call_target="tpu_custom_call" | custom-call | tf_op jit(solution)/shard_map/velocity/pallas_call | solution.py:579
  17.2 0.1 collective-permute-start.3
  17.9 0.3 %route.1.picks_ref = bf16[512,512]{1,0:T(8,128)(2,1)S(1)} custom-call(f32[4,16,128]{2,1,0:T(8,128)S(1)} %get-tuple-element.34.blocks_ref), custom_call_target="tpu_custom_call" | custom-call | bytes 1048576 | tf_op jit(solution)/shard_map/route/pallas_call | solution.py:473
  18.2 0.2 collective-permute-done.3.other_ref
  18.4 0.0 copy-done
  18.4 0.0 copy-done.1
  18.4 0.0 copy-done.2
  18.4 6.6 %decode.1 = (f32[8,256]{1,0:T(8,128)}, bf16[96,1024]{1,0:T(8,128)(2,1)}) custom-call(f32[4,16,128]{2,1,0:T(8,128)S(1)} %get-tuple-element.34.blocks_ref, bf16[512,512]{1,0:T(8,128)(2,1)S(1)} %route.1.picks_ref, f32[4,8,128]{2,1,0:T(8,128)S(1)} %get-tuple-element.35.mine_ref, f32[4,8,128]{2,1,0:T(8,128)S(1)} %collective-permute-done.3.other_ref, ...), custom_call_target="tpu_custom_call" | custom-call | tf_op jit(solution)/shard_map/decode/pallas_call | solution.py:491
Async XLA Ops:
  1.4 8.2 %collective-permute-start.1 = (f32[16,128]{1,0:T(8,128)S(1)}, f32[16,128]{1,0:T(8,128)S(1)}, u32[]{:S(2)}, u32[]{:S(2)}) collective-permute-start(f32[16,128]{1,0:T(8,128)S(1)} %pack.1.own_ref), channel_id=1, source_target_pairs={{12,0},{8,4},{4,8},{0,12},{24,16},{28,20},{16,24},{20,28},{13,1},{... | collective-permute-start | bytes 24584 | tf_op jit(solution)/shard_map/ppermute | solution.py:514
  6.5 3.7 %collective-permute-start = (f32[16,128]{1,0:T(8,128)S(1)}, f32[16,128]{1,0:T(8,128)S(1)}, u32[]{:S(2)}, u32[]{:S(2)}) collective-permute-start(f32[16,128]{1,0:T(8,128)S(1)} %pack.1.own_ref), channel_id=1, source_target_pairs={{4,0},{0,4},{12,8},{8,12},{20,16},{16,20},{28,24},{24,28},{5,1},{1... | collective-permute-start | bytes 24584 | tf_op jit(solution)/shard_map/ppermute | solution.py:514
  9.7 1.9 %collective-permute-start.2 = (f32[16,128]{1,0:T(8,128)S(1)}, f32[16,128]{1,0:T(8,128)S(1)}, u32[]{:S(2)}, u32[]{:S(2)}) collective-permute-start(f32[16,128]{1,0:T(8,128)S(1)} %collective-permute-done.1.later_ref.first_ref), channel_id=1, source_target_pairs={{0,16},{16,0},{1,17},{17,1},{2,18},{18,2},{3,19},{19,3},{4,20},{20... | collective-permute-start | bytes 24584 | tf_op jit(solution)/shard_map/ppermute | solution.py:506
  11.5 6.9 %copy-start = (bf16[27,768,96]{1,2,0:T(8,128)(2,1)S(1)}, bf16[27,768,96]{1,2,0:T(8,128)(2,1)}, u32[]{:S(2)}) copy-start(bf16[27,768,96]{1,2,0:T(8,128)(2,1)} %param.28) | copy-start | bytes 11943940
  11.5 6.9 %copy-start.1 = (s32[1,1,27,1024]{3,1,2,0:T(1,128)S(1)}, s32[1,1,27,1024]{3,1,2,0:T(1,128)}, u32[]{:S(2)}) copy-start(s32[1,1,27,1024]{3,1,2,0:T(1,128)} %param.27) | copy-start | bytes 331780
  11.6 6.9 %copy-start.2 = (f32[8,768]{1,0:T(8,128)S(1)}, f32[8,768]{1,0:T(8,128)}, u32[]{:S(2)}) copy-start(f32[8,768]{1,0:T(8,128)} %proj_ref.1) | copy-start | bytes 73732
  17.2 1.2 %collective-permute-start.3 = (f32[4,8,128]{2,1,0:T(8,128)S(1)}, f32[4,8,128]{2,1,0:T(8,128)S(1)}, u32[]{:S(2)}, u32[]{:S(2)}) collective-permute-start(f32[4,8,128]{2,1,0:T(8,128)S(1)} %get-tuple-element.35.mine_ref), channel_id=1, source_target_pairs={{0,16},{16,0},{1,17},{17,1},{2,18},{18,2},{3,19},{19,3},{4,20},{20... | collective-permute-start | bytes 49160 | tf_op jit(solution)/shard_map/ppermute | solution.py:506

commit v8 on v7

--- a/solution.py
+++ b/solution.py
@@ -155,59 +155,78 @@
     finish(*previous)
 
 
-def own_kernel(
-    own_ref,
-    mod_hbm,
-    in_hbm,
-    qkv_hbm,
-    gain_hbm,
-    out_hbm,
-    head_hbm,
-    pos_hbm,
-    mod_ref,
-    qkv_ref,
-    gain_ref,
-    out_ref,
-    head_ref,
-    table_ref,
-    hidden_ref,
-    query_ref,
-    key_ref,
-    value_ref,
-    in_ref,
-    sems,
-):
-    pos_rows = pos_hbm.shape[0]
-    copies = [
+def first_half():
+    return lax.axis_index("seq") < lax.axis_size("seq") // 2
+
+
+def weight_copies(sources, targets, sems):
+    mod_hbm, in_hbm_ref, qkv_hbm, gain_hbm, out_hbm, head_hbm, pos_hbm = sources
+    mod_ref, in_ref, qkv_ref, gain_ref, out_ref, head_ref, table_ref = targets
+    pairs = (
+        (pos_hbm, table_ref.at[0 : pos_hbm.shape[0]]),
+        (in_hbm_ref, in_ref),
+        (mod_hbm, mod_ref),
+        (gain_hbm, gain_ref),
+        (qkv_hbm, qkv_ref),
+        (head_hbm, head_ref),
+        (out_hbm, out_ref),
+    )
+    return [
         pltpu.make_async_copy(source, target, sems.at[i])
-        for i, (source, target) in enumerate(
-            (
-                (pos_hbm, table_ref.at[0:pos_rows]),
-                (in_hbm, in_ref),
-                (mod_hbm, mod_ref),
-                (gain_hbm, gain_ref),
-                (qkv_hbm, qkv_ref),
-                (head_hbm, head_ref),
-                (out_hbm, out_ref),
-            )
-        )
+        for i, (source, target) in enumerate(pairs)
     ]
-    for copy in copies:
-        copy.start()
+
+
+def own_work(pack_ref, in_ref, copies, outs):
+    mod_ref, qkv_ref, gain_ref, _, _, table_ref, hidden_ref, query_ref, key_ref, value_ref = outs
     for copy in copies[:4]:
         copy.wait()
     in_high, in_low = split_two(in_ref[...])
+    pos_rows = table_ref.shape[0] - 32
     table_ref[pos_rows : pos_rows + 32, :] = jnp.concatenate(
         [in_high, in_high, in_low, jnp.zeros_like(in_low)], axis=0
     ).astype(BF16)
-    hidden = hidden_rows(own_ref[...], table_ref)
+    hidden = hidden_rows(pack_ref[...], table_ref)
     hidden_ref[...] = hidden
     normed = modulated(hidden, mod_ref)
     copies[4].wait()
-    block = own_ref.shape[1]
-    project(normed, qkv_ref, gain_ref, query_ref, key_ref, value_ref, slice(0, block))
+    rows = slice(0, pack_ref.shape[1])
+    project(normed, qkv_ref, gain_ref, query_ref, key_ref, value_ref, rows)
     copies[5].wait()
     copies[6].wait()
+
+
+def copy_targets(in_ref, outs):
+    mod_ref, qkv_ref, gain_ref, out_ref, head_ref, table_ref = outs[:6]
+    return mod_ref, in_ref, qkv_ref, gain_ref, out_ref, head_ref, table_ref
+
+
+def early_kernel(*refs):
+    inputs, sources, pack_ref, outs = refs[:4], refs[4:11], refs[11], refs[12:22]
+    coord_ref, owner_ref, border_ref, in_ref, pack_sems, sems = refs[22:]
+    copies = weight_copies(sources, copy_targets(in_ref, outs), sems)
+
+    @pl.when(first_half())
+    def _():
+        for copy in copies:
+            copy.start()
+
+    pack_kernel(*inputs, pack_ref, coord_ref, owner_ref, border_ref, pack_sems)
+
+    @pl.when(first_half())
+    def _():
+        own_work(pack_ref, in_ref, copies, outs)
+
+
+def late_kernel(*refs):
+    pack_ref, sources, outs, (in_ref, sems) = refs[0], refs[1:8], refs[18:28], refs[28:]
+
+    @pl.when(jnp.logical_not(first_half()))
+    def _():
+        copies = weight_copies(sources, copy_targets(in_ref, outs), sems)
+        for copy in copies:
+            copy.start()
+        own_work(pack_ref, in_ref, copies, outs)
 
 
 def near_kernel(
@@ -514,57 +533,91 @@
     return lax.ppermute(x, ("pair", "seq"), routes)
 
 
-def whole_asset_velocity(packed, modulation, in_proj, qkv_proj, norm_gain, out_proj, head_proj):
+def pack_operands(latents, voxel_coords, owner_map, border_blocks):
+    return in_hbm(
+        latents[0],
+        jnp.swapaxes(voxel_coords, 0, 1),
+        owner_map.reshape(1, -1),
+        border_blocks[0, 0],
+    )
+
+
+def pack_scratch(block, border_blocks):
+    return [
+        pltpu.VMEM((3, 1, block), I32),
+        pltpu.VMEM((1, block), I32),
+        pltpu.VMEM(border_blocks.shape[2:], I32),
+    ]
+
+
+def whole_asset_velocity(
+    placed, modulation, in_proj, qkv_proj, norm_gain, out_proj, head_proj
+):
+    latents, _, _, border_blocks = placed
     count = lax.axis_size("seq")
-    block = packed.shape[1]
+    block = latents.shape[2]
     tokens = count * block
     width = in_proj.shape[1]
     inner = out_proj.shape[0]
-    first = seq_swap(packed, (3, 2))
-    near = seq_swap(packed, (1, 1))
-    swapped = swap_pair(first)
+    pos = jnp.asarray(position_parts(width))
     block_shapes = (
         pltpu.VMEM((block, width), F32),
         pltpu.VMEM((block, inner), BF16),
         pltpu.VMEM((block, inner), BF16),
         pltpu.VMEM((inner // 128, block, 128), BF16),
     )
+    held_shapes = (
+        pltpu.VMEM((5, 1, width), F32),
+        pltpu.VMEM(qkv_proj.shape, BF16),
+        pltpu.VMEM(norm_gain.shape, F32),
+        pltpu.VMEM(out_proj.shape, BF16),
+        pltpu.VMEM((LAT, width), F32),
+        pltpu.VMEM((pos.shape[0] + 32, width), BF16),
+        *block_shapes,
+    )
     block_cost = pl.CostEstimate(
         flops=2 * block * width * 4 * inner, bytes_accessed=6 << 20, transcendentals=0
     )
-    pos = jnp.asarray(position_parts(width))
+    params = pltpu.CompilerParams(vmem_limit_bytes=VMEM_GRANT)
+    sources = in_hbm(
+        modulation[0, 0][:, None, :],
+        in_proj,
+        qkv_proj,
+        norm_gain,
+        out_proj,
+        head_proj.T,
+        pos,
+    )
+    weight_scratch = [pltpu.VMEM(in_proj.shape, F32)]
+    weight_sems = pltpu.SemaphoreType.DMA((len(sources),))
+    packed, *held = pl.pallas_call(
+        early_kernel,
+        out_shape=(pltpu.VMEM((PACK_ROWS, block), F32), *held_shapes),
+        in_specs=[HBM] * 11,
+        out_specs=(VMEM,) * 11,
+        scratch_shapes=[
+            *pack_scratch(block, border_blocks),
+            *weight_scratch,
+            pltpu.SemaphoreType.DMA((4,)),
+            weight_sems,
+        ],
+        compiler_params=params,
+        name="pack_own_block",
+    )(*pack_operands(*placed), *sources)
+    first = seq_swap(packed, (3, 2))
+    near = seq_swap(packed, (1, 1))
+    swapped = swap_pair(first)
     held = pl.pallas_call(
-        own_kernel,
-        out_shape=(
-            pltpu.VMEM((5, 1, width), F32),
-            pltpu.VMEM(qkv_proj.shape, BF16),
-            pltpu.VMEM(norm_gain.shape, F32),
-            pltpu.VMEM(out_proj.shape, BF16),
-            pltpu.VMEM((LAT, width), F32),
-            pltpu.VMEM((pos.shape[0] + 32, width), BF16),
-            *block_shapes,
-        ),
-        in_specs=[VMEM] + [HBM] * 7,
+        late_kernel,
+        out_shape=held_shapes,
+        in_specs=[VMEM] + [HBM] * 7 + [VMEM] * 10,
         out_specs=(VMEM,) * 10,
-        scratch_shapes=[
-            pltpu.VMEM(in_proj.shape, F32),
-            pltpu.SemaphoreType.DMA((7,)),
-        ],
-        compiler_params=pltpu.CompilerParams(vmem_limit_bytes=VMEM_GRANT),
+        scratch_shapes=[*weight_scratch, weight_sems],
+        input_output_aliases={8 + i: i for i in range(10)},
+        compiler_params=params,
         cost_estimate=block_cost,
         name="own_block",
-    )(
-        packed,
-        *in_hbm(
-            modulation[0, 0][:, None, :],
-            in_proj,
-            qkv_proj,
-            norm_gain,
-            out_proj,
-            head_proj.T,
-            pos,
-        ),
-    )
+    )(packed, *sources, *held)
     weights, own_state = held[:6], held[6:]
     mod_rows, qkv_rows, gains, _, _, table = weights
     near_state = pl.pallas_call(
@@ -597,6 +650,19 @@
     )(packed, near, first, swapped, *weights, *own_state, *near_state)
 
 
+def pack_call(latents, voxel_coords, owner_map, border_blocks):
+    block = latents.shape[2]
+    return pl.pallas_call(
+        pack_kernel,
+        out_shape=pltpu.VMEM((PACK_ROWS, block), F32),
+        in_specs=[HBM] * 4,
+        out_specs=VMEM,
+        scratch_shapes=[*pack_scratch(block, border_blocks), pltpu.SemaphoreType.DMA((4,))],
+        compiler_params=pltpu.CompilerParams(vmem_limit_bytes=VMEM_GRANT),
+        name="pack",
+    )(*pack_operands(latents, voxel_coords, owner_map, border_blocks))
+
+
 def layer_norm(values):
     center = values - jnp.mean(values, axis=-1, keepdims=True)
     variance = jnp.mean(center * center, axis=-1, keepdims=True)
@@ -689,33 +755,13 @@
 ):
     count = lax.axis_size("seq")
     block = latents.shape[2]
-    packed = pl.pallas_call(
-        pack_kernel,
-        out_shape=pltpu.VMEM((PACK_ROWS, block), F32),
-        in_specs=[HBM] * 4,
-        out_specs=VMEM,
-        scratch_shapes=[
-            pltpu.VMEM((3, 1, block), I32),
-            pltpu.VMEM((1, block), I32),
-            pltpu.VMEM(border_blocks.shape[2:], I32),
-            pltpu.SemaphoreType.DMA((4,)),
-        ],
-        compiler_params=pltpu.CompilerParams(vmem_limit_bytes=VMEM_GRANT),
-        name="pack",
-    )(
-        *in_hbm(
-            latents[0],
-            jnp.swapaxes(voxel_coords, 0, 1),
-            owner_map.reshape(1, block),
-            border_blocks[0, 0],
-        )
-    )
+    placed = (latents, voxel_coords, owner_map, border_blocks)
     if count == 4 and count * block <= WHOLE_ASSET:
         velocity, blocks = whole_asset_velocity(
-            packed, modulation, in_proj, qkv_proj, norm_gain, out_proj, head_proj
+            placed, modulation, in_proj, qkv_proj, norm_gain, out_proj, head_proj
         )
     else:
-        blocks = lax.all_gather(packed, "seq", axis=0)
+        blocks = lax.all_gather(pack_call(*placed), "seq", axis=0)
         velocity = gathered_velocity(
             latents[0],
             voxel_coords[0],

time: 25.2 us -> 25.7 us (1.020)
  the two profiles are of different devices: /device:TPU:0 before, /device:TPU:3 now
where the time goes in v8:
time: 25.7 us; the launch traced here: 25.5 us
  Pallas kernels  17.8 us (69%)
  starting transfers between devices  4.18 us (16%)
  waiting for transfers between devices  2.19 us (9%)
  between operations  1.39 us (5%)
    pallas_call x1, Pallas kernels, decode_call(): pl.pallas_call(decode_kernel, out_shape=(jax.ShapeDtypeStruct((LAT, slots...  6.59 us
    pallas_call x1, Pallas kernels, whole_asset_velocity(): pl.pallas_call(velocity_kernel, out_shape=(pltpu.VMEM((count, LAT, block)...  5.6 us
    pallas_call x1, Pallas kernels, whole_asset_velocity(): pl.pallas_call(early_kernel, out_shape=(pltpu.VMEM((PACK_ROWS, block), F3...  3.85 us
    ppermute x2, starting transfers between devices, swap_pair(): return lax.ppermute(x, 'pair', [(0, 1), (1, 0)])  2.74 us
    ppermute x2, waiting for transfers between devices, seq_swap(): return lax.ppermute(x, ('pair', 'seq'), routes)  1.95 us
    ppermute x2, starting transfers between devices, seq_swap(): return lax.ppermute(x, ('pair', 'seq'), routes)  1.44 us
    pallas_call x1, Pallas kernels, whole_asset_velocity(): pl.pallas_call(near_kernel, out_shape=block_shapes, in_specs=[VMEM] * 6,...  1.35 us
  transfers between devices with their start and end apart: 4, of which 2 were waited for; matrix products, arithmetic and copies ran while one was open for 0% of the time, Pallas kernels for 7%

profile of v8, /device:TPU:3, one launch (start us, length us, event | category | flops | bytes accessed | tf_op | source)
XLA Modules:
  0.0 25.5 jit_solution(14960333147621793917)
XLA Ops:
  0.6 3.9 %pack_own_block.1 = (f32[16,128]{1,0:T(8,128)S(1)}, f32[5,1,1024]{2,1,0:T(1,128)S(1)}, bf16[1024,1536]{1,0:T(8,128)(2,1)S(1)}, f32[2,512]{1,0:T(2,128)S(1)}, bf1...) custom-call(f32[8,128]{1,0:T(8,128)} %bitcast.20, ...), custom_call_target="tpu_custom_call" | custom-call | tf_op jit(solution)/shard_map/pack_own_block/pallas_call | solution.py:593
  4.5 0.1 collective-permute-start.1
  4.6 1.4 %collective-permute-start = (f32[16,128]{1,0:T(8,128)S(1)}, f32[16,128]{1,0:T(8,128)S(1)}, u32[]{:S(2)}, u32[]{:S(2)}) collective-permute-start(f32[16,128]{1,0:T(8,128)S(1)} %get-tuple-element.31.refs_0_.own_ref), channel_id=1, source_target_pairs={{4,0},{0,4},{12,8},{8,12},{20,16},{16,20},{28,24},{24,28},{5,1},{1... | collective-permute-start | bytes 24584 | tf_op jit(solution)/shard_map/ppermute | solution.py:533
  5.9 0.1 own_block.1
  6.0 1.9 %collective-permute-done.1.later_ref.first_ref = f32[16,128]{1,0:T(8,128)S(1)} collective-permute-done((f32[16,128]{1,0:T(8,128)S(1)}, f32[16,128]{1,0:T(8,128)S(1)}, u32[]{:S(2)}, u32[]{:S(2)}) %collective-permute-start.1) | collective-permute-done | bytes 8224 | tf_op jit(solution)/shard_map/ppermute | solution.py:533
  8.0 2.7 %collective-permute-start.2 = (f32[16,128]{1,0:T(8,128)S(1)}, f32[16,128]{1,0:T(8,128)S(1)}, u32[]{:S(2)}, u32[]{:S(2)}) collective-permute-start(f32[16,128]{1,0:T(8,128)S(1)} %collective-permute-done.1.later_ref.first_ref), channel_id=1, source_target_pairs={{0,16},{16,0},{1,17},{17,1},{2,18},{18,2},{3,19},{19,3},{4,20},{20... | collective-permute-start | bytes 24584 | tf_op jit(solution)/shard_map/ppermute | solution.py:525
  10.7 0.0 collective-permute-done.near_ref
  10.7 1.4 %near_block.1 = (f32[128,1024]{1,0:T(8,128)S(1)}, bf16[128,512]{1,0:T(8,128)(2,1)S(1)}, bf16[128,512]{1,0:T(8,128)(2,1)S(1)}, bf16[4,128,128]{2,1,0:T(8,128)(2,1)S(1)}) custom-call(f32[16,128]{1,0:T(8,128)S(1)} %collective-permute-done.near_ref, f32[16,128]{1,0:T(8,128)S(1)} %collective-permute-done.1.later_ref.first_ref, ...), custom_call_target="tpu_custom_call" | custom-call | flops 536870912 | bytes 6291456 | tf_op jit(solution)/shard_map/near_block/pallas_call | solution.py:623
  12.1 0.0 collective-permute-done.2.swapped_ref
  12.1 0.0 copy-start
  12.1 0.0 copy-start.1
  12.1 0.0 copy-start.2
  12.1 5.6 %velocity.1 = (f32[4,8,128]{2,1,0:T(8,128)S(1)}, f32[4,16,128]{2,1,0:T(8,128)S(1)}) custom-call(f32[16,128]{1,0:T(8,128)S(1)} %get-tuple-element.31.refs_0_.own_ref, f32[16,128]{1,0:T(8,128)S(1)} %collective-permute-done.near_ref, f32[16,128]{1,0:T(8,128)S(1)} %collective-permute-done.1.later_ref.first_ref, ...), custom_call_target="tpu_custom_call" | custom-call | tf_op jit(solution)/shard_map/velocity/pallas_call | solution.py:632
  17.7 0.0 collective-permute-start.3
  18.4 0.3 %route.1.picks_ref = bf16[512,512]{1,0:T(8,128)(2,1)S(1)} custom-call(f32[4,16,128]{2,1,0:T(8,128)S(1)} %get-tuple-element.56.blocks_ref), custom_call_target="tpu_custom_call" | custom-call | bytes 1048576 | tf_op jit(solution)/shard_map/route/pallas_call | solution.py:492
  18.7 0.2 collective-permute-done.3.other_ref
  18.9 0.0 copy-done
  18.9 0.0 copy-done.1
  18.9 0.0 copy-done.2
  18.9 6.6 %decode.1 = (f32[8,256]{1,0:T(8,128)}, bf16[96,1024]{1,0:T(8,128)(2,1)}) custom-call(f32[4,16,128]{2,1,0:T(8,128)S(1)} %get-tuple-element.56.blocks_ref, bf16[512,512]{1,0:T(8,128)(2,1)S(1)} %route.1.picks_ref, f32[4,8,128]{2,1,0:T(8,128)S(1)} %get-tuple-element.57.mine_ref, f32[4,8,128]{2,1,0:T(8,128)S(1)} %collective-permute-done.3.other_ref, ...), custom_call_target="tpu_custom_call" | custom-call | tf_op jit(solution)/shard_map/decode/pallas_call | solution.py:510
Async XLA Ops:
  4.5 3.5 %collective-permute-start.1 = (f32[16,128]{1,0:T(8,128)S(1)}, f32[16,128]{1,0:T(8,128)S(1)}, u32[]{:S(2)}, u32[]{:S(2)}) collective-permute-start(f32[16,128]{1,0:T(8,128)S(1)} %get-tuple-element.31.refs_0_.own_ref), channel_id=1, source_target_pairs={{12,0},{8,4},{4,8},{0,12},{24,16},{28,20},{16,24},{20,28},{13,1},{... | collective-permute-start | bytes 24584 | tf_op jit(solution)/shard_map/ppermute | solution.py:533
  4.6 6.1 %collective-permute-start = (f32[16,128]{1,0:T(8,128)S(1)}, f32[16,128]{1,0:T(8,128)S(1)}, u32[]{:S(2)}, u32[]{:S(2)}) collective-permute-start(f32[16,128]{1,0:T(8,128)S(1)} %get-tuple-element.31.refs_0_.own_ref), channel_id=1, source_target_pairs={{4,0},{0,4},{12,8},{8,12},{20,16},{16,20},{28,24},{24,28},{5,1},{1... | collective-permute-start | bytes 24584 | tf_op jit(solution)/shard_map/ppermute | solution.py:533
  8.0 4.1 %collective-permute-start.2 = (f32[16,128]{1,0:T(8,128)S(1)}, f32[16,128]{1,0:T(8,128)S(1)}, u32[]{:S(2)}, u32[]{:S(2)}) collective-permute-start(f32[16,128]{1,0:T(8,128)S(1)} %collective-permute-done.1.later_ref.first_ref), channel_id=1, source_target_pairs={{0,16},{16,0},{1,17},{17,1},{2,18},{18,2},{3,19},{19,3},{4,20},{20... | collective-permute-start | bytes 24584 | tf_op jit(solution)/shard_map/ppermute | solution.py:525
  12.1 6.8 %copy-start = (bf16[27,768,96]{1,2,0:T(8,128)(2,1)S(1)}, bf16[27,768,96]{1,2,0:T(8,128)(2,1)}, u32[]{:S(2)}) copy-start(bf16[27,768,96]{1,2,0:T(8,128)(2,1)} %param.28) | copy-start | bytes 11943940
  12.1 6.8 %copy-start.1 = (s32[1,1,27,1024]{3,1,2,0:T(1,128)S(1)}, s32[1,1,27,1024]{3,1,2,0:T(1,128)}, u32[]{:S(2)}) copy-start(s32[1,1,27,1024]{3,1,2,0:T(1,128)} %param.27) | copy-start | bytes 331780
  12.1 6.8 %copy-start.2 = (f32[8,768]{1,0:T(8,128)S(1)}, f32[8,768]{1,0:T(8,128)}, u32[]{:S(2)}) copy-start(f32[8,768]{1,0:T(8,128)} %proj_ref.1) | copy-start | bytes 73732
  17.7 1.2 %collective-permute-start.3 = (f32[4,8,128]{2,1,0:T(8,128)S(1)}, f32[4,8,128]{2,1,0:T(8,128)S(1)}, u32[]{:S(2)}, u32[]{:S(2)}) collective-permute-start(f32[4,8,128]{2,1,0:T(8,128)S(1)} %get-tuple-element.57.mine_ref), channel_id=1, source_target_pairs={{0,16},{16,0},{1,17},{17,1},{2,18},{18,2},{3,19},{19,3},{4,20},{20... | collective-permute-start | bytes 49160 | tf_op jit(solution)/shard_map/ppermute | solution.py:525

commit v9 on v6

--- a/solution.py
+++ b/solution.py
@@ -137,7 +137,7 @@
         if which == 2:
             for half in range(group // 128):
                 lanes = slice(half * 128, (half + 1) * 128)
-                value_ref[col // 128 + half, rows, 0:128] = projected[:, lanes].astype(BF16)
+                value_ref[col // 128 + half, rows] = projected[:, lanes].astype(BF16)
         else:
             square = dot_ab((projected * projected).astype(BF16), averager)
             gains = gain_ref[which : which + 1, col : col + group]
@@ -155,9 +155,9 @@
     finish(*previous)
 
 
-def own_kernel(
+def first_kernel(
     own_ref,
-    later_ref,
+    mixed_ref,
     mod_hbm,
     in_hbm,
     qkv_hbm,
@@ -176,6 +176,7 @@
     key_ref,
     value_ref,
     in_ref,
+    normed_ref,
     sems,
 ):
     pos_rows = pos_hbm.shape[0]
@@ -201,12 +202,14 @@
     table_ref[pos_rows : pos_rows + 32, :] = jnp.concatenate(
         [in_high, in_high, in_low, jnp.zeros_like(in_low)], axis=0
     ).astype(BF16)
-    hidden = hidden_rows(own_ref[...], table_ref)
-    hidden_ref[...] = hidden
-    normed = modulated(hidden, mod_ref)
+    block = own_ref.shape[1]
+    hiddens = [hidden_rows(source[...], table_ref) for source in (own_ref, mixed_ref)]
+    for s, hidden in enumerate(hiddens):
+        hidden_ref[s * block : (s + 1) * block, :] = hidden
+        normed_ref[s * block : (s + 1) * block, :] = modulated(hidden, mod_ref)
     copies[4].wait()
-    block = own_ref.shape[1]
-    project(normed, qkv_ref, gain_ref, query_ref, key_ref, value_ref, slice(0, block))
+    rows = slice(0, len(hiddens) * block)
+    project(normed_ref[...], qkv_ref, gain_ref, query_ref, key_ref, value_ref, rows)
     copies[5].wait()
     copies[6].wait()
 
@@ -222,10 +225,10 @@
     out_ref,
     head_ref,
     table_ref,
-    own_hidden_ref,
-    own_query_ref,
-    own_key_ref,
-    own_value_ref,
+    done_hidden_ref,
+    done_query_ref,
+    done_key_ref,
+    done_value_ref,
     vel_ref,
     blocks_ref,
     hidden_ref,
@@ -246,41 +249,51 @@
     for place, source in zip(places, sources):
         blocks_ref[place] = source[...]
 
-    hidden_ref[0:block, :] = own_hidden_ref[...]
-    query_ref[0:block, :] = own_query_ref[...]
-    key_ref[0:block, :] = own_key_ref[...]
+    done = done_hidden_ref.shape[0] // block
+    here = slice(0, done * block)
+    ready = hidden_rows(sources[done][...], table_ref)
+    hidden_ref[here, :] = done_hidden_ref[...]
+    query_ref[here, :] = done_query_ref[...]
+    key_ref[here, :] = done_key_ref[...]
     for pair in range(inner // 128):
-        value_ref[pair, 0:block, 0:128] = own_value_ref[pair]
-    value_ref[:, :, 128:256] = jnp.ones((inner // 128, tokens, 128), BF16)
-    ready = hidden_rows(sources[1][...], table_ref)
-    for s in range(1, len(sources)):
+        value_ref[pair, here] = done_value_ref[pair]
+    for s in range(done, len(sources)):
         hidden = ready
         if s + 1 < len(sources):
             ready = hidden_rows(sources[s + 1][...], table_ref)
         hidden_ref[s * block : (s + 1) * block, :] = hidden
         normed_ref[s * block : (s + 1) * block, :] = modulated(hidden, mod_ref)
-    others = slice(block, tokens)
+    others = slice(done * block, tokens)
     project(normed_ref[others, :], qkv_ref, gain_ref, query_ref, key_ref, value_ref, others)
 
-    chunk = 256
-    first = lax.broadcasted_iota(I32, (chunk, 128), 1) < HEAD
-    todo = [(pair, q, half) for pair in range(inner // 128) for q in range(tokens // chunk) for half in range(2)]
-    def score(pair, q, half):
+    chunk = min(tokens, 512)
+    even = lax.broadcasted_iota(I32, (tokens, 128), 1) < HEAD
+    ones_rows = jnp.ones((16, tokens), BF16)
+    flipped = [value_ref[pair].T for pair in range(inner // 128)]
+    todo = [
+        (pair, half, q)
+        for pair in range(inner // 128)
+        for half in range(2)
+        for q in range(tokens // chunk)
+    ]
+
+    def score(pair, half, q):
         lanes = slice(pair * 128, (pair + 1) * 128)
-        query = query_ref[q * chunk : (q + 1) * chunk, lanes]
-        kept = jnp.where(first == (half == 0), query, jnp.zeros_like(query))
-        return dot_abt(kept, key_ref[:, lanes])
-    ready = score(*todo[0])
-    parts = []
-    for at, (pair, q, half) in enumerate(todo):
-        scores = ready
-        if at + 1 < len(todo):
-            ready = score(*todo[at + 1])
-        sums = dot_ab(jnp.exp(scores).astype(BF16), value_ref[pair])
-        parts.append(sums[:, 0:128] / sums[:, 128:256])
-        if half == 1:
-            att_ref[q * chunk : (q + 1) * chunk, pair * 128 : (pair + 1) * 128] = jnp.where(first, parts[0], parts[1]).astype(BF16)
-            parts = []
+        keys = key_ref[:, lanes]
+        kept = jnp.where(even == (half == 0), keys, jnp.zeros_like(keys))
+        return dot_abt(kept, query_ref[q * chunk : (q + 1) * chunk, lanes])
+
+    ready = [score(*item) for item in todo[:2]]
+    for at, (pair, half, q) in enumerate(todo):
+        scores = ready.pop(0)
+        if at + 2 < len(todo):
+            ready.append(score(*todo[at + 2]))
+        values = flipped[pair][half * HEAD : (half + 1) * HEAD]
+        values = jnp.concatenate([values, ones_rows], axis=0)
+        sums = dot_ab(values, jnp.exp(scores).astype(BF16))
+        dims = slice(pair * 128 + half * HEAD, pair * 128 + (half + 1) * HEAD)
+        mean = sums[0:HEAD] / sums[HEAD : HEAD + 1]
+        att_ref[dims, q * chunk : (q + 1) * chunk] = mean.astype(BF16)
 
     gate = mod_ref[2]
     head = head_ref[...]
@@ -290,7 +303,7 @@
     ones = jnp.ones((16, width), BF16)
     step = 128
     def attended(q):
-        return dot_ab(att_ref[q * step : (q + 1) * step, :], out_ref[...])
+        return dot_atb(att_ref[:, q * step : (q + 1) * step], out_ref[...])
     def middle(q, product):
         hidden = hidden_ref[q * step : (q + 1) * step, :] + gate * product
         center = hidden - jnp.mean(hidden, axis=1, keepdims=True)
@@ -497,7 +510,7 @@
     swapped = swap_pair(mixed)
     pos = jnp.asarray(position_parts(width))
     held = pl.pallas_call(
-        own_kernel,
+        first_kernel,
         out_shape=(
             pltpu.VMEM((5, 1, width), F32),
             pltpu.VMEM(qkv_proj.shape, BF16),
@@ -505,22 +518,23 @@
             pltpu.VMEM(out_proj.shape, BF16),
             pltpu.VMEM((LAT, width), F32),
             pltpu.VMEM((pos.shape[0] + 32, width), BF16),
-            pltpu.VMEM((block, width), F32),
-            pltpu.VMEM((block, inner), BF16),
-            pltpu.VMEM((block, inner), BF16),
-            pltpu.VMEM((inner // 128, block, 128), BF16),
+            pltpu.VMEM((2 * block, width), F32),
+            pltpu.VMEM((2 * block, inner), BF16),
+            pltpu.VMEM((2 * block, inner), BF16),
+            pltpu.VMEM((inner // 128, 2 * block, 128), BF16),
         ),
         in_specs=[VMEM] * 2 + [HBM] * 7,
         out_specs=(VMEM,) * 10,
         scratch_shapes=[
             pltpu.VMEM(in_proj.shape, F32),
+            pltpu.VMEM((2 * block, width), BF16),
             pltpu.SemaphoreType.DMA((7,)),
         ],
         compiler_params=pltpu.CompilerParams(vmem_limit_bytes=VMEM_GRANT),
         cost_estimate=pl.CostEstimate(
-            flops=2 * block * width * 4 * inner, bytes_accessed=6 << 20, transcendentals=0
+            flops=4 * block * width * 4 * inner, bytes_accessed=6 << 20, transcendentals=0
         ),
-        name="own_block",
+        name="first_blocks",
     )(
         packed,
         mixed,
@@ -547,8 +561,8 @@
             pltpu.VMEM((tokens, width), BF16),
             pltpu.VMEM((tokens, inner), BF16),
             pltpu.VMEM((tokens, inner), BF16),
-            pltpu.VMEM((inner // 128, tokens, 256), BF16),
-            pltpu.VMEM((tokens, inner), BF16),
+            pltpu.VMEM((inner // 128, tokens, 128), BF16),
+            pltpu.VMEM((inner, tokens), BF16),
         ],
         compiler_params=pltpu.CompilerParams(vmem_limit_bytes=VMEM_GRANT),
         name="velocity",

time: 24.7 us -> 24.3 us (0.984)
  Pallas kernels: 17 us -> 16.6 us
    pallas_call x1, Pallas kernels: 6.18 us -> 5.37 us  [whole_asset_velocity(): pl.pallas_call(velocity_kernel, out_shape=(pltpu.VMEM((count, LAT, block)...]
    pallas_call x1, Pallas kernels: 3.14 us -> 3.6 us  [whole_asset_velocity(): pl.pallas_call(first_kernel, out_shape=(pltpu.VMEM((5, 1, width), F32), p...]
  transfers between devices with their start and end apart: 4 -> 4, of which waited for: 0 -> 0; matrix products, arithmetic and copies ran while one was open for 0% -> 0% of each run, Pallas kernels for 14% -> 16%
where the time goes in v9:
time: 24.3 us; the launch traced here: 24.1 us
  Pallas kernels  16.6 us (68%)
  starting transfers between devices  6.1 us (25%)
  between operations  1.38 us (6%)
    pallas_call x1, Pallas kernels, decode_call(): pl.pallas_call(decode_kernel, out_shape=(jax.ShapeDtypeStruct((LAT, slots...  6.6 us
    ppermute x2, starting transfers between devices, seq_swap(): return lax.ppermute(x, ('pair', 'seq'), routes)  5.56 us
    pallas_call x1, Pallas kernels, whole_asset_velocity(): pl.pallas_call(velocity_kernel, out_shape=(pltpu.VMEM((count, LAT, block)...  5.37 us
    pallas_call x1, Pallas kernels, whole_asset_velocity(): pl.pallas_call(first_kernel, out_shape=(pltpu.VMEM((5, 1, width), F32), p...  3.6 us
    pallas_call x1, Pallas kernels, per_device(): pl.pallas_call(pack_kernel, out_shape=pltpu.VMEM((PACK_ROWS, block), F32)...  0.77 us
    ppermute x2, starting transfers between devices, swap_pair(): return lax.ppermute(x, 'pair', [(0, 1), (1, 0)])  0.53 us
  transfers between devices with their start and end apart: 4, of which 0 were waited for; matrix products, arithmetic and copies ran while one was open for 0% of the time, Pallas kernels for 16%

profile of v9, /device:TPU:0, one launch (start us, length us, event | category | flops | bytes accessed | tf_op | source)
XLA Modules:
  0.0 24.1 jit_solution(13716844853137369541)
XLA Ops:
  0.6 0.8 %pack.1.own_ref = f32[16,128]{1,0:T(8,128)S(1)} custom-call(f32[8,128]{1,0:T(8,128)} %bitcast.18, s32[3,1,128]{2,1,0:T(1,128)} %bitcast.19, s32[1,128]{1,0:T(1,128)} %bitcast.21, s32[2,8]{1,0:T(2,128)} %bitcast.20), custom_call_target="tpu_custom_call" | custom-call | tf_op jit(solution)/shard_map/pack/pallas_call | solution.py:664
  1.4 3.1 %collective-permute-start = (f32[16,128]{1,0:T(8,128)S(1)}, f32[16,128]{1,0:T(8,128)S(1)}, u32[]{:S(2)}, u32[]{:S(2)}) collective-permute-start(f32[16,128]{1,0:T(8,128)S(1)} %pack.1.own_ref), channel_id=1, source_target_pairs={{4,0},{0,4},{12,8},{8,12},{24,16},{28,20},{16,24},{20,28},{5,1},{1... | collective-permute-start | bytes 24584 | tf_op jit(solution)/shard_map/ppermute | solution.py:499
  4.5 2.5 %collective-permute-start.2 = (f32[16,128]{1,0:T(8,128)S(1)}, f32[16,128]{1,0:T(8,128)S(1)}, u32[]{:S(2)}, u32[]{:S(2)}) collective-permute-start(f32[16,128]{1,0:T(8,128)S(1)} %pack.1.own_ref), channel_id=1, source_target_pairs={{12,0},{8,4},{4,8},{0,12},{28,16},{24,20},{20,24},{16,28},{13,1},{... | collective-permute-start | bytes 24584 | tf_op jit(solution)/shard_map/ppermute | solution.py:499
  7.0 0.0 collective-permute-done.mixed_ref
  7.0 0.0 collective-permute-start.1
  7.0 3.6 %first_blocks.1 = (f32[5,1,1024]{2,1,0:T(1,128)S(1)}, bf16[1024,1536]{1,0:T(8,128)(2,1)S(1)}, f32[2,512]{1,0:T(2,128)S(1)}, bf16[512,1024]{1,0:T(8,128)(2,1)S(1)...) custom-call(f32[16,128]{1,0:T(8,128)S(1)} %pack.1.own_ref, ...), custom_call_target="tpu_custom_call" | custom-call | flops 1073741824 | bytes 6291456 | tf_op jit(solution)/shard_map/first_blocks/pallas_call | solution.py:512
  10.6 0.0 collective-permute-done.2.far_ref
  10.6 0.0 collective-permute-done.1.swapped_ref
  10.6 0.0 copy-start
  10.6 0.0 copy-start.1
  10.6 0.0 copy-start.2
  10.6 5.4 %velocity.1 = (f32[4,8,128]{2,1,0:T(8,128)S(1)}, f32[4,16,128]{2,1,0:T(8,128)S(1)}) custom-call(f32[16,128]{1,0:T(8,128)S(1)} %pack.1.own_ref, f32[16,128]{1,0:T(8,128)S(1)} %collective-permute-done.mixed_ref, f32[16,128]{1,0:T(8,128)S(1)} %collective-permute-done.1.swapped_ref, f32[16,128]{1,0:T(8,128)S(1)} %collective-permute-done.2.far_ref, ...), custom_call_target="tpu_custom_call" | custom-call | tf_op jit(solution)/shard_map/velocity/pallas_call | solution.py:551
  16.0 0.5 %collective-permute-start.3 = (f32[4,8,128]{2,1,0:T(8,128)S(1)}, f32[4,8,128]{2,1,0:T(8,128)S(1)}, u32[]{:S(2)}, u32[]{:S(2)}) collective-permute-start(f32[4,8,128]{2,1,0:T(8,128)S(1)} %get-tuple-element.27.mine_ref), channel_id=1, source_target_pairs={{0,16},{16,0},{1,17},{17,1},{2,18},{18,2},{3,19},{19,3},{4,20},{20... | collective-permute-start | bytes 49160 | tf_op jit(solution)/shard_map/ppermute | solution.py:491
  17.2 0.3 %route.1.picks_ref = bf16[512,512]{1,0:T(8,128)(2,1)S(1)} custom-call(f32[4,16,128]{2,1,0:T(8,128)S(1)} %get-tuple-element.26.blocks_ref), custom_call_target="tpu_custom_call" | custom-call | bytes 1048576 | tf_op jit(solution)/shard_map/route/pallas_call | solution.py:458
  17.5 0.0 collective-permute-done.3.other_ref
  17.5 0.0 copy-done
  17.5 0.0 copy-done.1
  17.5 0.0 copy-done.2
  17.5 6.6 %decode.1 = (f32[8,256]{1,0:T(8,128)}, bf16[96,1024]{1,0:T(8,128)(2,1)}) custom-call(f32[4,16,128]{2,1,0:T(8,128)S(1)} %get-tuple-element.26.blocks_ref, bf16[512,512]{1,0:T(8,128)(2,1)S(1)} %route.1.picks_ref, f32[4,8,128]{2,1,0:T(8,128)S(1)} %get-tuple-element.27.mine_ref, f32[4,8,128]{2,1,0:T(8,128)S(1)} %collective-permute-done.3.other_ref, ...), custom_call_target="tpu_custom_call" | custom-call | tf_op jit(solution)/shard_map/decode/pallas_call | solution.py:476
Async XLA Ops:
  1.4 5.6 %collective-permute-start = (f32[16,128]{1,0:T(8,128)S(1)}, f32[16,128]{1,0:T(8,128)S(1)}, u32[]{:S(2)}, u32[]{:S(2)}) collective-permute-start(f32[16,128]{1,0:T(8,128)S(1)} %pack.1.own_ref), channel_id=1, source_target_pairs={{4,0},{0,4},{12,8},{8,12},{24,16},{28,20},{16,24},{20,28},{5,1},{1... | collective-permute-start | bytes 24584 | tf_op jit(solution)/shard_map/ppermute | solution.py:499
  4.5 6.1 %collective-permute-start.2 = (f32[16,128]{1,0:T(8,128)S(1)}, f32[16,128]{1,0:T(8,128)S(1)}, u32[]{:S(2)}, u32[]{:S(2)}) collective-permute-start(f32[16,128]{1,0:T(8,128)S(1)} %pack.1.own_ref), channel_id=1, source_target_pairs={{12,0},{8,4},{4,8},{0,12},{28,16},{24,20},{20,24},{16,28},{13,1},{... | collective-permute-start | bytes 24584 | tf_op jit(solution)/shard_map/ppermute | solution.py:499
  7.0 3.6 %collective-permute-start.1 = (f32[16,128]{1,0:T(8,128)S(1)}, f32[16,128]{1,0:T(8,128)S(1)}, u32[]{:S(2)}, u32[]{:S(2)}) collective-permute-start(f32[16,128]{1,0:T(8,128)S(1)} %collective-permute-done.mixed_ref), channel_id=1, source_target_pairs={{0,16},{16,0},{1,17},{17,1},{2,18},{18,2},{3,19},{19,3},{4,20},{20... | collective-permute-start | bytes 24584 | tf_op jit(solution)/shard_map/ppermute | solution.py:491
  10.6 6.9 %copy-start = (bf16[27,768,96]{1,2,0:T(8,128)(2,1)S(1)}, bf16[27,768,96]{1,2,0:T(8,128)(2,1)}, u32[]{:S(2)}) copy-start(bf16[27,768,96]{1,2,0:T(8,128)(2,1)} %param.28) | copy-start | bytes 11943940
  10.6 6.9 %copy-start.1 = (s32[1,1,27,1024]{3,1,2,0:T(1,128)S(1)}, s32[1,1,27,1024]{3,1,2,0:T(1,128)}, u32[]{:S(2)}) copy-start(s32[1,1,27,1024]{3,1,2,0:T(1,128)} %param.27) | copy-start | bytes 331780
  10.6 6.9 %copy-start.2 = (f32[8,768]{1,0:T(8,128)S(1)}, f32[8,768]{1,0:T(8,128)}, u32[]{:S(2)}) copy-start(f32[8,768]{1,0:T(8,128)} %proj_ref.1) | copy-start | bytes 73732
  16.0 1.5 %collective-permute-start.3 = (f32[4,8,128]{2,1,0:T(8,128)S(1)}, f32[4,8,128]{2,1,0:T(8,128)S(1)}, u32[]{:S(2)}, u32[]{:S(2)}) collective-permute-start(f32[4,8,128]{2,1,0:T(8,128)S(1)} %get-tuple-element.27.mine_ref), channel_id=1, source_target_pairs={{0,16},{16,0},{1,17},{17,1},{2,18},{18,2},{3,19},{19,3},{4,20},{20... | collective-permute-start | bytes 49160 | tf_op jit(solution)/shard_map/ppermute | solution.py:491

commit v10 on v8

--- a/solution.py
+++ b/solution.py
@@ -137,7 +137,7 @@
         if which == 2:
             for half in range(group // 128):
                 lanes = slice(half * 128, (half + 1) * 128)
-                value_ref[col // 128 + half, rows, 0:128] = projected[:, lanes].astype(BF16)
+                value_ref[col // 128 + half, rows] = projected[:, lanes].astype(BF16)
         else:
             square = dot_ab((projected * projected).astype(BF16), averager)
             gains = gain_ref[which : which + 1, col : col + group]
@@ -155,8 +155,8 @@
     finish(*previous)
 
 
-def first_half():
-    return lax.axis_index("seq") < lax.axis_size("seq") // 2
+def at_front():
+    return lax.axis_index("seq") == 0
 
 
 def weight_copies(sources, targets, sems):
@@ -177,23 +177,12 @@
     ]
 
 
-def own_work(pack_ref, in_ref, copies, outs):
-    mod_ref, qkv_ref, gain_ref, _, _, table_ref, hidden_ref, query_ref, key_ref, value_ref = outs
-    for copy in copies[:4]:
-        copy.wait()
+def finish_table(in_ref, table_ref):
     in_high, in_low = split_two(in_ref[...])
-    pos_rows = table_ref.shape[0] - 32
-    table_ref[pos_rows : pos_rows + 32, :] = jnp.concatenate(
+    rows = table_ref.shape[0] - 32
+    table_ref[rows : rows + 32, :] = jnp.concatenate(
         [in_high, in_high, in_low, jnp.zeros_like(in_low)], axis=0
     ).astype(BF16)
-    hidden = hidden_rows(pack_ref[...], table_ref)
-    hidden_ref[...] = hidden
-    normed = modulated(hidden, mod_ref)
-    copies[4].wait()
-    rows = slice(0, pack_ref.shape[1])
-    project(normed, qkv_ref, gain_ref, query_ref, key_ref, value_ref, rows)
-    copies[5].wait()
-    copies[6].wait()
 
 
 def copy_targets(in_ref, outs):
@@ -202,71 +191,70 @@
 
 
 def early_kernel(*refs):
-    inputs, sources, pack_ref, outs = refs[:4], refs[4:11], refs[11], refs[12:22]
-    coord_ref, owner_ref, border_ref, in_ref, pack_sems, sems = refs[22:]
+    inputs, sources, pack_ref, outs = refs[:4], refs[4:11], refs[11], refs[12:18]
+    coord_ref, owner_ref, border_ref, in_ref, pack_sems, sems = refs[18:]
     copies = weight_copies(sources, copy_targets(in_ref, outs), sems)
 
-    @pl.when(first_half())
+    @pl.when(at_front())
     def _():
         for copy in copies:
             copy.start()
 
     pack_kernel(*inputs, pack_ref, coord_ref, owner_ref, border_ref, pack_sems)
 
-    @pl.when(first_half())
+    @pl.when(at_front())
     def _():
-        own_work(pack_ref, in_ref, copies, outs)
-
-
-def late_kernel(*refs):
-    pack_ref, sources, outs, (in_ref, sems) = refs[0], refs[1:8], refs[18:28], refs[28:]
-
-    @pl.when(jnp.logical_not(first_half()))
+        for copy in copies:
+            copy.wait()
+        finish_table(in_ref, outs[5])
+
+
+def first_kernel(*refs):
+    own_ref, mixed_ref, sources, outs, state = refs[0], refs[1], refs[2:9], refs[15:21], refs[21:25]
+    in_ref, normed_ref, sems = refs[25:]
+    mod_ref, qkv_ref, gain_ref, _, _, table_ref = outs
+    hidden_ref, query_ref, key_ref, value_ref = state
+    copies = weight_copies(sources, copy_targets(in_ref, outs), sems)
+    missing = jnp.logical_not(at_front())
+
+    @pl.when(missing)
     def _():
-        copies = weight_copies(sources, copy_targets(in_ref, outs), sems)
         for copy in copies:
             copy.start()
-        own_work(pack_ref, in_ref, copies, outs)
-
-
-def near_kernel(
-    near_ref,
-    later_ref,
-    mod_ref,
-    qkv_ref,
-    gain_ref,
-    table_ref,
-    hidden_ref,
-    query_ref,
-    key_ref,
-    value_ref,
-):
-    hidden = hidden_rows(near_ref[...], table_ref)
-    hidden_ref[...] = hidden
-    normed = modulated(hidden, mod_ref)
-    rows = slice(0, near_ref.shape[1])
-    project(normed, qkv_ref, gain_ref, query_ref, key_ref, value_ref, rows)
+        for copy in copies[:4]:
+            copy.wait()
+        finish_table(in_ref, table_ref)
+
+    block = own_ref.shape[1]
+    hiddens = [hidden_rows(source[...], table_ref) for source in (own_ref, mixed_ref)]
+    for s, hidden in enumerate(hiddens):
+        hidden_ref[s * block : (s + 1) * block, :] = hidden
+        normed_ref[s * block : (s + 1) * block, :] = modulated(hidden, mod_ref)
+
+    @pl.when(missing)
+    def _():
+        for copy in copies[4:]:
+            copy.wait()
+
+    rows = slice(0, len(hiddens) * block)
+    project(normed_ref[...], qkv_ref, gain_ref, query_ref, key_ref, value_ref, rows)
 
 
 def velocity_kernel(
     own_ref,
-    near_ref,
-    first_ref,
+    mixed_ref,
     swapped_ref,
+    far_ref,
     mod_ref,
     qkv_ref,
     gain_ref,
     out_ref,
     head_ref,
     table_ref,
-    own_hidden_ref,
-    own_query_ref,
-    own_key_ref,
-    own_value_ref,
-    near_hidden_ref,
-    near_query_ref,
-    near_key_ref,
-    near_value_ref,
+    done_hidden_ref,
+    done_query_ref,
+    done_key_ref,
+    done_value_ref,
     vel_ref,
     blocks_ref,
     hidden_ref,
@@ -282,52 +270,56 @@
     tokens = hidden_ref.shape[0]
     inner = out_ref.shape[0]
     block = own_ref.shape[1]
-    places = (me, me ^ 1, me ^ (3 - side), me ^ (2 + side))
-    sources = (own_ref, near_ref, first_ref, swapped_ref)
+    places = (me, me ^ (1 + side), me ^ (2 - side), me ^ 3)
+    sources = (own_ref, mixed_ref, swapped_ref, far_ref)
     for place, source in zip(places, sources):
         blocks_ref[place] = source[...]
 
-    value_ref[:, :, 128:256] = jnp.ones((inner // 128, tokens, 128), BF16)
-    ready = hidden_rows(first_ref[...], table_ref)
-    done = (
-        (own_hidden_ref, own_query_ref, own_key_ref, own_value_ref),
-        (near_hidden_ref, near_query_ref, near_key_ref, near_value_ref),
-    )
-    for s, (hidden, query, key, value) in enumerate(done):
-        here = slice(s * block, (s + 1) * block)
-        hidden_ref[here, :] = hidden[...]
-        query_ref[here, :] = query[...]
-        key_ref[here, :] = key[...]
-        for pair in range(inner // 128):
-            value_ref[pair, here, 0:128] = value[pair]
-    for s in range(len(done), len(sources)):
+    done = done_hidden_ref.shape[0] // block
+    here = slice(0, done * block)
+    ready = hidden_rows(sources[done][...], table_ref)
+    hidden_ref[here, :] = done_hidden_ref[...]
+    query_ref[here, :] = done_query_ref[...]
+    key_ref[here, :] = done_key_ref[...]
+    for pair in range(inner // 128):
+        value_ref[pair, here] = done_value_ref[pair]
+    for s in range(done, len(sources)):
         hidden = ready
         if s + 1 < len(sources):
             ready = hidden_rows(sources[s + 1][...], table_ref)
         hidden_ref[s * block : (s + 1) * block, :] = hidden
         normed_ref[s * block : (s + 1) * block, :] = modulated(hidden, mod_ref)
-    others = slice(len(done) * block, tokens)
+    others = slice(done * block, tokens)
     project(normed_ref[others, :], qkv_ref, gain_ref, query_ref, key_ref, value_ref, others)
 
-    chunk = 256
-    even = lax.broadcasted_iota(I32, (chunk, 128), 1) < HEAD
-    todo = [(pair, q, half) for pair in range(inner // 128) for q in range(tokens // chunk) for half in range(2)]
-    def score(pair, q, half):
+    chunk = min(tokens, 512)
+    even = lax.broadcasted_iota(I32, (tokens, 128), 1) < HEAD
+    ones_rows = jnp.ones((16, tokens), BF16)
+    flipped = [value_ref[pair].T for pair in range(inner // 128)]
+    todo = [
+        (pair, half, q)
+        for pair in range(inner // 128)
+        for half in range(2)
+        for q in range(tokens // chunk)
+    ]
+
+    def score(pair, half, q):
         lanes = slice(pair * 128, (pair + 1) * 128)
-        query = query_ref[q * chunk : (q + 1) * chunk, lanes]
-        kept = jnp.where(even == (half == 0), query, jnp.zeros_like(query))
-        return dot_abt(kept, key_ref[:, lanes])
-    ready = score(*todo[0])
-    parts = []
-    for at, (pair, q, half) in enumerate(todo):
-        scores = ready
-        if at + 1 < len(todo):
-            ready = score(*todo[at + 1])
-        sums = dot_ab(jnp.exp(scores).astype(BF16), value_ref[pair])
-        parts.append(sums[:, 0:128] / sums[:, 128:256])
-        if half == 1:
-            att_ref[q * chunk : (q + 1) * chunk, pair * 128 : (pair + 1) * 128] = jnp.where(even, parts[0], parts[1]).astype(BF16)
-            parts = []
+        keys = key_ref[:, lanes]
+        kept = jnp.where(even == (half == 0), keys, jnp.zeros_like(keys))
+        return dot_abt(kept, query_ref[q * chunk : (q + 1) * chunk, lanes])
+
+    ready = [score(*item) for item in todo[:2]]
+    for at, (pair, half, q) in enumerate(todo):
+        scores = ready.pop(0)
+        if at + 2 < len(todo):
+            ready.append(score(*todo[at + 2]))
+        values = flipped[pair][half * HEAD : (half + 1) * HEAD]
+        values = jnp.concatenate([values, ones_rows], axis=0)
+        sums = dot_ab(values, jnp.exp(scores).astype(BF16))
+        dims = slice(pair * 128 + half * HEAD, pair * 128 + (half + 1) * HEAD)
+        mean = sums[0:HEAD] / sums[HEAD : HEAD + 1]
+        att_ref[dims, q * chunk : (q + 1) * chunk] = mean.astype(BF16)
 
     gate = mod_ref[2]
     head = head_ref[...]
@@ -337,7 +329,7 @@
     ones = jnp.ones((16, width), BF16)
     step = 128
     def attended(q):
-        return dot_ab(att_ref[q * step : (q + 1) * step, :], out_ref[...])
+        return dot_atb(att_ref[:, q * step : (q + 1) * step], out_ref[...])
     def middle(q, product):
         hidden = hidden_ref[q * step : (q + 1) * step, :] + gate * product
         center = hidden - jnp.mean(hidden, axis=1, keepdims=True)
@@ -561,10 +553,10 @@
     inner = out_proj.shape[0]
     pos = jnp.asarray(position_parts(width))
     block_shapes = (
-        pltpu.VMEM((block, width), F32),
-        pltpu.VMEM((block, inner), BF16),
-        pltpu.VMEM((block, inner), BF16),
-        pltpu.VMEM((inner // 128, block, 128), BF16),
+        pltpu.VMEM((2 * block, width), F32),
+        pltpu.VMEM((2 * block, inner), BF16),
+        pltpu.VMEM((2 * block, inner), BF16),
+        pltpu.VMEM((inner // 128, 2 * block, 128), BF16),
     )
     held_shapes = (
         pltpu.VMEM((5, 1, width), F32),
@@ -573,10 +565,9 @@
         pltpu.VMEM(out_proj.shape, BF16),
         pltpu.VMEM((LAT, width), F32),
         pltpu.VMEM((pos.shape[0] + 32, width), BF16),
-        *block_shapes,
     )
     block_cost = pl.CostEstimate(
-        flops=2 * block * width * 4 * inner, bytes_accessed=6 << 20, transcendentals=0
+        flops=4 * block * width * 4 * inner, bytes_accessed=6 << 20, transcendentals=0
     )
     params = pltpu.CompilerParams(vmem_limit_bytes=VMEM_GRANT)
     sources = in_hbm(
@@ -594,7 +585,7 @@
         early_kernel,
         out_shape=(pltpu.VMEM((PACK_ROWS, block), F32), *held_shapes),
         in_specs=[HBM] * 11,
-        out_specs=(VMEM,) * 11,
+        out_specs=(VMEM,) * 7,
         scratch_shapes=[
             *pack_scratch(block, border_blocks),
             *weight_scratch,
@@ -602,52 +593,41 @@
             weight_sems,
         ],
         compiler_params=params,
-        name="pack_own_block",
+        name="pack",
     )(*pack_operands(*placed), *sources)
-    first = seq_swap(packed, (3, 2))
-    near = seq_swap(packed, (1, 1))
-    swapped = swap_pair(first)
+    mixed = seq_swap(packed, (1, 2))
+    far = seq_swap(packed, (3, 3))
+    swapped = swap_pair(mixed)
     held = pl.pallas_call(
-        late_kernel,
-        out_shape=held_shapes,
-        in_specs=[VMEM] + [HBM] * 7 + [VMEM] * 10,
+        first_kernel,
+        out_shape=(*held_shapes, *block_shapes),
+        in_specs=[VMEM] * 2 + [HBM] * 7 + [VMEM] * 6,
         out_specs=(VMEM,) * 10,
-        scratch_shapes=[*weight_scratch, weight_sems],
-        input_output_aliases={8 + i: i for i in range(10)},
+        scratch_shapes=[*weight_scratch, pltpu.VMEM((2 * block, width), BF16), weight_sems],
+        input_output_aliases={9 + i: i for i in range(6)},
         compiler_params=params,
         cost_estimate=block_cost,
-        name="own_block",
-    )(packed, *sources, *held)
-    weights, own_state = held[:6], held[6:]
-    mod_rows, qkv_rows, gains, _, _, table = weights
-    near_state = pl.pallas_call(
-        near_kernel,
-        out_shape=block_shapes,
-        in_specs=[VMEM] * 6,
-        out_specs=(VMEM,) * 4,
-        compiler_params=pltpu.CompilerParams(vmem_limit_bytes=VMEM_GRANT),
-        cost_estimate=block_cost,
-        name="near_block",
-    )(near, first, mod_rows, qkv_rows, gains, table)
+        name="first_blocks",
+    )(packed, mixed, *sources, *held)
     return pl.pallas_call(
         velocity_kernel,
         out_shape=(
             pltpu.VMEM((count, LAT, block), F32),
             pltpu.VMEM((count, PACK_ROWS, block), F32),
         ),
-        in_specs=[VMEM] * 18,
+        in_specs=[VMEM] * 14,
         out_specs=(VMEM, VMEM),
         scratch_shapes=[
             pltpu.VMEM((tokens, width), F32),
             pltpu.VMEM((tokens, width), BF16),
             pltpu.VMEM((tokens, inner), BF16),
             pltpu.VMEM((tokens, inner), BF16),
-            pltpu.VMEM((inner // 128, tokens, 256), BF16),
-            pltpu.VMEM((tokens, inner), BF16),
+            pltpu.VMEM((inner // 128, tokens, 128), BF16),
+            pltpu.VMEM((inner, tokens), BF16),
         ],
         compiler_params=pltpu.CompilerParams(vmem_limit_bytes=VMEM_GRANT),
         name="velocity",
-    )(packed, near, first, swapped, *weights, *own_state, *near_state)
+    )(packed, mixed, swapped, far, *held)
 
 
 def pack_call(latents, voxel_coords, owner_map, border_blocks):

time: 25.7 us -> 23.3 us (0.907)
  the two profiles are of different devices: /device:TPU:3 before, /device:TPU:0 now
where the time goes in v10:
time: 23.3 us; the launch traced here: 23.2 us
  Pallas kernels  16.9 us (73%)
  starting transfers between devices  3.93 us (17%)
  between operations  1.35 us (6%)
  waiting for transfers between devices  0.94 us (4%)
    pallas_call x1, Pallas kernels, decode_call(): pl.pallas_call(decode_kernel, out_shape=(jax.ShapeDtypeStruct((LAT, slots...  6.58 us
    pallas_call x1, Pallas kernels, whole_asset_velocity(): pl.pallas_call(velocity_kernel, out_shape=(pltpu.VMEM((count, LAT, block)...  5.32 us
    ppermute x2, starting transfers between devices, seq_swap(): return lax.ppermute(x, ('pair', 'seq'), routes)  3.77 us
    pallas_call x1, Pallas kernels, whole_asset_velocity(): pl.pallas_call(early_kernel, out_shape=(pltpu.VMEM((PACK_ROWS, block), F3...  2.63 us
    pallas_call x1, Pallas kernels, whole_asset_velocity(): pl.pallas_call(first_kernel, out_shape=(*held_shapes, *block_shapes), in_...  2.1 us
    ppermute x2, waiting for transfers between devices, seq_swap(): return lax.ppermute(x, ('pair', 'seq'), routes)  0.71 us
  transfers between devices with their start and end apart: 4, of which 2 were waited for; matrix products, arithmetic and copies ran while one was open for 0% of the time, Pallas kernels for 10%

profile of v10, /device:TPU:0, one launch (start us, length us, event | category | flops | bytes accessed | tf_op | source)
XLA Modules:
  0.0 23.2 jit_solution(6537963055622780305)
XLA Ops:
  0.6 2.6 %pack.1 = (f32[16,128]{1,0:T(8,128)S(1)}, f32[5,1,1024]{2,1,0:T(1,128)S(1)}, bf16[1024,1536]{1,0:T(8,128)(2,1)S(1)}, f32[2,512]{1,0:T(2,128)S(1)}, bf16[512,1024...) custom-call(f32[8,128]{1,0:T(8,128)} %bitcast.20, s32[3,1,128]{2,1,0:T(1,128)} %bitcast.21, ...), custom_call_target="tpu_custom_call" | custom-call | tf_op jit(solution)/shard_map/pack/pallas_call | solution.py:584
  3.3 1.3 %collective-permute-start = (f32[16,128]{1,0:T(8,128)S(1)}, f32[16,128]{1,0:T(8,128)S(1)}, u32[]{:S(2)}, u32[]{:S(2)}) collective-permute-start(f32[16,128]{1,0:T(8,128)S(1)} %get-tuple-element.23.refs_0_.own_ref), channel_id=1, source_target_pairs={{4,0},{0,4},{12,8},{8,12},{24,16},{28,20},{16,24},{20,28},{5,1},{1... | collective-permute-start | bytes 24584 | tf_op jit(solution)/shard_map/ppermute | solution.py:525
  4.6 2.5 %collective-permute-start.2 = (f32[16,128]{1,0:T(8,128)S(1)}, f32[16,128]{1,0:T(8,128)S(1)}, u32[]{:S(2)}, u32[]{:S(2)}) collective-permute-start(f32[16,128]{1,0:T(8,128)S(1)} %get-tuple-element.23.refs_0_.own_ref), channel_id=1, source_target_pairs={{12,0},{8,4},{4,8},{0,12},{28,16},{24,20},{20,24},{16,28},{13,1},{... | collective-permute-start | bytes 24584 | tf_op jit(solution)/shard_map/ppermute | solution.py:525
  7.0 0.0 collective-permute-done.refs_1_.mixed_ref
  7.0 0.2 collective-permute-start.1
  7.2 2.1 %first_blocks.1 = (f32[5,1,1024]{2,1,0:T(1,128)S(1)}, bf16[1024,1536]{1,0:T(8,128)(2,1)S(1)}, f32[2,512]{1,0:T(2,128)S(1)}, bf16[512,1024]{1,0:T(8,128)(2,1)S(1)...) custom-call(f32[16,128]{1,0:T(8,128)S(1)} %get-tuple-element.23.refs, ...), custom_call_target="tpu_custom_call", output_to_operand_aliasing={{0}: (9, {}), {1}: (10, {}), {2}: (11, {}), {3}: (12, {}), ... | custom-call | flops 1073741824 | bytes 6291456 | tf_op jit(solution)/shard_map/first_blocks/pallas_call | solution.py:601
  9.3 0.7 %collective-permute-done.2.far_ref = f32[16,128]{1,0:T(8,128)S(1)} collective-permute-done((f32[16,128]{1,0:T(8,128)S(1)}, f32[16,128]{1,0:T(8,128)S(1)}, u32[]{:S(2)}, u32[]{:S(2)}) %collective-permute-start.2) | collective-permute-done | bytes 8224 | tf_op jit(solution)/shard_map/ppermute | solution.py:525
  10.0 0.0 collective-permute-done.1.swapped_ref
  10.0 0.0 copy-start
  10.0 0.0 copy-start.1
  10.0 0.0 copy-start.2
  10.0 5.3 %velocity.1 = (f32[4,8,128]{2,1,0:T(8,128)S(1)}, f32[4,16,128]{2,1,0:T(8,128)S(1)}) custom-call(f32[16,128]{1,0:T(8,128)S(1)} %get-tuple-element.23.refs_0_.own_ref, f32[16,128]{1,0:T(8,128)S(1)} %collective-permute-done.refs_1_.mixed_ref, f32[16,128]{1,0:T(8,128)S(1)} %collective-permute-done.1.swapped_ref, f32[16,128]{1,0:T(8,128)S(1)} %collective-permute-done.2.far_ref, ...), custom_call_target="tpu_custom_call" | custom-call | tf_op jit(solution)/shard_map/velocity/pallas_call | solution.py:612
  15.3 0.0 collective-permute-start.3
  16.0 0.3 %route.1.picks_ref = bf16[512,512]{1,0:T(8,128)(2,1)S(1)} custom-call(f32[4,16,128]{2,1,0:T(8,128)S(1)} %get-tuple-element.40.blocks_ref), custom_call_target="tpu_custom_call" | custom-call | bytes 1048576 | tf_op jit(solution)/shard_map/route/pallas_call | solution.py:484
  16.3 0.2 %collective-permute-done.3.other_ref = f32[4,8,128]{2,1,0:T(8,128)S(1)} collective-permute-done((f32[4,8,128]{2,1,0:T(8,128)S(1)}, f32[4,8,128]{2,1,0:T(8,128)S(1)}, u32[]{:S(2)}, u32[]{:S(2)}) %collective-permute-start.3) | collective-permute-done | bytes 16416 | tf_op jit(solution)/shard_map/ppermute | solution.py:517
  16.6 0.0 copy-done
  16.6 0.0 copy-done.1
  16.6 0.0 copy-done.2
  16.6 6.6 %decode.1 = (f32[8,256]{1,0:T(8,128)}, bf16[96,1024]{1,0:T(8,128)(2,1)}) custom-call(f32[4,16,128]{2,1,0:T(8,128)S(1)} %get-tuple-element.40.blocks_ref, bf16[512,512]{1,0:T(8,128)(2,1)S(1)} %route.1.picks_ref, f32[4,8,128]{2,1,0:T(8,128)S(1)} %get-tuple-element.41.mine_ref, f32[4,8,128]{2,1,0:T(8,128)S(1)} %collective-permute-done.3.other_ref, ...), custom_call_target="tpu_custom_call" | custom-call | tf_op jit(solution)/shard_map/decode/pallas_call | solution.py:502
Async XLA Ops:
  3.3 3.8 %collective-permute-start = (f32[16,128]{1,0:T(8,128)S(1)}, f32[16,128]{1,0:T(8,128)S(1)}, u32[]{:S(2)}, u32[]{:S(2)}) collective-permute-start(f32[16,128]{1,0:T(8,128)S(1)} %get-tuple-element.23.refs_0_.own_ref), channel_id=1, source_target_pairs={{4,0},{0,4},{12,8},{8,12},{24,16},{28,20},{16,24},{20,28},{5,1},{1... | collective-permute-start | bytes 24584 | tf_op jit(solution)/shard_map/ppermute | solution.py:525
  4.6 5.4 %collective-permute-start.2 = (f32[16,128]{1,0:T(8,128)S(1)}, f32[16,128]{1,0:T(8,128)S(1)}, u32[]{:S(2)}, u32[]{:S(2)}) collective-permute-start(f32[16,128]{1,0:T(8,128)S(1)} %get-tuple-element.23.refs_0_.own_ref), channel_id=1, source_target_pairs={{12,0},{8,4},{4,8},{0,12},{28,16},{24,20},{20,24},{16,28},{13,1},{... | collective-permute-start | bytes 24584 | tf_op jit(solution)/shard_map/ppermute | solution.py:525
  7.0 3.0 %collective-permute-start.1 = (f32[16,128]{1,0:T(8,128)S(1)}, f32[16,128]{1,0:T(8,128)S(1)}, u32[]{:S(2)}, u32[]{:S(2)}) collective-permute-start(f32[16,128]{1,0:T(8,128)S(1)} %collective-permute-done.refs_1_.mixed_ref), channel_id=1, source_target_pairs={{0,16},{16,0},{1,17},{17,1},{2,18},{18,2},{3,19},{19,3},{4,20},{20... | collective-permute-start | bytes 24584 | tf_op jit(solution)/shard_map/ppermute | solution.py:517
  10.0 6.5 %copy-start = (bf16[27,768,96]{1,2,0:T(8,128)(2,1)S(1)}, bf16[27,768,96]{1,2,0:T(8,128)(2,1)}, u32[]{:S(2)}) copy-start(bf16[27,768,96]{1,2,0:T(8,128)(2,1)} %param.28) | copy-start | bytes 11943940
  10.0 6.5 %copy-start.1 = (s32[1,1,27,1024]{3,1,2,0:T(1,128)S(1)}, s32[1,1,27,1024]{3,1,2,0:T(1,128)}, u32[]{:S(2)}) copy-start(s32[1,1,27,1024]{3,1,2,0:T(1,128)} %param.27) | copy-start | bytes 331780
  10.0 6.5 %copy-start.2 = (f32[8,768]{1,0:T(8,128)S(1)}, f32[8,768]{1,0:T(8,128)}, u32[]{:S(2)}) copy-start(f32[8,768]{1,0:T(8,128)} %proj_ref.1) | copy-start | bytes 73732
  15.3 1.2 %collective-permute-start.3 = (f32[4,8,128]{2,1,0:T(8,128)S(1)}, f32[4,8,128]{2,1,0:T(8,128)S(1)}, u32[]{:S(2)}, u32[]{:S(2)}) collective-permute-start(f32[4,8,128]{2,1,0:T(8,128)S(1)} %get-tuple-element.41.mine_ref), channel_id=1, source_target_pairs={{0,16},{16,0},{1,17},{17,1},{2,18},{18,2},{3,19},{19,3},{4,20},{20... | collective-permute-start | bytes 49160 | tf_op jit(solution)/shard_map/ppermute | solution.py:517

commit v11 on v10

--- a/solution.py
+++ b/solution.py
@@ -197,14 +197,14 @@
 
     @pl.when(at_front())
     def _():
-        for copy in copies:
+        for copy in copies[:5]:
             copy.start()
 
     pack_kernel(*inputs, pack_ref, coord_ref, owner_ref, border_ref, pack_sems)
 
     @pl.when(at_front())
     def _():
-        for copy in copies:
+        for copy in copies[:5]:
             copy.wait()
         finish_table(in_ref, outs[5])
 
@@ -219,8 +219,14 @@
 
     @pl.when(missing)
     def _():
-        for copy in copies:
+        for copy in copies[:5]:
             copy.start()
+
+    for copy in copies[5:]:
+        copy.start()
+
+    @pl.when(missing)
+    def _():
         for copy in copies[:4]:
             copy.wait()
         finish_table(in_ref, table_ref)
@@ -233,11 +239,12 @@
 
     @pl.when(missing)
     def _():
-        for copy in copies[4:]:
-            copy.wait()
+        copies[4].wait()
 
     rows = slice(0, len(hiddens) * block)
     project(normed_ref[...], qkv_ref, gain_ref, query_ref, key_ref, value_ref, rows)
+    for copy in copies[5:]:
+        copy.wait()
 
 
 def velocity_kernel(

time: 23.3 us -> 23.3 us (level)
  Pallas kernels: 16.9 us -> 16.6 us
    pallas_call x1, Pallas kernels: 2.63 us -> 2.34 us  [whole_asset_velocity(): pl.pallas_call(early_kernel, out_shape=(pltpu.VMEM((PACK_ROWS, block), F3...]
    ppermute x2, starting transfers between devices: 3.77 us -> 4.06 us  [seq_swap(): return lax.ppermute(x, ('pair', 'seq'), routes)]
where the time goes in v11:
time: 23.3 us; the launch traced here: 23.2 us
  Pallas kernels  16.6 us (71%)
  starting transfers between devices  4.07 us (17%)
  between operations  1.35 us (6%)
  waiting for transfers between devices  1.08 us (5%)
    pallas_call x1, Pallas kernels, decode_call(): pl.pallas_call(decode_kernel, out_shape=(jax.ShapeDtypeStruct((LAT, slots...  6.58 us
    pallas_call x1, Pallas kernels, whole_asset_velocity(): pl.pallas_call(velocity_kernel, out_shape=(pltpu.VMEM((count, LAT, block)...  5.33 us
    ppermute x2, starting transfers between devices, seq_swap(): return lax.ppermute(x, ('pair', 'seq'), routes)  4.06 us
    pallas_call x1, Pallas kernels, whole_asset_velocity(): pl.pallas_call(early_kernel, out_shape=(pltpu.VMEM((PACK_ROWS, block), F3...  2.34 us
    pallas_call x1, Pallas kernels, whole_asset_velocity(): pl.pallas_call(first_kernel, out_shape=(*held_shapes, *block_shapes), in_...  2.11 us
    ppermute x2, waiting for transfers between devices, seq_swap(): return lax.ppermute(x, ('pair', 'seq'), routes)  0.85 us
  transfers between devices with their start and end apart: 4, of which 2 were waited for; matrix products, arithmetic and copies ran while one was open for 0% of the time, Pallas kernels for 10%

profile of v11, /device:TPU:0, one launch (start us, length us, event | category | flops | bytes accessed | tf_op | source)
XLA Modules:
  0.0 23.2 jit_solution(820940773963051916)
XLA Ops:
  0.6 2.3 %pack.1 = (f32[16,128]{1,0:T(8,128)S(1)}, f32[5,1,1024]{2,1,0:T(1,128)S(1)}, bf16[1024,1536]{1,0:T(8,128)(2,1)S(1)}, f32[2,512]{1,0:T(2,128)S(1)}, bf16[512,1024...) custom-call(f32[8,128]{1,0:T(8,128)} %bitcast.20, s32[3,1,128]{2,1,0:T(1,128)} %bitcast.21, ...), custom_call_target="tpu_custom_call" | custom-call | tf_op jit(solution)/shard_map/pack/pallas_call | solution.py:591
  3.0 1.6 %collective-permute-start = (f32[16,128]{1,0:T(8,128)S(1)}, f32[16,128]{1,0:T(8,128)S(1)}, u32[]{:S(2)}, u32[]{:S(2)}) collective-permute-start(f32[16,128]{1,0:T(8,128)S(1)} %get-tuple-element.23.refs_0_.own_ref), channel_id=1, source_target_pairs={{4,0},{0,4},{12,8},{8,12},{24,16},{28,20},{16,24},{20,28},{5,1},{1... | collective-permute-start | bytes 24584 | tf_op jit(solution)/shard_map/ppermute | solution.py:532
  4.6 2.5 %collective-permute-start.2 = (f32[16,128]{1,0:T(8,128)S(1)}, f32[16,128]{1,0:T(8,128)S(1)}, u32[]{:S(2)}, u32[]{:S(2)}) collective-permute-start(f32[16,128]{1,0:T(8,128)S(1)} %get-tuple-element.23.refs_0_.own_ref), channel_id=1, source_target_pairs={{12,0},{8,4},{4,8},{0,12},{28,16},{24,20},{20,24},{16,28},{13,1},{... | collective-permute-start | bytes 24584 | tf_op jit(solution)/shard_map/ppermute | solution.py:532
  7.0 0.0 collective-permute-done.refs_1_.mixed_ref
  7.0 0.0 collective-permute-start.1
  7.0 2.1 %first_blocks.1 = (f32[5,1,1024]{2,1,0:T(1,128)S(1)}, bf16[1024,1536]{1,0:T(8,128)(2,1)S(1)}, f32[2,512]{1,0:T(2,128)S(1)}, bf16[512,1024]{1,0:T(8,128)(2,1)S(1)...) custom-call(f32[16,128]{1,0:T(8,128)S(1)} %get-tuple-element.23.refs, ...), custom_call_target="tpu_custom_call", output_to_operand_aliasing={{0}: (9, {}), {1}: (10, {}), {2}: (11, {}), {3}: (12, {}), ... | custom-call | flops 1073741824 | bytes 6291456 | tf_op jit(solution)/shard_map/first_blocks/pallas_call | solution.py:608
  9.2 0.8 %collective-permute-done.2.far_ref = f32[16,128]{1,0:T(8,128)S(1)} collective-permute-done((f32[16,128]{1,0:T(8,128)S(1)}, f32[16,128]{1,0:T(8,128)S(1)}, u32[]{:S(2)}, u32[]{:S(2)}) %collective-permute-start.2) | collective-permute-done | bytes 8224 | tf_op jit(solution)/shard_map/ppermute | solution.py:532
  10.0 0.0 collective-permute-done.1.swapped_ref
  10.0 0.0 copy-start
  10.0 0.0 copy-start.1
  10.0 0.0 copy-start.2
  10.0 5.3 %velocity.1 = (f32[4,8,128]{2,1,0:T(8,128)S(1)}, f32[4,16,128]{2,1,0:T(8,128)S(1)}) custom-call(f32[16,128]{1,0:T(8,128)S(1)} %get-tuple-element.23.refs_0_.own_ref, f32[16,128]{1,0:T(8,128)S(1)} %collective-permute-done.refs_1_.mixed_ref, f32[16,128]{1,0:T(8,128)S(1)} %collective-permute-done.1.swapped_ref, f32[16,128]{1,0:T(8,128)S(1)} %collective-permute-done.2.far_ref, ...), custom_call_target="tpu_custom_call" | custom-call | tf_op jit(solution)/shard_map/velocity/pallas_call | solution.py:619
  15.4 0.0 collective-permute-start.3
  16.0 0.3 %route.1.picks_ref = bf16[512,512]{1,0:T(8,128)(2,1)S(1)} custom-call(f32[4,16,128]{2,1,0:T(8,128)S(1)} %get-tuple-element.40.blocks_ref), custom_call_target="tpu_custom_call" | custom-call | bytes 1048576 | tf_op jit(solution)/shard_map/route/pallas_call | solution.py:491
  16.3 0.2 %collective-permute-done.3.other_ref = f32[4,8,128]{2,1,0:T(8,128)S(1)} collective-permute-done((f32[4,8,128]{2,1,0:T(8,128)S(1)}, f32[4,8,128]{2,1,0:T(8,128)S(1)}, u32[]{:S(2)}, u32[]{:S(2)}) %collective-permute-start.3) | collective-permute-done | bytes 16416 | tf_op jit(solution)/shard_map/ppermute | solution.py:524
  16.6 0.0 copy-done
  16.6 0.0 copy-done.1
  16.6 0.0 copy-done.2
  16.6 6.6 %decode.1 = (f32[8,256]{1,0:T(8,128)}, bf16[96,1024]{1,0:T(8,128)(2,1)}) custom-call(f32[4,16,128]{2,1,0:T(8,128)S(1)} %get-tuple-element.40.blocks_ref, bf16[512,512]{1,0:T(8,128)(2,1)S(1)} %route.1.picks_ref, f32[4,8,128]{2,1,0:T(8,128)S(1)} %get-tuple-element.41.mine_ref, f32[4,8,128]{2,1,0:T(8,128)S(1)} %collective-permute-done.3.other_ref, ...), custom_call_target="tpu_custom_call" | custom-call | tf_op jit(solution)/shard_map/decode/pallas_call | solution.py:509
Async XLA Ops:
  3.0 4.1 %collective-permute-start = (f32[16,128]{1,0:T(8,128)S(1)}, f32[16,128]{1,0:T(8,128)S(1)}, u32[]{:S(2)}, u32[]{:S(2)}) collective-permute-start(f32[16,128]{1,0:T(8,128)S(1)} %get-tuple-element.23.refs_0_.own_ref), channel_id=1, source_target_pairs={{4,0},{0,4},{12,8},{8,12},{24,16},{28,20},{16,24},{20,28},{5,1},{1... | collective-permute-start | bytes 24584 | tf_op jit(solution)/shard_map/ppermute | solution.py:532
  4.6 5.4 %collective-permute-start.2 = (f32[16,128]{1,0:T(8,128)S(1)}, f32[16,128]{1,0:T(8,128)S(1)}, u32[]{:S(2)}, u32[]{:S(2)}) collective-permute-start(f32[16,128]{1,0:T(8,128)S(1)} %get-tuple-element.23.refs_0_.own_ref), channel_id=1, source_target_pairs={{12,0},{8,4},{4,8},{0,12},{28,16},{24,20},{20,24},{16,28},{13,1},{... | collective-permute-start | bytes 24584 | tf_op jit(solution)/shard_map/ppermute | solution.py:532
  7.0 3.0 %collective-permute-start.1 = (f32[16,128]{1,0:T(8,128)S(1)}, f32[16,128]{1,0:T(8,128)S(1)}, u32[]{:S(2)}, u32[]{:S(2)}) collective-permute-start(f32[16,128]{1,0:T(8,128)S(1)} %collective-permute-done.refs_1_.mixed_ref), channel_id=1, source_target_pairs={{0,16},{16,0},{1,17},{17,1},{2,18},{18,2},{3,19},{19,3},{4,20},{20... | collective-permute-start | bytes 24584 | tf_op jit(solution)/shard_map/ppermute | solution.py:524
  10.0 6.6 %copy-start = (bf16[27,768,96]{1,2,0:T(8,128)(2,1)S(1)}, bf16[27,768,96]{1,2,0:T(8,128)(2,1)}, u32[]{:S(2)}) copy-start(bf16[27,768,96]{1,2,0:T(8,128)(2,1)} %param.28) | copy-start | bytes 11943940
  10.0 6.6 %copy-start.1 = (s32[1,1,27,1024]{3,1,2,0:T(1,128)S(1)}, s32[1,1,27,1024]{3,1,2,0:T(1,128)}, u32[]{:S(2)}) copy-start(s32[1,1,27,1024]{3,1,2,0:T(1,128)} %param.27) | copy-start | bytes 331780
  10.0 6.6 %copy-start.2 = (f32[8,768]{1,0:T(8,128)S(1)}, f32[8,768]{1,0:T(8,128)}, u32[]{:S(2)}) copy-start(f32[8,768]{1,0:T(8,128)} %proj_ref.1) | copy-start | bytes 73732
  15.4 1.2 %collective-permute-start.3 = (f32[4,8,128]{2,1,0:T(8,128)S(1)}, f32[4,8,128]{2,1,0:T(8,128)S(1)}, u32[]{:S(2)}, u32[]{:S(2)}) collective-permute-start(f32[4,8,128]{2,1,0:T(8,128)S(1)} %get-tuple-element.41.mine_ref), channel_id=1, source_target_pairs={{0,16},{16,0},{1,17},{17,1},{2,18},{18,2},{3,19},{19,3},{4,20},{20... | collective-permute-start | bytes 49160 | tf_op jit(solution)/shard_map/ppermute | solution.py:524
